TPU v7x, 512 devices: a whole 4x4x16 slice. The times are simulated.
512 devices in a mesh: dom: 64 (over y, z), edge: 8 (over x, core).
Axes of the slice: x: 4, y: 4, z: 16, core: 2. Of those that a mesh axis runs over, the one named last changes fastest.
Arguments:
- node_rows: bfloat16 [16384, 512], P('dom'), may hold values from -6 to 6
- w_first: bfloat16 [1536, 512], replicated, may hold values from -0.15625 to 0.15625
- w_second: bfloat16 [512, 128], replicated, may hold values from -0.25 to 0.25
- w_third: bfloat16 [128], replicated, may hold values from -1 to 1
- src_row: int32 [524288], P(('dom', 'edge')), may hold values from 0 to 255, as said below
- requests: int32 [32768, 8], P(('dom', 'edge')), may hold values from 0 to 255
- slot_index: int32 [524288], P(('dom', 'edge')), may hold values from 0 to 511
- labels: int32 [524288], P(('dom', 'edge')), may hold values from 0 to 1
- live_count: int32 [512], P(('dom', 'edge')), may hold values from 204 to 1024, as said below
Outputs:
- grad_first: float32 [1536, 512], P('edge', 'dom')
- grad_second: float32 [512, 128], P('dom', 'edge')
- grad_third: float32 [128], replicated
- pair_loss: float32 [], replicated
- node_grad: float32 [16384, 512], P(('dom', 'edge'))
Inputs may be any that keep to these rules, and one draw needn't show every extreme that they name: `src_row`: each device's 1024 entries are sorted, non-decreasing. `live_count`: some device is full in every draw.
All inputs are finite; a program needn't handle non-finite values.
Results may differ from a plain program's by a relative error of at most 0.0048.
Values may be sent and summed in bfloat16 or wider, within the bound.
No kernel may reach another device: no remote copies, remote signals or barrier semaphores. Data moves between devices by JAX's collectives and lax.ppermute only.
A program may use at most 64 MiB of HBM per device.

v0:
```python
import math

import jax
import jax.numpy as jnp
from jax import lax
from jax.sharding import PartitionSpec as P


def dsilu(values):
    sig = jax.nn.sigmoid(values)
    return sig * (1.0 + values * (1.0 - sig))


def first_dim(left, right):
    return lax.dot_general(
        left, right, (((0,), (0,)), ((), ())), preferred_element_type=jnp.float32
    )


def last_dim(left, right):
    return lax.dot_general(
        left, right, (((1,), (1,)), ((), ())), preferred_element_type=jnp.float32
    )


def collect(values, index, count):
    onehot = (jnp.arange(count, dtype=jnp.int32)[:, None] == index[None, :]).astype(jnp.float32)
    return jnp.dot(
        onehot, values, precision=lax.Precision.HIGHEST, preferred_element_type=jnp.float32
    )


def pair_pass(near_rows, far_rows, w_first, w_second, w_third, labels, is_live, loss_scale, width):
    product = (near_rows.astype(jnp.float32) * far_rows.astype(jnp.float32)).astype(jnp.bfloat16)
    features = jnp.concatenate([near_rows, far_rows, product], axis=1)
    pre_first = jnp.dot(features, w_first, preferred_element_type=jnp.float32)
    first = jax.nn.silu(pre_first).astype(jnp.bfloat16)
    pre_second = jnp.dot(first, w_second, preferred_element_type=jnp.float32)
    second = jax.nn.silu(pre_second).astype(jnp.bfloat16)
    logits = jnp.dot(second, w_third, preferred_element_type=jnp.float32)
    target = labels.astype(jnp.float32)
    slope = is_live * (jax.nn.sigmoid(logits) - target)
    pair_loss = loss_scale * jnp.sum(is_live * (jax.nn.softplus(logits) - target * logits))
    grad_third = loss_scale * jnp.dot(
        slope, second.astype(jnp.float32), precision=lax.Precision.HIGHEST
    )
    back_second = (
        slope[:, None] * w_third.astype(jnp.float32)[None, :] * dsilu(pre_second)
    ).astype(jnp.bfloat16)
    grad_second = loss_scale * first_dim(first, back_second)
    back_first = (last_dim(back_second, w_second) * dsilu(pre_first)).astype(jnp.bfloat16)
    grad_first = loss_scale * first_dim(features, back_first)
    feature_grad = last_dim(back_first, w_first)
    block_a = feature_grad[:, :width]
    block_b = feature_grad[:, width : 2 * width]
    block_c = feature_grad[:, 2 * width :]
    near_grad = block_a + block_c * far_rows.astype(jnp.float32)
    far_grad = block_b + block_c * near_rows.astype(jnp.float32)
    return (grad_first, grad_second, grad_third, pair_loss, near_grad, far_grad)


def body(node_rows, w_first, w_second, w_third, src_row, requests, slot_index, labels, live_count):
    width = node_rows.shape[1]
    own_count = node_rows.shape[0]
    per_device = src_row.shape[0]
    loss_scale = 1.0 / math.sqrt(per_device * lax.axis_size("dom") * lax.axis_size("edge"))
    asked_here = lax.all_to_all(requests, "dom", split_axis=0, concat_axis=0, tiled=True)
    answer = jnp.take(node_rows, asked_here, axis=0)
    replies = lax.all_to_all(answer, "dom", split_axis=0, concat_axis=0, tiled=True)
    slot_total = replies.shape[0] * replies.shape[1]
    far_rows = jnp.take(replies.reshape(slot_total, width), slot_index, axis=0)
    near_rows = jnp.take(node_rows, src_row, axis=0)
    is_live = (jnp.arange(per_device, dtype=jnp.int32) < live_count[0]).astype(jnp.float32)
    g_first, g_second, g_third, loss_part, near_grad, far_grad = pair_pass(
        near_rows, far_rows, w_first, w_second, w_third, labels, is_live, loss_scale, width
    )
    slot_grad = collect(far_grad, slot_index, slot_total)
    slot_grad = slot_grad.reshape(replies.shape[0], replies.shape[1], width)
    returned = lax.all_to_all(slot_grad, "dom", split_axis=0, concat_axis=0, tiled=True)
    owned = collect(near_grad, src_row, own_count)
    owned = owned + collect(
        returned.reshape(slot_total, width), asked_here.reshape(slot_total), own_count
    )
    node_share = lax.psum_scatter(owned, "edge", scatter_dimension=0, tiled=True)
    dom_first_part, dom_second_part = (
        lax.psum_scatter(g_first, "dom", scatter_dimension=1, tiled=True),
        lax.psum_scatter(g_second, "dom", scatter_dimension=0, tiled=True),
    )
    first_share, second_share = (
        lax.psum_scatter(dom_first_part, "edge", scatter_dimension=0, tiled=True),
        lax.psum_scatter(dom_second_part, "edge", scatter_dimension=1, tiled=True),
    )
    loss_total, third_total = lax.psum((loss_part, g_third), ("dom", "edge"))
    return (first_share, second_share, third_total, loss_total, node_share)


def solution(mesh):
    in_specs = (
        P("dom", None),
        P(),
        P(),
        P(),
        P(("dom", "edge")),
        P(("dom", "edge"), None),
        P(("dom", "edge")),
        P(("dom", "edge")),
        P(("dom", "edge")),
    )
    out_specs = (P("edge", "dom"), P("dom", "edge"), P(), P(), P(("dom", "edge"), None))
    return jax.shard_map(body, mesh=mesh, in_specs=in_specs, out_specs=out_specs, check_vma=False)
```

profile of v0, /device:TPU:6, one launch (start us, length us, event | category | flops | bytes accessed | tf_op | source)
XLA Modules:
  0.0 1182.7 jit_solution(12475231957884691018)
XLA Ops:
  7.2 0.9 copy.18
  8.1 32.9 %all_to_all.25 = s32[64,1,8]{2,1,0:T(1,128)S(1)} all-to-all(s32[64,1,8]{2,1,0:T(1,128)S(1)} %bitcast.43), channel_id=1, replica_groups=mesh['dom'=64,'edge'=8] {'dom'}, dimensions={0} | all-to-all | bytes 4096 | tf_op jit(solution)/shard_map/all_to_all | solution.py:67
  41.1 3.0 gather_fusion.1
  44.2 0.9 bitcast_select_fusion
  45.1 4.6 all-to-all-start.1
  50.5 4.0 gather_fusion
  54.5 25.9 %all-to-all-done.1 = bf16[64,8,512]{2,1,0:T(8,128)(2,1)S(1)} async-done(((bf16[64,8,512]{2,1,0:T(8,128)(2,1)}), bf16[64,8,512]{2,1,0:T(8,128)(2,1)S(1)}, u32[]{:S(2)}, u32[]{:S(2)}) %all-to-all-start.1) | async-done | bytes 524320 | tf_op jit(solution)/shard_map/all_to_all | solution.py:69
  80.4 5.1 gather_fusion.2
  85.5 1.9 fusion.3
  87.4 3.2 multiply_convert_fusion.1
  91.3 0.6 fusion.22
  91.9 1.4 convolution_multiply_fusion.1
  93.3 3.9 multiply_convert_fusion
  97.5 5.4 convolution_multiply_fusion
  102.9 1.2 copy-done.13
  104.1 1.8 fusion.29
  105.9 2.7 copy-done.7
  108.6 3.2 fusion.11
  111.8 6.8 all-to-all-start.2
  118.6 1.3 dynamic-slice
  121.0 0.7 reduce.3
  121.8 240.2 %all-reduce.4.cloned.1.call-done = f32[512,128]{1,0:T(8,128)} async-done(((f32[512,128]{1,0:T(8,128)}), f32[512,128]{1,0:T(8,128)}) %all-reduce.4.cloned.1.call-update) | async-done | bytes 262160
  362.1 0.7 constant_dynamic-slice_fusion
  362.7 0.7 copy.21
  363.5 4.0 fusion.5
  367.5 691.4 %reduce-scatter.9.cloned.1.call-done = f32[1536,8]{0,1:T(8,128)} async-done(((f32[1536,512]{0,1:T(8,128)}), f32[1536,8]{0,1:T(8,128)}) %reduce-scatter.9.cloned.1.call-update) | async-done | bytes 49168 | tf_op jit(solution)/shard_map/reduce_scatter | solution.py:86
  1059.0 2.0 copy.19
  1061.0 1.5 convolution_add_fusion
  1063.4 99.8 %all-reduce.1 = (f32[128]{0:T(128)}, f32[]{:T(128)}) all-reduce(f32[128]{0:T(128)S(1)} %fusion.15, f32[]{:T(128)S(6)} %mul.99), channel_id=1, replica_groups=mesh['dom'=64,'edge'=8] {'dom','edge'}, use_global_device_ids=true, to_apply=%region_4.5 | all-reduce | flops 129 | bytes 1032 | tf_op jit(solution)/shard_map/psum | solution.py:93
  1163.2 1.4 copy.22
  1164.6 1.6 copy.20
  1166.1 10.1 reduce-scatter.11.cloned.1.call-done
  (54 shorter events, 2.2 us)
Async XLA Ops:
  7.2 80.2 %copy-start = (bf16[1536,512]{1,0:T(8,128)(2,1)S(1)}, bf16[1536,512]{1,0:T(8,128)(2,1)}, u32[]{:S(2)}) copy-start(bf16[1536,512]{1,0:T(8,128)(2,1)} %param.10) | copy-start | bytes 4718596
  44.1 6.3 copy-start.11
  44.1 6.3 copy-start.8
  44.1 6.3 copy-start.1
  45.1 35.3 %all-to-all-start.1 = ((bf16[64,8,512]{2,1,0:T(8,128)(2,1)}), bf16[64,8,512]{2,1,0:T(8,128)(2,1)S(1)}, u32[]{:S(2)}, u32[]{:S(2)}) async-start(bf16[64,8,512]{2,1,0:T(8,128)(2,1)} %bitcast_select_fusion), calls=%async_computation.1 | async-start | bytes 1048576 | tf_op jit(solution)/shard_map/all_to_all | solution.py:69
  49.7 312.3 %all-reduce.4.cloned.1.call-start = ((), (), s32[]{:S(2)}) async-start(), calls=%async_computation.11 | async-start | bytes 524288
  50.5 4.0 copy-start.9
  87.3 3.3 copy-start.2
  87.4 3.2 copy-start.4
  87.4 3.2 copy-start.6
  87.4 3.2 copy-start.12
  90.6 0.7 copy-start.10
  91.1 0.8 copy-start.14
  93.3 4.1 copy-start.3
  97.2 961.7 %reduce-scatter.9.cloned.1.call-start = ((), (), s32[]{:S(2)}) async-start(), calls=%async_computation.7 | async-start | bytes 3194880 | tf_op jit(solution)/shard_map/reduce_scatter | solution.py:86
  102.9 1.2 copy-start.13
  104.1 4.5 copy-start.5
  105.9 2.7 copy-start.7
  111.8 949.3 %all-to-all-start.2 = ((f32[64,8,512]{2,1,0:T(8,128)}), f32[64,8,512]{2,1,0:T(8,128)S(1)}, u32[]{:S(2)}, u32[]{:S(2)}) async-start(f32[64,8,512]{2,1,0:T(8,128)} %fusion.11), calls=%async_computation.3 | async-start | bytes 2097152 | tf_op jit(solution)/shard_map/all_to_all | solution.py:79
  118.5 1044.7 %reduce-scatter.15.cloned.1.call-start = ((), (), s32[]{:S(2)}) async-start(), calls=%async_computation.10 | async-start | bytes 73728
  363.5 801.1 %reduce-scatter.13.cloned.1.call-start = ((), (), s32[]{:S(2)}) async-start(), calls=%async_computation.9 | async-start | bytes 884736
  1061.0 115.2 %reduce-scatter.11.cloned.1.call-start = ((), (), s32[]{:S(2)}) async-start(), calls=%async_computation.8 | async-start | bytes 589824 | tf_op jit(solution)/shard_map/reduce_scatter | solution.py:84
Sparse Core Ops, SparseCore 0:
  97.3 264.6 all-reduce.3
  367.1 691.8 reduce-scatter.8
  1062.0 31.9 reduce-scatter.14
  1096.7 38.0 reduce-scatter.12
  1138.3 37.9 reduce-scatter.10
where the time goes:
time: 1190 us; the launch traced here: 1180 us
  waiting for transfers between devices  968 us (81%)
  blocking collectives  133 us (11%)
  matrix products  25.2 us (2%)
  local copies, waits for them, and re-layouts  25.1 us (2%)
  between operations  16 us (1%)
    reduce_scatter x1, waiting for transfers between devices, body(): lax.psum_scatter(g_first, 'dom', scatter_dimension=1, tiled=True)  691 us
    unnamed x8, waiting for transfers between devices  240 us
    psum x1, blocking collectives, body(): loss_total, third_total = lax.psum((loss_part, g_third), ('dom', 'edge'))  99.8 us
    all_to_all x1, blocking collectives, body(): lax.all_to_all(requests, 'dom', split_axis=0, concat_axis=0, tiled=True)  32.9 us
    all_to_all x1, waiting for transfers between devices, body(): lax.all_to_all(answer, 'dom', split_axis=0, concat_axis=0, tiled=True)  25.9 us
  transfers between devices with their start and end apart: 7, of which 4 were waited for; matrix products, arithmetic and copies ran while one was open for 2% of the time, Pallas kernels for 0%

commit v1 on v0

v1 whole, which is shorter than its diff:
```python
import math

import jax
import jax.numpy as jnp
from jax import lax
from jax.sharding import PartitionSpec as P

BF = jnp.bfloat16
F32 = jnp.float32


def dsilu(values):
    sig = jax.nn.sigmoid(values)
    return sig * (1.0 + values * (1.0 - sig))


def first_dim(left, right):
    return lax.dot_general(left, right, (((0,), (0,)), ((), ())), preferred_element_type=F32)


def last_dim(left, right):
    return lax.dot_general(left, right, (((1,), (1,)), ((), ())), preferred_element_type=F32)


def halves(values):
    high = lax.reduce_precision(values, 8, 7)
    return high.astype(BF), (values - high).astype(BF)


def onehot_rows(index, count):
    return (jnp.arange(count, dtype=jnp.int32)[:, None] == index[None, :]).astype(BF)


def collect(values, index, count):
    onehot = onehot_rows(index, count)
    high, low = halves(values)
    return jnp.dot(onehot, high, preferred_element_type=F32) + jnp.dot(
        onehot, low, preferred_element_type=F32
    )


def pair_pass(near_rows, far_rows, w_first, w_second, w_third, labels, is_live, loss_scale, width):
    product = (near_rows.astype(F32) * far_rows.astype(F32)).astype(BF)
    features = jnp.concatenate([near_rows, far_rows, product], axis=1)
    pre_first = jnp.dot(features, w_first, preferred_element_type=F32)
    first = jax.nn.silu(pre_first).astype(BF)
    pre_second = jnp.dot(first, w_second, preferred_element_type=F32)
    second = jax.nn.silu(pre_second).astype(BF)
    logits = jnp.dot(second, w_third, preferred_element_type=F32)
    target = labels.astype(F32)
    slope = is_live * (jax.nn.sigmoid(logits) - target)
    pair_loss = loss_scale * jnp.sum(is_live * (jax.nn.softplus(logits) - target * logits))
    grad_third = loss_scale * jnp.dot(slope, second.astype(F32), precision=lax.Precision.HIGHEST)
    back_second = (slope[:, None] * w_third.astype(F32)[None, :] * dsilu(pre_second)).astype(BF)
    grad_second_t = loss_scale * first_dim(back_second, first)
    back_first = (last_dim(back_second, w_second) * dsilu(pre_first)).astype(BF)
    grad_first = loss_scale * first_dim(features, back_first)
    feature_grad = last_dim(back_first, w_first)
    block_a = feature_grad[:, :width]
    block_b = feature_grad[:, width : 2 * width]
    block_c = feature_grad[:, 2 * width :]
    near_grad = block_a + block_c * far_rows.astype(F32)
    far_grad = block_b + block_c * near_rows.astype(F32)
    return (grad_first, grad_second_t, grad_third, pair_loss, near_grad, far_grad)


def body(node_rows, w_first, w_second, w_third, src_row, requests, slot_index, labels, live_count):
    own_count, width = node_rows.shape
    per_device = src_row.shape[0]
    parts, cap = requests.shape
    n_edge = lax.axis_size("edge")
    chips = n_edge // 2
    slots = parts * cap
    hidden = w_first.shape[1]
    hidden2 = w_second.shape[1]
    loss_scale = 1.0 / math.sqrt(per_device * parts * n_edge)
    edge = lax.axis_index("edge")
    chip, core = edge // 2, edge % 2
    sibling = [(i, i ^ 1) for i in range(n_edge)]

    def ahead(step):
        return [(i, (i + 2 * step) % n_edge) for i in range(n_edge)]

    steps = (1, chips - 1) + tuple(range(2, chips - 1))

    def by_core(blocks):
        rolled = jnp.roll(blocks, -2 * chip, axis=0)
        rolled = rolled.reshape((chips, 2) + blocks.shape[1:])
        kept = lax.dynamic_index_in_dim(rolled, core, 1, keepdims=False)
        sent = lax.dynamic_index_in_dim(rolled, 1 - core, 1, keepdims=False)
        return kept + lax.ppermute(sent, "edge", sibling)

    asked_here = lax.all_to_all(requests, "dom", split_axis=0, concat_axis=0, tiled=True)
    asked_flat = asked_here.reshape(slots)
    answer = jnp.take(node_rows, asked_flat, axis=0, mode="clip").reshape(parts, cap, width)
    replies = lax.all_to_all(answer, "dom", split_axis=0, concat_axis=0, tiled=True)
    far_rows = jnp.take(replies.reshape(slots, width), slot_index, axis=0, mode="clip")
    near_rows = jnp.take(node_rows, src_row, axis=0, mode="clip")
    is_live = (jnp.arange(per_device, dtype=jnp.int32) < live_count[0]).astype(F32)
    g_first, g_second_t, g_third, loss_part, near_grad, far_grad = pair_pass(
        near_rows, far_rows, w_first, w_second, w_third, labels, is_live, loss_scale, width
    )

    slot_grad = collect(far_grad, slot_index, slots).astype(BF).reshape(parts, cap, width)
    returned = lax.all_to_all(slot_grad, "dom", split_axis=0, concat_axis=0, tiled=True)

    rows1 = g_first.shape[0] // n_edge
    rows2 = hidden2 // n_edge
    extra = jnp.zeros((8, hidden), F32).at[0, :hidden2].set(g_third).at[1, 0].set(loss_part)
    blocks = jnp.concatenate(
        [
            g_first.reshape(n_edge, rows1, hidden),
            g_second_t.reshape(n_edge, rows2, hidden),
            jnp.broadcast_to(extra, (n_edge, 8, hidden)),
        ],
        axis=1,
    )
    chip_sum = by_core(blocks)
    total = chip_sum[0]
    rows = rows1 + rows2
    for step in steps:
        high, low = halves(chip_sum[step])
        packed = jnp.concatenate([high, low[rows:]], axis=0)
        got = lax.ppermute(packed, "edge", ahead(step)).astype(F32)
        total = total + jnp.concatenate([got[:rows], got[rows : rows + 8] + got[rows + 8 :]], axis=0)

    share = hidden // parts
    small = jnp.concatenate([total[rows, :hidden2], total[rows + 1, :share]]).reshape(-1, share).T
    small_high, small_low = halves(small)
    n_small = small.shape[1]
    columns = total[:rows].T.reshape(parts, share, rows).astype(BF)
    sent = jnp.concatenate(
        [
            columns,
            jnp.broadcast_to(small_high, (parts, share, n_small)),
            jnp.broadcast_to(small_low, (parts, share, n_small)),
        ],
        axis=2,
    )
    got = lax.all_to_all(sent, "dom", split_axis=0, concat_axis=0, tiled=True)
    got = jnp.sum(got.astype(F32), axis=0)
    first_share = got[:, :rows1].T
    second_share = got[:, rows1:rows]
    small = got[:, rows : rows + n_small] + got[:, rows + n_small :]
    small = small.T.reshape(-1)
    third_total = small[:hidden2]
    loss_total = small[hidden2]

    owned = collect(near_grad, src_row, own_count)
    owned = owned + jnp.dot(
        onehot_rows(asked_flat, own_count),
        returned.reshape(slots, width),
        preferred_element_type=F32,
    )
    node_chip = by_core(owned.reshape(n_edge, own_count // n_edge, width))
    node_share = node_chip[0]
    for step in steps:
        node_share = node_share + lax.ppermute(node_chip[step], "edge", ahead(step))
    return (first_share, second_share, third_total, loss_total, node_share)


def solution(mesh):
    in_specs = (
        P("dom", None),
        P(),
        P(),
        P(),
        P(("dom", "edge")),
        P(("dom", "edge"), None),
        P(("dom", "edge")),
        P(("dom", "edge")),
        P(("dom", "edge")),
    )
    out_specs = (P("edge", "dom"), P("dom", "edge"), P(), P(), P(("dom", "edge"), None))
    return jax.shard_map(body, mesh=mesh, in_specs=in_specs, out_specs=out_specs, check_vma=False)
```

time: 1190 us -> 185 us (0.16)
  waiting for transfers between devices: 968 us -> 47.6 us
  blocking collectives: 133 us -> 32.9 us
  starting transfers between devices: 11.8 us -> 42.4 us
  between operations: 16 us -> 2.63 us
    reduce_scatter x2 -> x0, waiting for transfers between devices: 701 us -> none  [the longest x1 691 us: body(): lax.psum_scatter(g_first, 'dom', scatter_dimension=1, tiled=True)]
    unnamed x8 -> x0, waiting for transfers between devices: 240 us -> none
    psum x1 -> x0, blocking collectives: 99.8 us -> none  [body(): loss_total, third_total = lax.psum((loss_part, g_third), ('dom', 'edge'))]
    ppermute x0 -> x8, starting transfers between devices: none -> 23.9 us  [the longest x3 10.6 us: body(): node_share = node_share + lax.ppermute(node_chip[step], 'edge', ahead(step))]
  transfers between devices with their start and end apart: 7 -> 11, of which waited for: 4 -> 6; matrix products, arithmetic and copies ran while one was open for 2% -> 12% of each run, Pallas kernels for 0% -> 0%
where the time goes in v1:
time: 185 us; the launch traced here: 184 us
  waiting for transfers between devices  47.6 us (26%)
  starting transfers between devices  42.4 us (23%)
  blocking collectives  32.9 us (18%)
  local copies, waits for them, and re-layouts  26.1 us (14%)
  matrix products  20.5 us (11%)
  other arithmetic  11.7 us (6%)
  between operations  2.63 us (1%)
    all_to_all x1, blocking collectives, body(): lax.all_to_all(requests, 'dom', split_axis=0, concat_axis=0, tiled=True)  32.9 us
    all_to_all x1, waiting for transfers between devices, body(): lax.all_to_all(answer, 'dom', split_axis=0, concat_axis=0, tiled=True)  24.8 us
    ppermute x3, starting transfers between devices, body(): node_share = node_share + lax.ppermute(node_chip[step], 'edge', ahead(step))  10.6 us
    ppermute x3, starting transfers between devices, body(): got = lax.ppermute(packed, 'edge', ahead(step)).astype(F32)  9.2 us
    all_to_all x1, waiting for transfers between devices, body(): got = lax.all_to_all(sent, 'dom', split_axis=0, concat_axis=0, tiled=True)  8.32 us
    all_to_all x1, waiting for transfers between devices, body(): lax.all_to_all(slot_grad, 'dom', split_axis=0, concat_axis=0, tiled=True)  7.65 us
    all_to_all x1, starting transfers between devices, body(): got = lax.all_to_all(sent, 'dom', split_axis=0, concat_axis=0, tiled=True)  7.21 us
    all_to_all x1, starting transfers between devices, body(): lax.all_to_all(slot_grad, 'dom', split_axis=0, concat_axis=0, tiled=True)  6.75 us
  transfers between devices with their start and end apart: 11, of which 6 were waited for; matrix products, arithmetic and copies ran while one was open for 12% of the time, Pallas kernels for 0%

profile of v1, /device:TPU:6, one launch (start us, length us, event | category | flops | bytes accessed | tf_op | source)
XLA Modules:
  0.0 184.0 jit_solution(12106810999024542581)
XLA Ops:
  1.5 32.9 %all_to_all.24 = s32[64,1,8]{2,1,0:T(1,128)S(1)} all-to-all(s32[64,1,8]{2,1,0:T(1,128)S(1)} %bitcast.113), channel_id=1, replica_groups=mesh['dom'=64,'edge'=8] {'dom'}, dimensions={0} | all-to-all | bytes 4096 | tf_op jit(solution)/shard_map/all_to_all | solution.py:93
  35.8 3.7 %gather_fusion.1 = bf16[512,512]{1,0:T(8,128)(2,1)} fusion(bf16[256,512]{1,0:T(8,128)(2,1)} %param.13, s32[1024]{0:T(1024)S(1)} %pad_clamp_fusion), kind=kCustom, calls=%fused_computation.1 | custom fusion | bytes 1050624 | tf_op jit(solution)/shard_map/jit(_take)/gather | solution.py:95
  39.5 4.6 %all-to-all-start.1 = ((bf16[64,8,512]{2,1,0:T(8,128)(2,1)}), bf16[64,8,512]{2,1,0:T(8,128)(2,1)S(1)}, u32[]{:S(2)}, u32[]{:S(2)}) async-start(bf16[64,8,512]{2,1,0:T(8,128)(2,1)} %bitcast.1), calls=%async_computation.1 | async-start | bytes 1048576 | tf_op jit(solution)/shard_map/all_to_all | solution.py:96
  44.3 5.0 %gather_fusion = bf16[1024,512]{1,0:T(8,128)(2,1)} fusion(bf16[256,512]{1,0:T(8,128)(2,1)S(1)} %copy-done.1, s32[1024]{0:T(1024)S(1)} %broadcast_clamp_fusion.1), kind=kCustom, calls=%fused_computation | custom fusion | bytes 2101248 | tf_op jit(solution)/shard_map/jit(_take)/gather | solution.py:98
  50.0 24.8 %all-to-all-done.1 = bf16[64,8,512]{2,1,0:T(8,128)(2,1)S(1)} async-done(((bf16[64,8,512]{2,1,0:T(8,128)(2,1)}), bf16[64,8,512]{2,1,0:T(8,128)(2,1)S(1)}, u32[]{:S(2)}, u32[]{:S(2)}) %all-to-all-start.1) | async-done | bytes 524320 | tf_op jit(solution)/shard_map/all_to_all | solution.py:96
  74.8 4.0 %gather_fusion.2 = bf16[1024,512]{1,0:T(8,128)(2,1)S(1)} fusion(bf16[512,512]{1,0:T(8,128)(2,1)S(1)} %bitcast.104, s32[1024]{0:T(1024)S(1)} %broadcast_clamp_fusion), kind=kCustom, calls=%fused_computation.2 | custom fusion | bytes 2101248 | tf_op jit(solution)/shard_map/jit(_take)/gather | solution.py:97
  78.8 1.6 fusion.6
  80.4 2.1 %multiply_convert_fusion.1 = (bf16[1024,512]{1,0:T(8,128)(2,1)S(1)}, f32[1024,512]{1,0:T(8,128)S(1)}) fusion(bf16[1536,512]{1,0:T(8,128)(2,1)S(1)} %copy-done, bf16[1024,512]{1,0:T(8,128)(2,1)S(1)} %fusion.6, bf16[1024,512]{1,0:T(8,128)(2,1)S(1)} %gather_fusion.2, bf16[1024,512]{1,0:T(8,128)(2,1)S(1)} %copy-done.3), kind=kOutput, calls=%fused_computation.32 | convolution fusion | flops 1622671360 | bytes 7864320 | tf_op jit(solution)/shard_map/dot_general | solution.py:45
  85.5 3.5 %convolution_multiply_fusion = f32[1536,512]{1,0:T(8,128)} fusion(bf16[1024,512]{1,0:T(8,128)(2,1)S(1)} %multiply_convert_fusion, bf16[1024,512]{1,0:T(8,128)(2,1)S(1)} %fusion.6, bf16[1024,512]{1,0:T(8,128)(2,1)S(1)} %gather_fusion.2, bf16[1024,512]{1,0:T(8,128)(2,1)S(1)} %copy-done.3), kind=kOutput, calls=%fused_computation.14 | convolution fusion | flops 1620836352 | bytes 7340032 | tf_op jit(solution)/shard_map/dot_general | solution.py:18
  90.0 3.9 %fusion.2 = f32[8,216,512]{2,1,0:T(8,128)S(1)} fusion(s32[]{:T(128)S(6)} %select_n.46, f32[8,192,512]{2,1,0:T(8,128)} %bitcast.107, f32[8,16,512]{2,1,0:T(8,128)S(1)} %bitcast.112, f32[8,8,512]{2,1,0:T(8,128)S(1)} %broadcast_in_dim.32), kind=kLoop, calls=%fused_computation.11 | loop fusion | flops 4423680 | bytes 7077892 | tf_op jit(solution)/shard_map/jit(_roll_dynamic)/concatenate | solution.py:87
  93.8 1.8 copy-done.2
  97.2 2.1 %collective-permute-start = (f32[4,216,512]{2,1,0:T(8,128)}, f32[4,216,512]{2,1,0:T(8,128)}, u32[]{:S(2)}, u32[]{:S(2)}) collective-permute-start(f32[4,216,512]{2,1,0:T(8,128)} %dynamic-slice_bitcast_fusion), channel_id=1, source_target_pairs={{0,1},{1,0},{2,3},{3,2},{4,5},{5,4},{6,7},{7,6},{8,9},{9,8},{10,11... | collective-permute-start | bytes 5308424 | tf_op jit(solution)/shard_map/ppermute | solution.py:91
  99.3 3.1 %fusion.59 = f32[1024,1536]{1,0:T(8,128)S(1)} fusion(bf16[1024,512]{1,0:T(8,128)(2,1)} %copy-done.12, bf16[1536,512]{1,0:T(8,128)(2,1)S(1)} %copy-done), kind=kOutput, calls=%fused_computation.122 | convolution fusion | flops 1610612736 | bytes 8912896 | tf_op jit(solution)/shard_map/dot_general | solution.py:22
  103.3 1.8 copy-done.11
  105.1 1.6 fusion.15
  106.7 6.8 %all-to-all-start.3 = ((bf16[64,8,512]{2,1,0:T(8,128)(2,1)}), bf16[64,8,512]{2,1,0:T(8,128)(2,1)S(1)}, u32[]{:S(2)}, u32[]{:S(2)}) async-start(bf16[64,8,512]{2,1,0:T(8,128)(2,1)} %fusion.15), calls=%async_computation.3 | async-start | bytes 1048576 | tf_op jit(solution)/shard_map/all_to_all | solution.py:105
  113.4 2.4 %bitcast_add_fusion = f32[4,216,512]{2,1,0:T(8,128)S(1)} fusion(f32[4,216,512]{2,1,0:T(8,128)} %collective-permute-done, f32[4,2,216,512]{3,2,1,0:T(8,128)} %bitcast.106, s32[]{:T(128)S(6)} %select_n.48), kind=kLoop, calls=%fused_computation.34 | loop fusion | flops 442368 | bytes 5308420 | tf_op jit(solution)/shard_map/add | solution.py:91
  116.2 2.4 %collective-permute-start.1 = (bf16[224,512]{1,0:T(8,128)(2,1)S(1)}, bf16[224,512]{1,0:T(8,128)(2,1)S(1)}, u32[]{:S(2)}, u32[]{:S(2)}) collective-permute-start(bf16[224,512]{1,0:T(8,128)(2,1)S(1)} %pad_maximum_fusion.4), channel_id=1, source_target_pairs={{0,2},{1,3},{2,4},{3,5},{4,6},{5,7},{6,0},{7,1},{8,10},{9,11},{10,... | collective-permute-start | bytes 688136 | tf_op jit(solution)/shard_map/ppermute | solution.py:124
  118.7 3.4 %collective-permute-start.2 = (bf16[224,512]{1,0:T(8,128)(2,1)S(1)}, bf16[224,512]{1,0:T(8,128)(2,1)S(1)}, u32[]{:S(2)}, u32[]{:S(2)}) collective-permute-start(bf16[224,512]{1,0:T(8,128)(2,1)S(1)} %pad_maximum_fusion.5), channel_id=1, source_target_pairs={{0,6},{1,7},{2,0},{3,1},{4,2},{5,3},{6,4},{7,5},{8,14},{9,15},{10,... | collective-permute-start | bytes 688136 | tf_op jit(solution)/shard_map/ppermute | solution.py:124
  122.1 3.4 %collective-permute-start.3 = (bf16[224,512]{1,0:T(8,128)(2,1)S(1)}, bf16[224,512]{1,0:T(8,128)(2,1)S(1)}, u32[]{:S(2)}, u32[]{:S(2)}) collective-permute-start(bf16[224,512]{1,0:T(8,128)(2,1)S(1)} %pad_maximum_fusion.6), channel_id=1, source_target_pairs={{0,4},{1,5},{2,6},{3,7},{4,0},{5,1},{6,2},{7,3},{8,12},{9,13},{10,... | collective-permute-start | bytes 688136 | tf_op jit(solution)/shard_map/ppermute | solution.py:124
  125.5 3.6 %fusion.21 = f32[256,512]{1,0:T(8,128)} fusion(s32[1024]{0:T(1024)S(1)} %copy-done.8, bf16[1024,512]{1,0:T(8,128)(2,1)S(1)} %gather_fusion.2, f32[1024,1536]{1,0:T(8,128)} %copy-done.11), kind=kOutput, calls=%fused_computation.46 | convolution fusion | flops 271319040 | bytes 5771264 | tf_op jit(solution)/shard_map/dot_general | solution.py:37
  129.2 5.0 %collective-permute-done.2 = bf16[224,512]{1,0:T(8,128)(2,1)S(1)} collective-permute-done((bf16[224,512]{1,0:T(8,128)(2,1)S(1)}, bf16[224,512]{1,0:T(8,128)(2,1)S(1)}, u32[]{:S(2)}, u32[]{:S(2)}) %collective-permute-start.2) | collective-permute-done | bytes 229408 | tf_op jit(solution)/shard_map/ppermute | solution.py:124
  135.6 1.7 fusion.33
  138.4 7.7 %all-to-all-done.3 = bf16[64,8,512]{2,1,0:T(8,128)(2,1)S(1)} async-done(((bf16[64,8,512]{2,1,0:T(8,128)(2,1)}), bf16[64,8,512]{2,1,0:T(8,128)(2,1)S(1)}, u32[]{:S(2)}, u32[]{:S(2)}) %all-to-all-start.3) | async-done | bytes 524320 | tf_op jit(solution)/shard_map/all_to_all | solution.py:105
  146.3 3.0 %fusion.16 = f32[256,512]{1,0:T(8,128)S(1)} fusion(f32[256,512]{1,0:T(8,128)S(1)} %fusion.25, f32[256,512]{1,0:T(8,128)} %fusion.21, s32[1024]{0:T(1024)S(1)} %copy-done.8, bf16[1024,512]{1,0:T(8,128)(2,1)S(1)} %gather_fusion.2, f32[1024,1536]{1,0:T(8,128)} %copy-done.11), kind=kOutput, calls=%fused_computation.41 | convolution fusion | flops 272105472 | bytes 6819840 | tf_op jit(solution)/shard_map/dot_general | solution.py:37
  149.5 1.9 %collective-permute-start.4 = (f32[4,32,512]{2,1,0:T(8,128)S(1)}, f32[4,32,512]{2,1,0:T(8,128)S(1)}, u32[]{:S(2)}, u32[]{:S(2)}) collective-permute-start(f32[4,32,512]{2,1,0:T(8,128)S(1)} %dynamic-slice_bitcast_fusion.1), channel_id=1, source_target_pairs={{0,1},{1,0},{2,3},{3,2},{4,5},{5,4},{6,7},{7,6},{8,9},{9,8},{10,11... | collective-permute-start | bytes 786440 | tf_op jit(solution)/shard_map/ppermute | solution.py:91
  152.3 7.2 %all-to-all-start.2 = ((bf16[64,8,242]{2,1,0:T(8,128)(2,1)}), bf16[64,8,242]{2,1,0:T(8,128)(2,1)S(1)}, u32[]{:S(2)}, u32[]{:S(2)}) async-start(bf16[64,8,242]{2,1,0:T(8,128)(2,1)} %pad_maximum_fusion.3), calls=%async_computation.2 | async-start | bytes 524288 | tf_op jit(solution)/shard_map/all_to_all | solution.py:140
  159.6 3.6 %collective-permute-start.7 = (f32[32,512]{1,0:T(8,128)S(1)}, f32[32,512]{1,0:T(8,128)S(1)}, u32[]{:S(2)}, u32[]{:S(2)}) collective-permute-start(f32[32,512]{1,0:T(8,128)S(1)} %get-tuple-element.39), channel_id=1, source_target_pairs={{0,4},{1,5},{2,6},{3,7},{4,0},{5,1},{6,2},{7,3},{8,12},{9,13},{10,... | collective-permute-start | bytes 196616 | tf_op jit(solution)/shard_map/ppermute | solution.py:158
  163.2 1.9 %collective-permute-start.6 = (f32[32,512]{1,0:T(8,128)S(1)}, f32[32,512]{1,0:T(8,128)S(1)}, u32[]{:S(2)}, u32[]{:S(2)}) collective-permute-start(f32[32,512]{1,0:T(8,128)S(1)} %get-tuple-element.40), channel_id=1, source_target_pairs={{0,6},{1,7},{2,0},{3,1},{4,2},{5,3},{6,4},{7,5},{8,14},{9,15},{10,... | collective-permute-start | bytes 196616 | tf_op jit(solution)/shard_map/ppermute | solution.py:158
  165.2 5.1 %collective-permute-start.5 = (f32[32,512]{1,0:T(8,128)S(1)}, f32[32,512]{1,0:T(8,128)S(1)}, u32[]{:S(2)}, u32[]{:S(2)}) collective-permute-start(f32[32,512]{1,0:T(8,128)S(1)} %get-tuple-element.38), channel_id=1, source_target_pairs={{0,2},{1,3},{2,4},{3,5},{4,6},{5,7},{6,0},{7,1},{8,10},{9,11},{10,... | collective-permute-start | bytes 196616 | tf_op jit(solution)/shard_map/ppermute | solution.py:158
  170.6 1.6 collective-permute-done.5
  172.8 8.3 %all-to-all-done.2 = bf16[64,8,242]{2,1,0:T(8,128)(2,1)S(1)} async-done(((bf16[64,8,242]{2,1,0:T(8,128)(2,1)}), bf16[64,8,242]{2,1,0:T(8,128)(2,1)S(1)}, u32[]{:S(2)}, u32[]{:S(2)}) %all-to-all-start.2) | async-done | bytes 247840 | tf_op jit(solution)/shard_map/all_to_all | solution.py:140
  (92 shorter events, 15.9 us)
Async XLA Ops:
  0.6 79.8 %copy-start = (bf16[1536,512]{1,0:T(8,128)(2,1)S(1)}, bf16[1536,512]{1,0:T(8,128)(2,1)}, u32[]{:S(2)}) copy-start(bf16[1536,512]{1,0:T(8,128)(2,1)} %param.14) | copy-start | bytes 4718596
  35.8 8.4 %copy-start.8 = (s32[1024]{0:T(1024)S(1)}, s32[1024]{0:T(1024)}, u32[]{:S(2)}) copy-start(s32[1024]{0:T(1024)} %param.17) | copy-start | bytes 12292
  35.8 8.4 %copy-start.1 = (bf16[256,512]{1,0:T(8,128)(2,1)S(1)}, bf16[256,512]{1,0:T(8,128)(2,1)}, u32[]{:S(2)}) copy-start(bf16[256,512]{1,0:T(8,128)(2,1)} %param.13) | copy-start | bytes 786436
  39.5 35.3 %all-to-all-start.1 = ((bf16[64,8,512]{2,1,0:T(8,128)(2,1)}), bf16[64,8,512]{2,1,0:T(8,128)(2,1)S(1)}, u32[]{:S(2)}, u32[]{:S(2)}) async-start(bf16[64,8,512]{2,1,0:T(8,128)(2,1)} %bitcast.1), calls=%async_computation.1 | async-start | bytes 1048576 | tf_op jit(solution)/shard_map/all_to_all | solution.py:96
  44.3 5.1 %copy-start.9 = (bf16[128]{0:T(256)(128)(2,1)S(1)}, bf16[128]{0:T(256)(128)(2,1)}, u32[]{:S(2)}) copy-start(bf16[128]{0:T(256)(128)(2,1)} %param.16) | copy-start | bytes 772
  44.3 5.7 %copy-start.7 = (s32[1024]{0:T(1024)S(1)}, s32[1024]{0:T(1024)}, u32[]{:S(2)}) copy-start(s32[1024]{0:T(1024)} %param.19) | copy-start | bytes 12292
  78.8 1.6 copy-start.3
  80.4 2.1 %copy-start.10 = (bf16[512,128]{1,0:T(8,128)(2,1)S(1)}, bf16[512,128]{1,0:T(8,128)(2,1)}, u32[]{:S(2)}) copy-start(bf16[512,128]{1,0:T(8,128)(2,1)} %param.15) | copy-start | bytes 393220
  82.5 0.7 copy-start.6
  85.5 3.5 %copy-start.12 = (bf16[1024,512]{1,0:T(8,128)(2,1)}, bf16[1024,512]{1,0:T(8,128)(2,1)S(1)}, u32[]{:S(2)}) copy-start(bf16[1024,512]{1,0:T(8,128)(2,1)S(1)} %multiply_convert_fusion) | copy-start | bytes 3145732
  93.8 1.8 copy-start.2
  97.2 16.3 %collective-permute-start = (f32[4,216,512]{2,1,0:T(8,128)}, f32[4,216,512]{2,1,0:T(8,128)}, u32[]{:S(2)}, u32[]{:S(2)}) collective-permute-start(f32[4,216,512]{2,1,0:T(8,128)} %dynamic-slice_bitcast_fusion), channel_id=1, source_target_pairs={{0,1},{1,0},{2,3},{3,2},{4,5},{5,4},{6,7},{7,6},{8,9},{9,8},{10,11... | collective-permute-start | bytes 5308424 | tf_op jit(solution)/shard_map/ppermute | solution.py:91
  99.3 3.2 %copy-start.4 = (bf16[1024,512]{1,0:T(8,128)(2,1)S(1)}, bf16[1024,512]{1,0:T(8,128)(2,1)}, u32[]{:S(2)}) copy-start(bf16[1024,512]{1,0:T(8,128)(2,1)} %gather_fusion) | copy-start | bytes 3145732
  102.4 2.7 %copy-start.11 = (f32[1024,1536]{1,0:T(8,128)}, f32[1024,1536]{1,0:T(8,128)S(1)}, u32[]{:S(2)}) copy-start(f32[1024,1536]{1,0:T(8,128)S(1)} %fusion.59) | copy-start | bytes 18874372
  106.7 39.3 %all-to-all-start.3 = ((bf16[64,8,512]{2,1,0:T(8,128)(2,1)}), bf16[64,8,512]{2,1,0:T(8,128)(2,1)S(1)}, u32[]{:S(2)}, u32[]{:S(2)}) async-start(bf16[64,8,512]{2,1,0:T(8,128)(2,1)} %fusion.15), calls=%async_computation.3 | async-start | bytes 1048576 | tf_op jit(solution)/shard_map/all_to_all | solution.py:105
  116.2 12.9 %collective-permute-start.1 = (bf16[224,512]{1,0:T(8,128)(2,1)S(1)}, bf16[224,512]{1,0:T(8,128)(2,1)S(1)}, u32[]{:S(2)}, u32[]{:S(2)}) collective-permute-start(bf16[224,512]{1,0:T(8,128)(2,1)S(1)} %pad_maximum_fusion.4), channel_id=1, source_target_pairs={{0,2},{1,3},{2,4},{3,5},{4,6},{5,7},{6,0},{7,1},{8,10},{9,11},{10,... | collective-permute-start | bytes 688136 | tf_op jit(solution)/shard_map/ppermute | solution.py:124
  118.7 15.5 %collective-permute-start.2 = (bf16[224,512]{1,0:T(8,128)(2,1)S(1)}, bf16[224,512]{1,0:T(8,128)(2,1)S(1)}, u32[]{:S(2)}, u32[]{:S(2)}) collective-permute-start(bf16[224,512]{1,0:T(8,128)(2,1)S(1)} %pad_maximum_fusion.5), channel_id=1, source_target_pairs={{0,6},{1,7},{2,0},{3,1},{4,2},{5,3},{6,4},{7,5},{8,14},{9,15},{10,... | collective-permute-start | bytes 688136 | tf_op jit(solution)/shard_map/ppermute | solution.py:124
  122.1 12.1 %collective-permute-start.3 = (bf16[224,512]{1,0:T(8,128)(2,1)S(1)}, bf16[224,512]{1,0:T(8,128)(2,1)S(1)}, u32[]{:S(2)}, u32[]{:S(2)}) collective-permute-start(bf16[224,512]{1,0:T(8,128)(2,1)S(1)} %pad_maximum_fusion.6), channel_id=1, source_target_pairs={{0,4},{1,5},{2,6},{3,7},{4,0},{5,1},{6,2},{7,3},{8,12},{9,13},{10,... | collective-permute-start | bytes 688136 | tf_op jit(solution)/shard_map/ppermute | solution.py:124
  134.6 0.8 copy-start.5
  149.5 10.0 %collective-permute-start.4 = (f32[4,32,512]{2,1,0:T(8,128)S(1)}, f32[4,32,512]{2,1,0:T(8,128)S(1)}, u32[]{:S(2)}, u32[]{:S(2)}) collective-permute-start(f32[4,32,512]{2,1,0:T(8,128)S(1)} %dynamic-slice_bitcast_fusion.1), channel_id=1, source_target_pairs={{0,1},{1,0},{2,3},{3,2},{4,5},{5,4},{6,7},{7,6},{8,9},{9,8},{10,11... | collective-permute-start | bytes 786440 | tf_op jit(solution)/shard_map/ppermute | solution.py:91
  152.3 28.8 %all-to-all-start.2 = ((bf16[64,8,242]{2,1,0:T(8,128)(2,1)}), bf16[64,8,242]{2,1,0:T(8,128)(2,1)S(1)}, u32[]{:S(2)}, u32[]{:S(2)}) async-start(bf16[64,8,242]{2,1,0:T(8,128)(2,1)} %pad_maximum_fusion.3), calls=%async_computation.2 | async-start | bytes 524288 | tf_op jit(solution)/shard_map/all_to_all | solution.py:140
  159.6 10.7 %collective-permute-start.7 = (f32[32,512]{1,0:T(8,128)S(1)}, f32[32,512]{1,0:T(8,128)S(1)}, u32[]{:S(2)}, u32[]{:S(2)}) collective-permute-start(f32[32,512]{1,0:T(8,128)S(1)} %get-tuple-element.39), channel_id=1, source_target_pairs={{0,4},{1,5},{2,6},{3,7},{4,0},{5,1},{6,2},{7,3},{8,12},{9,13},{10,... | collective-permute-start | bytes 196616 | tf_op jit(solution)/shard_map/ppermute | solution.py:158
  163.2 7.4 %collective-permute-start.6 = (f32[32,512]{1,0:T(8,128)S(1)}, f32[32,512]{1,0:T(8,128)S(1)}, u32[]{:S(2)}, u32[]{:S(2)}) collective-permute-start(f32[32,512]{1,0:T(8,128)S(1)} %get-tuple-element.40), channel_id=1, source_target_pairs={{0,6},{1,7},{2,0},{3,1},{4,2},{5,3},{6,4},{7,5},{8,14},{9,15},{10,... | collective-permute-start | bytes 196616 | tf_op jit(solution)/shard_map/ppermute | solution.py:158
  165.2 7.0 %collective-permute-start.5 = (f32[32,512]{1,0:T(8,128)S(1)}, f32[32,512]{1,0:T(8,128)S(1)}, u32[]{:S(2)}, u32[]{:S(2)}) collective-permute-start(f32[32,512]{1,0:T(8,128)S(1)} %get-tuple-element.38), channel_id=1, source_target_pairs={{0,2},{1,3},{2,4},{3,5},{4,6},{5,7},{6,0},{7,1},{8,10},{9,11},{10,... | collective-permute-start | bytes 196616 | tf_op jit(solution)/shard_map/ppermute | solution.py:158

commit v2 on v1

v2 whole, which is shorter than its diff:
```python
import functools
import math

import jax
import jax.numpy as jnp
from jax import lax
from jax.experimental import pallas as pl
from jax.experimental.pallas import tpu as pltpu
from jax.sharding import PartitionSpec as P

BF = jnp.bfloat16
F32 = jnp.float32
I32 = jnp.int32
MIB = 1 << 20
TILE = 512
WHOLE = pl.BlockSpec(memory_space=pltpu.VMEM)
SCALARS = pl.BlockSpec(memory_space=pltpu.SMEM)


def dot(left, right, left_dim=1, right_dim=0):
    return lax.dot_general(
        left, right, (((left_dim,), (right_dim,)), ((), ())), preferred_element_type=F32
    )


def halves(values):
    high = values.astype(BF)
    return high, (values - high.astype(F32)).astype(BF)


def onehot(index, shape, axis):
    return jnp.where(index == lax.broadcasted_iota(I32, shape, axis), 1.0, 0.0).astype(BF)


def params(mib):
    return pltpu.CompilerParams(vmem_limit_bytes=mib * MIB)


def cost(flops, nbytes):
    return pl.CostEstimate(flops=flops, bytes_accessed=nbytes, transcendentals=0)


def answer_kernel(asked_ref, node_ref, out_ref):
    own_count, slots = node_ref.shape[0], asked_ref.shape[1]
    pick = onehot(asked_ref[...], (own_count, slots), 0)
    out_ref[...] = dot(pick, node_ref[...], 0, 0).astype(BF)


def pair_kernel(
    scale, live_ref, cols_ref, slots_ref, node_ref, rep_ref, wf_ref, ws_ref, wt_ref,
    slot_out, first_out, bfirst_out, bsecond_out, extra_out, acc,
):
    step = pl.program_id(0)
    tile = cols_ref.shape[0]
    own_count, width = node_ref.shape
    slots = rep_ref.shape[0]
    hidden2 = ws_ref.shape[1]

    @pl.when(step == 0)
    def _():
        acc[...] = jnp.zeros_like(acc)
        extra_out[...] = jnp.zeros_like(extra_out)

    near = dot(onehot(cols_ref[:, 0:1], (tile, own_count), 1), node_ref[...])
    far = dot(onehot(cols_ref[:, 1:2], (tile, slots), 1), rep_ref[...])
    target = cols_ref[:, 2:3].astype(F32)
    product = (near * far).astype(BF)
    near_b = near.astype(BF)
    pre_first = (
        dot(near_b, wf_ref[:width])
        + dot(far.astype(BF), wf_ref[width : 2 * width])
        + dot(product, wf_ref[2 * width :])
    )
    sig = jax.nn.sigmoid(pre_first)
    first = (pre_first * sig).astype(BF)
    slope_first = sig * (1.0 + pre_first * (1.0 - sig))
    first_out[...] = first
    pre_second = dot(first, ws_ref[...])
    sig = jax.nn.sigmoid(pre_second)
    second = (pre_second * sig).astype(BF).astype(F32)
    slope_second = sig * (1.0 + pre_second * (1.0 - sig))
    w_third = wt_ref[...].astype(F32)
    logits = jnp.sum(second * w_third, axis=1, keepdims=True)
    place = step * tile + lax.broadcasted_iota(I32, (tile, 1), 0)
    live = jnp.where(place < live_ref[0], 1.0, 0.0)
    slope = live * (jax.nn.sigmoid(logits) - target)
    softplus = jnp.maximum(logits, 0.0) + jnp.log1p(jnp.exp(-jnp.abs(logits)))
    loss = jnp.sum(live * (softplus - target * logits), axis=0, keepdims=True)
    extra_out[0:1, :hidden2] += scale * jnp.sum(slope * second, axis=0, keepdims=True)
    extra_out[1:2, :hidden2] += jnp.broadcast_to(scale * loss, (1, hidden2))
    back_second = (slope * w_third * slope_second).astype(BF)
    bsecond_out[...] = back_second
    back_first = (dot(back_second, ws_ref[...], 1, 1) * slope_first).astype(BF)
    bfirst_out[...] = back_first
    block_b = dot(back_first, wf_ref[width : 2 * width], 1, 1)
    block_c = dot(back_first, wf_ref[2 * width :], 1, 1)
    high, low = halves(block_b + block_c * near)
    place = onehot(slots_ref[...], (slots, tile), 0)
    acc[...] += dot(place, high) + dot(place, low)

    @pl.when(step == pl.num_programs(0) - 1)
    def _():
        slot_out[...] = acc[...].astype(BF)


def weight_kernel(
    scale, n_edge, edge_ref, lines_ref, node_ref, rep_ref, first_ref, bfirst_ref, bsecond_ref, extra_ref,
    kept_out, sent_out, grads, grads2,
):
    own_count, width = node_ref.shape
    slots = rep_ref.shape[0]
    edges = lines_ref.shape[1]
    chips = n_edge // 2
    rows1 = 3 * width // n_edge
    rows2 = grads2.shape[0] // n_edge
    bfirst = bfirst_ref[...]
    near = dot(node_ref[...], onehot(lines_ref[0:1, :], (own_count, edges), 0), 0, 0)
    grads[:width] = scale * dot(near.astype(BF), bfirst)
    far = dot(rep_ref[...], onehot(lines_ref[1:2, :], (slots, edges), 0), 0, 0)
    grads[width : 2 * width] = scale * dot(far.astype(BF), bfirst)
    grads[2 * width :] = scale * dot((near * far).astype(BF), bfirst)
    grads2[...] = scale * dot(bsecond_ref[...], first_ref[...], 0, 0)
    edge = edge_ref[0]
    chip = edge // 2
    core = edge % 2
    for j in range(chips):
        there = 2 * ((chip + j) % chips)
        for out, owner in ((kept_out, there + core), (sent_out, there + 1 - core)):
            out[j, :rows1] = grads[pl.ds(pl.multiple_of(owner * rows1, 8), rows1), :]
            out[j, rows1 : rows1 + rows2] = grads2[pl.ds(pl.multiple_of(owner * rows2, 8), rows2), :]
            out[j, rows1 + rows2 :] = extra_ref[...]


def near_kernel(lines_ref, cols_ref, rep_ref, bfirst_ref, wf_ref, out_ref):
    edges = lines_ref.shape[1]
    slots, width = rep_ref.shape
    bfirst = bfirst_ref[...]
    far = dot(onehot(cols_ref[:, 1:2], (edges, slots), 1), rep_ref[...])
    block_a = dot(bfirst, wf_ref[:width], 1, 1)
    block_c = dot(bfirst, wf_ref[2 * width :], 1, 1)
    high, low = halves(block_a + block_c * far)
    place = onehot(lines_ref[0:1, :], (out_ref.shape[0], edges), 0)
    out_ref[...] = dot(place, high) + dot(place, low)


def owned_kernel(n_edge, edge_ref, asked_ref, near_ref, back_ref, kept_out, sent_out, total):
    own_count = near_ref.shape[0]
    chips = n_edge // 2
    rows = own_count // n_edge
    place = onehot(asked_ref[...], (own_count, asked_ref.shape[1]), 0)
    total[...] = near_ref[...] + dot(place, back_ref[...])
    edge = edge_ref[0]
    chip = edge // 2
    core = edge % 2
    for j in range(chips):
        there = 2 * ((chip + j) % chips)
        for out, owner in ((kept_out, there + core), (sent_out, there + 1 - core)):
            out[j] = total[pl.ds(pl.multiple_of(owner * rows, 8), rows), :]


def body(node_rows, w_first, w_second, w_third, src_row, requests, slot_index, labels, live_count):
    own_count, width = node_rows.shape
    edges = src_row.shape[0]
    parts, cap = requests.shape
    n_edge = lax.axis_size("edge")
    chips = n_edge // 2
    slots = parts * cap
    hidden, hidden2 = w_second.shape
    scale = 1.0 / math.sqrt(edges * parts * n_edge)
    edge = lax.axis_index("edge").astype(I32).reshape(1)
    sibling = [(i, i ^ 1) for i in range(n_edge)]

    def ahead(step):
        return [(i, (i + 2 * step) % n_edge) for i in range(n_edge)]

    steps = (1, chips - 1) + tuple(range(2, chips - 1))
    rows1 = 3 * width // n_edge
    rows2 = hidden2 // n_edge
    rows = rows1 + rows2
    cols = jnp.stack([src_row, slot_index, labels], axis=1)
    lines = jnp.stack([src_row, slot_index], axis=0)

    asked_here = lax.all_to_all(requests, "dom", split_axis=0, concat_axis=0, tiled=True)
    asked_line = asked_here.reshape(1, slots)
    answer = pl.pallas_call(
        answer_kernel,
        out_shape=jax.ShapeDtypeStruct((slots, width), BF),
        in_specs=[WHOLE, WHOLE],
        out_specs=WHOLE,
        compiler_params=params(8),
        name="answer",
    )(asked_line, node_rows)
    replies = lax.all_to_all(
        answer.reshape(parts, cap, width), "dom", split_axis=0, concat_axis=0, tiled=True
    ).reshape(slots, width)

    def fixed(shape):
        return pl.BlockSpec(shape, lambda i: (0,) * len(shape), pipeline_mode=pl.Buffered(1))

    def tiles(count):
        return pl.BlockSpec((TILE, count), lambda i: (i, 0))

    slot_grad, first, back_first, back_second, extra = pl.pallas_call(
        functools.partial(pair_kernel, scale),
        grid=(edges // TILE,),
        out_shape=(
            jax.ShapeDtypeStruct((slots, width), BF),
            jax.ShapeDtypeStruct((edges, hidden), BF),
            jax.ShapeDtypeStruct((edges, hidden), BF),
            jax.ShapeDtypeStruct((edges, hidden2), BF),
            jax.ShapeDtypeStruct((8, hidden), F32),
        ),
        in_specs=[
            SCALARS,
            tiles(3),
            pl.BlockSpec((1, TILE), lambda i: (0, i)),
            fixed((own_count, width)),
            fixed((slots, width)),
            fixed((3 * width, hidden)),
            fixed((hidden, hidden2)),
            fixed((1, hidden2)),
        ],
        out_specs=(
            pl.BlockSpec((slots, width), lambda i: (0, 0)),
            tiles(hidden),
            tiles(hidden),
            tiles(hidden2),
            pl.BlockSpec((8, hidden), lambda i: (0, 0)),
        ),
        scratch_shapes=[pltpu.VMEM((slots, width), F32)],
        compiler_params=params(32),
        cost_estimate=cost(6 * 10**9, 8 * MIB),
        name="pair",
    )(
        live_count, cols, slot_index.reshape(1, edges), node_rows, replies, w_first, w_second,
        w_third.reshape(1, hidden2),
    )

    returned = lax.all_to_all(
        slot_grad.reshape(parts, cap, width), "dom", split_axis=0, concat_axis=0, tiled=True
    ).reshape(slots, width)

    block = jax.ShapeDtypeStruct((chips, rows + 8, hidden), F32)
    kept, sent = pl.pallas_call(
        functools.partial(weight_kernel, scale, n_edge),
        out_shape=(block, block),
        in_specs=[SCALARS] + [WHOLE] * 7,
        out_specs=(WHOLE, WHOLE),
        scratch_shapes=[pltpu.VMEM((3 * width, hidden), F32), pltpu.VMEM((hidden2, hidden), F32)],
        compiler_params=params(32),
        cost_estimate=cost(3 * 10**9, 8 * MIB),
        name="weights",
    )(edge, lines, node_rows, replies, first, back_first, back_second, extra)
    chip_sum = kept + lax.ppermute(sent, "edge", sibling)
    total = chip_sum[0]
    for step in steps:
        high = lax.reduce_precision(chip_sum[step], 8, 7)
        low = chip_sum[step][rows:] - high[rows:]
        packed = jnp.concatenate([high.astype(BF), low.astype(BF)], axis=0)
        got = lax.ppermute(packed, "edge", ahead(step)).astype(F32)
        total = total + jnp.concatenate([got[:rows], got[rows : rows + 8] + got[rows + 8 :]], axis=0)

    share = hidden // parts
    small = jnp.concatenate([total[rows, :hidden2], total[rows + 1, :share]]).reshape(-1, share).T
    small_high = lax.reduce_precision(small, 8, 7)
    small_low = (small - small_high).astype(BF)
    n_small = small.shape[1]
    columns = total[:rows].T.reshape(parts, share, rows).astype(BF)
    packed = jnp.concatenate(
        [
            columns,
            jnp.broadcast_to(small_high.astype(BF), (parts, share, n_small)),
            jnp.broadcast_to(small_low, (parts, share, n_small)),
        ],
        axis=2,
    )
    got = lax.all_to_all(packed, "dom", split_axis=0, concat_axis=0, tiled=True)
    got = jnp.sum(got.astype(F32), axis=0)
    first_share = got[:, :rows1].T
    second_share = got[:, rows1:rows]
    small = got[:, rows : rows + n_small] + got[:, rows + n_small :]
    small = small.T.reshape(-1)
    third_total = small[:hidden2]
    loss_total = small[hidden2]

    near_part = pl.pallas_call(
        near_kernel,
        out_shape=jax.ShapeDtypeStruct((own_count, width), F32),
        in_specs=[WHOLE] * 5,
        out_specs=WHOLE,
        compiler_params=params(32),
        cost_estimate=cost(3 * 10**9, 4 * MIB),
        name="near",
    )(lines, cols, replies, back_first, w_first)
    block = jax.ShapeDtypeStruct((chips, own_count // n_edge, width), F32)
    kept, sent = pl.pallas_call(
        functools.partial(owned_kernel, n_edge),
        out_shape=(block, block),
        in_specs=[SCALARS] + [WHOLE] * 3,
        out_specs=(WHOLE, WHOLE),
        scratch_shapes=[pltpu.VMEM((own_count, width), F32)],
        compiler_params=params(8),
        name="owned",
    )(edge, asked_line, near_part, returned)
    node_chip = kept + lax.ppermute(sent, "edge", sibling)
    node_share = node_chip[0]
    for step in steps:
        node_share = node_share + lax.ppermute(node_chip[step], "edge", ahead(step))
    return (first_share, second_share, third_total, loss_total, node_share)


def solution(mesh):
    in_specs = (
        P("dom", None),
        P(),
        P(),
        P(),
        P(("dom", "edge")),
        P(("dom", "edge"), None),
        P(("dom", "edge")),
        P(("dom", "edge")),
        P(("dom", "edge")),
    )
    out_specs = (P("edge", "dom"), P("dom", "edge"), P(), P(), P(("dom", "edge"), None))
    return jax.shard_map(body, mesh=mesh, in_specs=in_specs, out_specs=out_specs, check_vma=False)
```

time: 185 us -> 174 us (0.941)
  matrix products: 20.5 us -> 0 us
  Pallas kernels: 0 us -> 15.2 us
  local copies, waits for them, and re-layouts: 26.1 us -> 12.3 us
  waiting for transfers between devices: 47.6 us -> 59.9 us
  other arithmetic: 11.7 us -> 8.62 us
    dot_general x13 -> x0, matrix products: 20.5 us -> none  [the longest x2 5.14 us: collect(): jnp.dot(onehot, high, preferred_element_type=F32)]
    pallas_call x0 -> x5, Pallas kernels: none -> 15.2 us  [the longest x1 8.28 us: body(): pl.pallas_call(functools.partial(pair_kernel, scale), grid=(edges // TILE...]
    gather x3 -> x0, local copies, waits for them, and re-layouts: 12.7 us -> none  [the longest x1 5.03 us: body(): near_rows = jnp.take(node_rows, src_row, axis=0, mode='clip')]
    all_to_all x3, waiting for transfers between devices: 40.8 us -> 50.5 us  [the longest x1 29.7 us: body(): lax.all_to_all(answer.reshape(parts, cap, width), 'dom', split_axis=0, co...]
    ppermute x2, waiting for transfers between devices: 0.01 us -> 5.16 us  [the longest x1 3.66 us: body(): chip_sum = kept + lax.ppermute(sent, 'edge', sibling)]
    ppermute x3, waiting for transfers between devices: 4.97 us -> 0.01 us  [body(): got = lax.ppermute(packed, 'edge', ahead(step)).astype(F32)]
    ppermute x3, waiting for transfers between devices: 1.88 us -> 4.31 us  [body(): node_share = node_share + lax.ppermute(node_chip[step], 'edge', ahead(step))]
    add x2, other arithmetic: 2.45 us -> 0.43 us  [the longest x1 0.39 us: body(): chip_sum = kept + lax.ppermute(sent, 'edge', sibling)]
  transfers between devices with their start and end apart: 11 -> 11, of which waited for: 6 -> 6; matrix products, arithmetic and copies ran while one was open for 12% -> 7% of each run, Pallas kernels for 0% -> 2%
where the time goes in v2:
time: 174 us; the launch traced here: 172 us
  waiting for transfers between devices  59.9 us (34%)
  starting transfers between devices  41.3 us (24%)
  blocking collectives  32.9 us (19%)
  Pallas kernels  15.2 us (9%)
  local copies, waits for them, and re-layouts  12.3 us (7%)
  other arithmetic  8.62 us (5%)
    all_to_all x1, blocking collectives, body(): lax.all_to_all(requests, 'dom', split_axis=0, concat_axis=0, tiled=True)  32.9 us
    all_to_all x1, waiting for transfers between devices, body(): lax.all_to_all(answer.reshape(parts, cap, width), 'dom', split_axis=0, co...  29.7 us
    all_to_all x1, waiting for transfers between devices, body(): lax.all_to_all(slot_grad.reshape(parts, cap, width), 'dom', split_axis=0,...  20.8 us
    ppermute x3, starting transfers between devices, body(): got = lax.ppermute(packed, 'edge', ahead(step)).astype(F32)  9.72 us
    ppermute x3, starting transfers between devices, body(): node_share = node_share + lax.ppermute(node_chip[step], 'edge', ahead(step))  9.27 us
    pallas_call x1, Pallas kernels, body(): pl.pallas_call(functools.partial(pair_kernel, scale), grid=(edges // TILE...  8.28 us
    all_to_all x1, starting transfers between devices, body(): got = lax.all_to_all(packed, 'dom', split_axis=0, concat_axis=0, tiled=True)  7.08 us
    all_to_all x1, starting transfers between devices, body(): lax.all_to_all(slot_grad.reshape(parts, cap, width), 'dom', split_axis=0,...  6.76 us
  transfers between devices with their start and end apart: 11, of which 6 were waited for; matrix products, arithmetic and copies ran while one was open for 7% of the time, Pallas kernels for 2%

profile of v2, /device:TPU:6, one launch (start us, length us, event | category | flops | bytes accessed | tf_op | source)
XLA Modules:
  0.0 172.1 jit_solution(9597715042086820596)
XLA Ops:
  1.5 32.9 %all_to_all.24 = s32[64,1,8]{2,1,0:T(1,128)S(1)} all-to-all(s32[64,1,8]{2,1,0:T(1,128)S(1)} %bitcast.71), channel_id=1, replica_groups=mesh['dom'=64,'edge'=8] {'dom'}, dimensions={0} | all-to-all | bytes 4096 | tf_op jit(solution)/shard_map/all_to_all | solution.py:183
  35.8 0.9 copy-done
  36.7 1.1 answer.1
  37.9 4.6 %all-to-all-start.1 = ((bf16[64,8,512]{2,1,0:T(8,128)(2,1)}), bf16[64,8,512]{2,1,0:T(8,128)(2,1)S(1)}, u32[]{:S(2)}, u32[]{:S(2)}) async-start(bf16[64,8,512]{2,1,0:T(8,128)(2,1)} %bitcast.4), calls=%async_computation.1 | async-start | bytes 1048576 | tf_op jit(solution)/shard_map/all_to_all | solution.py:193
  43.5 29.7 %all-to-all-done.1 = bf16[64,8,512]{2,1,0:T(8,128)(2,1)S(1)} async-done(((bf16[64,8,512]{2,1,0:T(8,128)(2,1)}), bf16[64,8,512]{2,1,0:T(8,128)(2,1)S(1)}, u32[]{:S(2)}, u32[]{:S(2)}) %all-to-all-start.1) | async-done | bytes 524320 | tf_op jit(solution)/shard_map/all_to_all | solution.py:193
  73.2 8.3 %pair.1 = (bf16[512,512]{1,0:T(8,128)(2,1)}, bf16[1024,512]{1,0:T(8,128)(2,1)S(1)}, bf16[1024,512]{1,0:T(8,128)(2,1)S(1)}, bf16[1024,128]{1,0:T(8,128)(2,1)S(1)}, f32[8,512]{1,0:T(8,128)S(1)}) custom-call(s32[1]{0:T(128)S(6)} %copy.40.live_ref, s32[1024,3]{1,0:T(8,128)S(1)} %copy.34.cols_ref, s32[1,1024]{1,0:T(1,128)S(1)} %bitcast.68, ...), custom_call_target="tpu_custom_call" | custom-call | flops 6000000000 | bytes 8388608 | tf_op jit(solution)/shard_map/pair/pallas_call | solution.py:203
  81.5 3.0 %weights.1 = (f32[4,216,512]{2,1,0:T(8,128)S(1)}, f32[4,216,512]{2,1,0:T(8,128)S(1)}) custom-call(s32[1]{0:T(128)} %bitcast.edge_ref, s32[2,1024]{1,0:T(2,128)S(1)} %pad_add_fusion.1.lines_ref, bf16[256,512]{1,0:T(8,128)(2,1)S(1)} %copy-done.1, bf16[512,512]{1,0:T(8,128)(2,1)S(1)} %bitcast.64, bf16[1024,512]{1,0:T(8,128)(2,1)S(1)} %get-tuple-element.14.first_ref, ...), custom_call_target="tpu_custom_call" | custom-call | flops 3000000000 | bytes 8388608 | tf_op jit(solution)/shard_map/weights/pallas_call | solution.py:244
  84.4 1.9 %collective-permute-start = (f32[4,216,512]{2,1,0:T(8,128)S(1)}, f32[4,216,512]{2,1,0:T(8,128)S(1)}, u32[]{:S(2)}, u32[]{:S(2)}) collective-permute-start(f32[4,216,512]{2,1,0:T(8,128)S(1)} %get-tuple-element.19), channel_id=1, source_target_pairs={{0,1},{1,0},{2,3},{3,2},{4,5},{5,4},{6,7},{7,6},{8,9},{9,8},{10,11... | collective-permute-start | bytes 5308424 | tf_op jit(solution)/shard_map/ppermute | solution.py:254
  86.4 3.7 %collective-permute-done = f32[4,216,512]{2,1,0:T(8,128)S(1)} collective-permute-done((f32[4,216,512]{2,1,0:T(8,128)S(1)}, f32[4,216,512]{2,1,0:T(8,128)S(1)}, u32[]{:S(2)}, u32[]{:S(2)}) %collective-permute-start) | collective-permute-done | bytes 1769504 | tf_op jit(solution)/shard_map/ppermute | solution.py:254
  90.7 0.9 pad_maximum_fusion.2
  91.7 2.7 %collective-permute-start.2 = (bf16[224,512]{1,0:T(8,128)(2,1)}, bf16[224,512]{1,0:T(8,128)(2,1)S(1)}, u32[]{:S(2)}, u32[]{:S(2)}) collective-permute-start(bf16[224,512]{1,0:T(8,128)(2,1)} %pad_maximum_fusion.2), channel_id=1, source_target_pairs={{0,6},{1,7},{2,0},{3,1},{4,2},{5,3},{6,4},{7,5},{8,14},{9,15},{10,... | collective-permute-start | bytes 688136 | tf_op jit(solution)/shard_map/ppermute | solution.py:260
  95.1 3.0 %collective-permute-start.3 = (bf16[224,512]{1,0:T(8,128)(2,1)}, bf16[224,512]{1,0:T(8,128)(2,1)}, u32[]{:S(2)}, u32[]{:S(2)}) collective-permute-start(bf16[224,512]{1,0:T(8,128)(2,1)} %pad_maximum_fusion.3), channel_id=1, source_target_pairs={{0,4},{1,5},{2,6},{3,7},{4,0},{5,1},{6,2},{7,3},{8,12},{9,13},{10,... | collective-permute-start | bytes 688136 | tf_op jit(solution)/shard_map/ppermute | solution.py:260
  98.9 4.0 %collective-permute-start.1 = (bf16[224,512]{1,0:T(8,128)(2,1)}, bf16[224,512]{1,0:T(8,128)(2,1)}, u32[]{:S(2)}, u32[]{:S(2)}) collective-permute-start(bf16[224,512]{1,0:T(8,128)(2,1)} %pad_maximum_fusion.1), channel_id=1, source_target_pairs={{0,2},{1,3},{2,4},{3,5},{4,6},{5,7},{6,0},{7,1},{8,10},{9,11},{10,... | collective-permute-start | bytes 688136 | tf_op jit(solution)/shard_map/ppermute | solution.py:260
  102.9 6.8 %all-to-all-start.3 = ((bf16[64,8,512]{2,1,0:T(8,128)(2,1)}), bf16[64,8,512]{2,1,0:T(8,128)(2,1)S(1)}, u32[]{:S(2)}, u32[]{:S(2)}) async-start(bf16[64,8,512]{2,1,0:T(8,128)(2,1)} %bitcast.25), calls=%async_computation.3 | async-start | bytes 1048576 | tf_op jit(solution)/shard_map/all_to_all | solution.py:239
  109.7 1.0 slice.161
  110.6 1.0 convert_element_type.75
  111.7 1.0 slice.149
  112.7 1.0 convert_element_type.65
  113.7 1.2 fusion.2
  115.9 1.7 %fusion.3 = bf16[512,208]{0,1:T(8,128)(2,1)} fusion(f32[216,512]{1,0:T(8,128)} %copy-done.9), kind=kLoop, calls=%fused_computation.16 | loop fusion | bytes 425984 | tf_op jit(solution)/shard_map/convert_element_type | solution.py:268
  117.6 1.1 copy.35
  119.6 20.8 %all-to-all-done.3 = bf16[64,8,512]{2,1,0:T(8,128)(2,1)S(1)} async-done(((bf16[64,8,512]{2,1,0:T(8,128)(2,1)}), bf16[64,8,512]{2,1,0:T(8,128)(2,1)S(1)}, u32[]{:S(2)}, u32[]{:S(2)}) %all-to-all-start.3) | async-done | bytes 524320 | tf_op jit(solution)/shard_map/all_to_all | solution.py:239
  140.4 7.1 %all-to-all-start.2 = ((bf16[64,8,242]{2,1,0:T(8,128)(2,1)}), bf16[64,8,242]{2,1,0:T(8,128)(2,1)S(1)}, u32[]{:S(2)}, u32[]{:S(2)}) async-start(bf16[64,8,242]{2,1,0:T(8,128)(2,1)} %pad_maximum_fusion), calls=%async_computation.2 | async-start | bytes 524288 | tf_op jit(solution)/shard_map/all_to_all | solution.py:277
  147.5 1.2 copy-done.7
  148.7 2.5 %near.1.near_ref = f32[256,512]{1,0:T(8,128)S(1)} custom-call(s32[2,1024]{1,0:T(2,128)S(1)} %pad_add_fusion.1.lines_ref, s32[1024,3]{1,0:T(8,128)S(1)} %copy.34.cols_ref, bf16[512,512]{1,0:T(8,128)(2,1)S(1)} %bitcast.65, bf16[1024,512]{1,0:T(8,128)(2,1)S(1)} %copy-done.7, bf16[1536,512]{1,0:T(8,128)(2,1)S(1)} %copy-done.3), custom_call_target="tpu_custom_call" | custom-call | flops 3000000000 | bytes 4194304 | tf_op jit(solution)/shard_map/near/pallas_call | solution.py:286
  151.5 1.9 %collective-permute-start.4 = (f32[4,32,512]{2,1,0:T(8,128)S(1)}, f32[4,32,512]{2,1,0:T(8,128)S(1)}, u32[]{:S(2)}, u32[]{:S(2)}) collective-permute-start(f32[4,32,512]{2,1,0:T(8,128)S(1)} %get-tuple-element.22), channel_id=1, source_target_pairs={{0,1},{1,0},{2,3},{3,2},{4,5},{5,4},{6,7},{7,6},{8,9},{9,8},{10,11... | collective-permute-start | bytes 786440 | tf_op jit(solution)/shard_map/ppermute | solution.py:305
  153.5 1.5 collective-permute-done.4
  155.0 2.8 %collective-permute-start.5 = (f32[32,512]{1,0:T(8,128)S(1)}, f32[32,512]{1,0:T(8,128)S(1)}, u32[]{:S(2)}, u32[]{:S(2)}) collective-permute-start(f32[32,512]{1,0:T(8,128)S(1)} %get-tuple-element.32), channel_id=1, source_target_pairs={{0,2},{1,3},{2,4},{3,5},{4,6},{5,7},{6,0},{7,1},{8,10},{9,11},{10,... | collective-permute-start | bytes 196616 | tf_op jit(solution)/shard_map/ppermute | solution.py:308
  157.8 3.4 %collective-permute-start.7 = (f32[32,512]{1,0:T(8,128)S(1)}, f32[32,512]{1,0:T(8,128)S(1)}, u32[]{:S(2)}, u32[]{:S(2)}) collective-permute-start(f32[32,512]{1,0:T(8,128)S(1)} %get-tuple-element.33), channel_id=1, source_target_pairs={{0,4},{1,5},{2,6},{3,7},{4,0},{5,1},{6,2},{7,3},{8,12},{9,13},{10,... | collective-permute-start | bytes 196616 | tf_op jit(solution)/shard_map/ppermute | solution.py:308
  161.3 3.0 %collective-permute-start.6 = (f32[32,512]{1,0:T(8,128)S(1)}, f32[32,512]{1,0:T(8,128)S(1)}, u32[]{:S(2)}, u32[]{:S(2)}) collective-permute-start(f32[32,512]{1,0:T(8,128)S(1)} %get-tuple-element.34), channel_id=1, source_target_pairs={{0,6},{1,7},{2,0},{3,1},{4,2},{5,3},{6,4},{7,5},{8,14},{9,15},{10,... | collective-permute-start | bytes 196616 | tf_op jit(solution)/shard_map/ppermute | solution.py:308
  164.3 1.2 collective-permute-done.7
  165.5 3.2 %collective-permute-done.6 = f32[32,512]{1,0:T(8,128)S(1)} collective-permute-done((f32[32,512]{1,0:T(8,128)S(1)}, f32[32,512]{1,0:T(8,128)S(1)}, u32[]{:S(2)}, u32[]{:S(2)}) %collective-permute-start.6) | collective-permute-done | bytes 65568 | tf_op jit(solution)/shard_map/ppermute | solution.py:308
  (66 shorter events, 10.3 us)
Async XLA Ops:
  0.6 42.5 %copy-start.10 = (s32[1024]{0:T(1024)S(1)}, s32[1024]{0:T(1024)}, u32[]{:S(2)}) copy-start(s32[1024]{0:T(1024)} %param.13) | copy-start | bytes 12292
  0.6 42.5 %copy-start.2 = (s32[1024]{0:T(1024)S(1)}, s32[1024]{0:T(1024)}, u32[]{:S(2)}) copy-start(s32[1024]{0:T(1024)} %param.15) | copy-start | bytes 12292
  0.7 42.5 %copy-start.11 = (s32[1024]{0:T(1024)S(1)}, s32[1024]{0:T(1024)}, u32[]{:S(2)}) copy-start(s32[1024]{0:T(1024)} %param.16) | copy-start | bytes 12292
  0.7 72.5 %copy-start.5 = (bf16[128]{0:T(256)(128)(2,1)S(1)}, bf16[128]{0:T(256)(128)(2,1)}, u32[]{:S(2)}) copy-start(bf16[128]{0:T(256)(128)(2,1)} %param.12) | copy-start | bytes 772
  0.7 72.5 %copy-start.4 = (bf16[512,128]{1,0:T(8,128)(2,1)S(1)}, bf16[512,128]{1,0:T(8,128)(2,1)}, u32[]{:S(2)}) copy-start(bf16[512,128]{1,0:T(8,128)(2,1)} %ws_ref.1) | copy-start | bytes 393220
  35.8 1.0 copy-start
  36.7 36.4 %copy-start.1 = (bf16[256,512]{1,0:T(8,128)(2,1)S(1)}, bf16[256,512]{1,0:T(8,128)(2,1)}, u32[]{:S(2)}) copy-start(bf16[256,512]{1,0:T(8,128)(2,1)} %node_ref.5) | copy-start | bytes 786436
  36.7 36.4 %copy-start.3 = (bf16[1536,512]{1,0:T(8,128)(2,1)S(1)}, bf16[1536,512]{1,0:T(8,128)(2,1)}, u32[]{:S(2)}) copy-start(bf16[1536,512]{1,0:T(8,128)(2,1)} %wf_ref.3) | copy-start | bytes 4718596
  37.9 35.3 %all-to-all-start.1 = ((bf16[64,8,512]{2,1,0:T(8,128)(2,1)}), bf16[64,8,512]{2,1,0:T(8,128)(2,1)S(1)}, u32[]{:S(2)}, u32[]{:S(2)}) async-start(bf16[64,8,512]{2,1,0:T(8,128)(2,1)} %bitcast.4), calls=%async_computation.1 | async-start | bytes 1048576 | tf_op jit(solution)/shard_map/all_to_all | solution.py:193
  81.5 3.0 %copy-start.6 = (bf16[1024,512]{1,0:T(8,128)(2,1)}, bf16[1024,512]{1,0:T(8,128)(2,1)S(1)}, u32[]{:S(2)}) copy-start(bf16[1024,512]{1,0:T(8,128)(2,1)S(1)} %get-tuple-element.15.bfirst_ref) | copy-start | bytes 3145732
  84.4 5.6 %collective-permute-start = (f32[4,216,512]{2,1,0:T(8,128)S(1)}, f32[4,216,512]{2,1,0:T(8,128)S(1)}, u32[]{:S(2)}, u32[]{:S(2)}) collective-permute-start(f32[4,216,512]{2,1,0:T(8,128)S(1)} %get-tuple-element.19), channel_id=1, source_target_pairs={{0,1},{1,0},{2,3},{3,2},{4,5},{5,4},{6,7},{7,6},{8,9},{9,8},{10,11... | collective-permute-start | bytes 5308424 | tf_op jit(solution)/shard_map/ppermute | solution.py:254
  90.4 1.3 copy-start.8
  91.7 19.9 %collective-permute-start.2 = (bf16[224,512]{1,0:T(8,128)(2,1)}, bf16[224,512]{1,0:T(8,128)(2,1)S(1)}, u32[]{:S(2)}, u32[]{:S(2)}) collective-permute-start(bf16[224,512]{1,0:T(8,128)(2,1)} %pad_maximum_fusion.2), channel_id=1, source_target_pairs={{0,6},{1,7},{2,0},{3,1},{4,2},{5,3},{6,4},{7,5},{8,14},{9,15},{10,... | collective-permute-start | bytes 688136 | tf_op jit(solution)/shard_map/ppermute | solution.py:260
  95.1 14.5 %collective-permute-start.3 = (bf16[224,512]{1,0:T(8,128)(2,1)}, bf16[224,512]{1,0:T(8,128)(2,1)}, u32[]{:S(2)}, u32[]{:S(2)}) collective-permute-start(bf16[224,512]{1,0:T(8,128)(2,1)} %pad_maximum_fusion.3), channel_id=1, source_target_pairs={{0,4},{1,5},{2,6},{3,7},{4,0},{5,1},{6,2},{7,3},{8,12},{9,13},{10,... | collective-permute-start | bytes 688136 | tf_op jit(solution)/shard_map/ppermute | solution.py:260
  98.9 12.9 %collective-permute-start.1 = (bf16[224,512]{1,0:T(8,128)(2,1)}, bf16[224,512]{1,0:T(8,128)(2,1)}, u32[]{:S(2)}, u32[]{:S(2)}) collective-permute-start(bf16[224,512]{1,0:T(8,128)(2,1)} %pad_maximum_fusion.1), channel_id=1, source_target_pairs={{0,2},{1,3},{2,4},{3,5},{4,6},{5,7},{6,0},{7,1},{8,10},{9,11},{10,... | collective-permute-start | bytes 688136 | tf_op jit(solution)/shard_map/ppermute | solution.py:260
  102.9 37.5 %all-to-all-start.3 = ((bf16[64,8,512]{2,1,0:T(8,128)(2,1)}), bf16[64,8,512]{2,1,0:T(8,128)(2,1)S(1)}, u32[]{:S(2)}, u32[]{:S(2)}) async-start(bf16[64,8,512]{2,1,0:T(8,128)(2,1)} %bitcast.25), calls=%async_computation.3 | async-start | bytes 1048576 | tf_op jit(solution)/shard_map/all_to_all | solution.py:239
  114.9 0.8 copy-start.9
  140.4 28.9 %all-to-all-start.2 = ((bf16[64,8,242]{2,1,0:T(8,128)(2,1)}), bf16[64,8,242]{2,1,0:T(8,128)(2,1)S(1)}, u32[]{:S(2)}, u32[]{:S(2)}) async-start(bf16[64,8,242]{2,1,0:T(8,128)(2,1)} %pad_maximum_fusion), calls=%async_computation.2 | async-start | bytes 524288 | tf_op jit(solution)/shard_map/all_to_all | solution.py:277
  147.5 1.2 copy-start.7
  151.5 3.4 %collective-permute-start.4 = (f32[4,32,512]{2,1,0:T(8,128)S(1)}, f32[4,32,512]{2,1,0:T(8,128)S(1)}, u32[]{:S(2)}, u32[]{:S(2)}) collective-permute-start(f32[4,32,512]{2,1,0:T(8,128)S(1)} %get-tuple-element.22), channel_id=1, source_target_pairs={{0,1},{1,0},{2,3},{3,2},{4,5},{5,4},{6,7},{7,6},{8,9},{9,8},{10,11... | collective-permute-start | bytes 786440 | tf_op jit(solution)/shard_map/ppermute | solution.py:305
  155.0 9.3 %collective-permute-start.5 = (f32[32,512]{1,0:T(8,128)S(1)}, f32[32,512]{1,0:T(8,128)S(1)}, u32[]{:S(2)}, u32[]{:S(2)}) collective-permute-start(f32[32,512]{1,0:T(8,128)S(1)} %get-tuple-element.32), channel_id=1, source_target_pairs={{0,2},{1,3},{2,4},{3,5},{4,6},{5,7},{6,0},{7,1},{8,10},{9,11},{10,... | collective-permute-start | bytes 196616 | tf_op jit(solution)/shard_map/ppermute | solution.py:308
  157.8 7.7 %collective-permute-start.7 = (f32[32,512]{1,0:T(8,128)S(1)}, f32[32,512]{1,0:T(8,128)S(1)}, u32[]{:S(2)}, u32[]{:S(2)}) collective-permute-start(f32[32,512]{1,0:T(8,128)S(1)} %get-tuple-element.33), channel_id=1, source_target_pairs={{0,4},{1,5},{2,6},{3,7},{4,0},{5,1},{6,2},{7,3},{8,12},{9,13},{10,... | collective-permute-start | bytes 196616 | tf_op jit(solution)/shard_map/ppermute | solution.py:308
  161.3 7.4 %collective-permute-start.6 = (f32[32,512]{1,0:T(8,128)S(1)}, f32[32,512]{1,0:T(8,128)S(1)}, u32[]{:S(2)}, u32[]{:S(2)}) collective-permute-start(f32[32,512]{1,0:T(8,128)S(1)} %get-tuple-element.34), channel_id=1, source_target_pairs={{0,6},{1,7},{2,0},{3,1},{4,2},{5,3},{6,4},{7,5},{8,14},{9,15},{10,... | collective-permute-start | bytes 196616 | tf_op jit(solution)/shard_map/ppermute | solution.py:308

commit v3 on v2

--- a/solution.py
+++ b/solution.py
@@ -14,6 +14,7 @@
 MIB = 1 << 20
 TILE = 512
 WHOLE = pl.BlockSpec(memory_space=pltpu.VMEM)
+FREE = pl.CostEstimate(flops=0, bytes_accessed=0, transcendentals=0)
 SCALARS = pl.BlockSpec(memory_space=pltpu.SMEM)
 
 
@@ -156,6 +157,65 @@
         there = 2 * ((chip + j) % chips)
         for out, owner in ((kept_out, there + core), (sent_out, there + 1 - core)):
             out[j] = total[pl.ds(pl.multiple_of(owner * rows, 8), rows), :]
+
+
+def chip_kernel(rows, kept_ref, got_ref, own_out, *packs):
+    own_out[...] = kept_ref[0] + got_ref[0]
+    for j, out in enumerate(packs):
+        high, low = halves(kept_ref[j + 1] + got_ref[j + 1])
+        out[: rows + 8] = high
+        out[rows + 8 :] = low[rows:]
+
+
+def total_kernel(parts, n_second, *refs):
+    own_ref, gots, out_ref = refs[0], refs[1:-2], refs[-1]
+    share = own_ref.shape[1] // parts
+    rows = own_ref.shape[0] - 8
+    lanes = out_ref.shape[1]
+    total = own_ref[...]
+    for ref in gots:
+        got = ref[...].astype(F32)
+        total = total + jnp.concatenate([got[:rows], got[rows : rows + 8] + got[rows + 8 :]], axis=0)
+    hidden = total.shape[1]
+    turned = jnp.concatenate([total[:rows], jnp.zeros((lanes - rows, hidden), F32)], axis=0).T
+    third = total[rows : rows + 1, :n_second]
+    loss = total[rows + 1 : rows + 2, :1]
+    mine = lax.broadcasted_iota(I32, (hidden, n_second), 0) % share
+    mine = mine == lax.broadcasted_iota(I32, (hidden, n_second), 1) % share
+    lane = lax.broadcasted_iota(I32, (n_second, lanes), 1) - rows
+    group = lax.broadcasted_iota(I32, (n_second, lanes), 0) // share
+    groups = n_second // share
+    for part, values in enumerate(halves(third)):
+        spread = jnp.where(mine, jnp.broadcast_to(values.astype(F32), (hidden, n_second)), 0.0)
+        turned = turned + dot(
+            spread.astype(BF), jnp.where(lane == group + part * groups, 1.0, 0.0).astype(BF)
+        )
+    lane = lax.broadcasted_iota(I32, (hidden, lanes), 1) - rows - 2 * groups
+    for part, values in enumerate(halves(loss)):
+        turned = turned + jnp.where(lane == part, values.astype(F32), 0.0)
+    out_ref[...] = turned.astype(BF)
+
+
+def final_kernel(rows1, rows2, got_ref, first_out, second_out, third_out, loss_out):
+    total = jnp.sum(got_ref[...].astype(F32), axis=0)
+    share, lanes = total.shape
+    rows = rows1 + rows2
+    n_second = third_out.shape[1]
+    groups = n_second // share
+    first_out[...] = total[:, :rows1]
+    second_out[...] = total[:, rows1:rows]
+    lane = lax.broadcasted_iota(I32, (lanes, n_second), 0) - rows
+    group = lax.broadcasted_iota(I32, (lanes, n_second), 1) // share
+    take = jnp.where((lane == group) | (lane == group + groups), 1.0, 0.0)
+    spread = lax.dot_general(
+        total, take, (((1,), (0,)), ((), ())),
+        precision=lax.Precision.HIGHEST, preferred_element_type=F32,
+    )
+    mine = lax.broadcasted_iota(I32, (share, n_second), 0)
+    mine = mine == lax.broadcasted_iota(I32, (share, n_second), 1) % share
+    third_out[...] = jnp.sum(jnp.where(mine, spread, 0.0), axis=0, keepdims=True)
+    place = rows + 2 * groups
+    loss_out[...] = total[0:1, place : place + 1] + total[0:1, place + 1 : place + 2]
 
 
 def body(node_rows, w_first, w_second, w_third, src_row, requests, slot_index, labels, live_count):
@@ -248,40 +308,20 @@
         out_specs=(WHOLE, WHOLE),
         scratch_shapes=[pltpu.VMEM((3 * width, hidden), F32), pltpu.VMEM((hidden2, hidden), F32)],
         compiler_params=params(32),
-        cost_estimate=cost(3 * 10**9, 8 * MIB),
+        cost_estimate=FREE,
         name="weights",
     )(edge, lines, node_rows, replies, first, back_first, back_second, extra)
-    chip_sum = kept + lax.ppermute(sent, "edge", sibling)
-    total = chip_sum[0]
-    for step in steps:
-        high = lax.reduce_precision(chip_sum[step], 8, 7)
-        low = chip_sum[step][rows:] - high[rows:]
-        packed = jnp.concatenate([high.astype(BF), low.astype(BF)], axis=0)
-        got = lax.ppermute(packed, "edge", ahead(step)).astype(F32)
-        total = total + jnp.concatenate([got[:rows], got[rows : rows + 8] + got[rows + 8 :]], axis=0)
-
-    share = hidden // parts
-    small = jnp.concatenate([total[rows, :hidden2], total[rows + 1, :share]]).reshape(-1, share).T
-    small_high = lax.reduce_precision(small, 8, 7)
-    small_low = (small - small_high).astype(BF)
-    n_small = small.shape[1]
-    columns = total[:rows].T.reshape(parts, share, rows).astype(BF)
-    packed = jnp.concatenate(
-        [
-            columns,
-            jnp.broadcast_to(small_high.astype(BF), (parts, share, n_small)),
-            jnp.broadcast_to(small_low, (parts, share, n_small)),
-        ],
-        axis=2,
-    )
-    got = lax.all_to_all(packed, "dom", split_axis=0, concat_axis=0, tiled=True)
-    got = jnp.sum(got.astype(F32), axis=0)
-    first_share = got[:, :rows1].T
-    second_share = got[:, rows1:rows]
-    small = got[:, rows : rows + n_small] + got[:, rows + n_small :]
-    small = small.T.reshape(-1)
-    third_total = small[:hidden2]
-    loss_total = small[hidden2]
+    pack = jax.ShapeDtypeStruct((rows + 16, hidden), BF)
+    own, *packs = pl.pallas_call(
+        functools.partial(chip_kernel, rows),
+        out_shape=(jax.ShapeDtypeStruct((rows + 8, hidden), F32),) + (pack,) * (chips - 1),
+        in_specs=[WHOLE] * 2,
+        out_specs=(WHOLE,) * chips,
+        compiler_params=params(16),
+        cost_estimate=FREE,
+        name="chip",
+    )(kept, lax.ppermute(sent, "edge", sibling))
+    gots = [lax.ppermute(packs[step - 1], "edge", ahead(step)) for step in steps]
 
     near_part = pl.pallas_call(
         near_kernel,
@@ -289,9 +329,39 @@
         in_specs=[WHOLE] * 5,
         out_specs=WHOLE,
         compiler_params=params(32),
-        cost_estimate=cost(3 * 10**9, 4 * MIB),
+        cost_estimate=FREE,
         name="near",
     )(lines, cols, replies, back_first, w_first)
+
+    share = hidden // parts
+    lanes = -(-(rows + 2 * (hidden2 // share) + 2) // 128) * 128
+    packed = pl.pallas_call(
+        functools.partial(total_kernel, parts, hidden2),
+        out_shape=jax.ShapeDtypeStruct((hidden, lanes), BF),
+        in_specs=[WHOLE] * chips + [pl.BlockSpec(memory_space=pl.ANY)],
+        out_specs=WHOLE,
+        compiler_params=params(16),
+        cost_estimate=FREE,
+        name="total",
+    )(own, *gots, near_part)
+    got = lax.all_to_all(
+        packed.reshape(parts, share, lanes), "dom", split_axis=0, concat_axis=0, tiled=True
+    )
+    first_t, second_share, third_total, loss_total = pl.pallas_call(
+        functools.partial(final_kernel, rows1, rows2),
+        out_shape=(
+            jax.ShapeDtypeStruct((share, rows1), F32),
+            jax.ShapeDtypeStruct((share, rows2), F32),
+            jax.ShapeDtypeStruct((1, hidden2), F32),
+            jax.ShapeDtypeStruct((1, 1), F32),
+        ),
+        in_specs=[WHOLE],
+        out_specs=(WHOLE,) * 4,
+        compiler_params=params(8),
+        cost_estimate=FREE,
+        name="final",
+    )(got)
+
     block = jax.ShapeDtypeStruct((chips, own_count // n_edge, width), F32)
     kept, sent = pl.pallas_call(
         functools.partial(owned_kernel, n_edge),
@@ -300,13 +370,16 @@
         out_specs=(WHOLE, WHOLE),
         scratch_shapes=[pltpu.VMEM((own_count, width), F32)],
         compiler_params=params(8),
+        cost_estimate=FREE,
         name="owned",
     )(edge, asked_line, near_part, returned)
     node_chip = kept + lax.ppermute(sent, "edge", sibling)
     node_share = node_chip[0]
     for step in steps:
         node_share = node_share + lax.ppermute(node_chip[step], "edge", ahead(step))
-    return (first_share, second_share, third_total, loss_total, node_share)
+    return (
+        first_t.T, second_share, third_total.reshape(hidden2), loss_total.reshape(()), node_share
+    )
 
 
 def solution(mesh):

time: 174 us -> 157 us (0.902)
  waiting for transfers between devices: 59.9 us -> 48.7 us
  other arithmetic: 8.62 us -> 1.44 us
  local copies, waits for them, and re-layouts: 12.3 us -> 6.25 us
  starting transfers between devices: 41.3 us -> 47.3 us
  Pallas kernels: 15.2 us -> 17.1 us
    all_to_all x1, waiting for transfers between devices: 20.8 us -> 1.34 us  [body(): lax.all_to_all(slot_grad.reshape(parts, cap, width), 'dom', split_axis=0,...]
    all_to_all x1, starting transfers between devices: 7.08 us -> 13.8 us  [body(): lax.all_to_all(packed.reshape(parts, share, lanes), 'dom', split_axis=0,...]
    ppermute x4, waiting for transfers between devices: 3.66 us -> 9.76 us  [the longest x3 6.1 us: body(): lax.ppermute(packs[step - 1], 'edge', ahead(step))]
    slice x7 -> x0, local copies, waits for them, and re-layouts: 3.84 us -> none  [the longest x3 1.98 us: body(): got[:rows]]
    concatenate x5 -> x0, other arithmetic: 3.2 us -> none  [the longest x3 2.35 us: body(): packed = jnp.concatenate([high.astype(BF), low.astype(BF)], axis=0)]
    convert_element_type x2 -> x0, local copies, waits for them, and re-layouts: 2.78 us -> none  [body(): columns = total[:rows].T.reshape(parts, share, rows).astype(BF)]
    all_to_all x1, waiting for transfers between devices: 0.01 us -> 2.37 us  [body(): lax.all_to_all(packed.reshape(parts, share, lanes), 'dom', split_axis=0,...]
    convert_element_type x6 -> x0, other arithmetic: 2.23 us -> none  [the longest x3 2.01 us: body(): got = lax.ppermute(packed, 'edge', ahead(step)).astype(F32)]
  transfers between devices with their start and end apart: 11 -> 11, of which waited for: 6 -> 8; matrix products, arithmetic and copies ran while one was open for 7% -> 1% of each run, Pallas kernels for 2% -> 4%
where the time goes in v3:
time: 157 us; the launch traced here: 155 us
  waiting for transfers between devices  48.7 us (31%)
  starting transfers between devices  47.3 us (30%)
  blocking collectives  32.9 us (21%)
  Pallas kernels  17.1 us (11%)
  local copies, waits for them, and re-layouts  6.25 us (4%)
  between operations  1.57 us (1%)
    all_to_all x1, blocking collectives, body(): lax.all_to_all(requests, 'dom', split_axis=0, concat_axis=0, tiled=True)  32.9 us
    all_to_all x1, waiting for transfers between devices, body(): lax.all_to_all(answer.reshape(parts, cap, width), 'dom', split_axis=0, co...  29.7 us
    all_to_all x1, starting transfers between devices, body(): lax.all_to_all(packed.reshape(parts, share, lanes), 'dom', split_axis=0,...  13.8 us
    ppermute x3, starting transfers between devices, body(): lax.ppermute(packs[step - 1], 'edge', ahead(step))  9.29 us
    ppermute x3, starting transfers between devices, body(): node_share = node_share + lax.ppermute(node_chip[step], 'edge', ahead(step))  8.99 us
    pallas_call x1, Pallas kernels, body(): pl.pallas_call(functools.partial(pair_kernel, scale), grid=(edges // TILE...  8.18 us
    all_to_all x1, starting transfers between devices, body(): lax.all_to_all(slot_grad.reshape(parts, cap, width), 'dom', split_axis=0,...  6.75 us
    ppermute x3, waiting for transfers between devices, body(): lax.ppermute(packs[step - 1], 'edge', ahead(step))  6.1 us
  transfers between devices with their start and end apart: 11, of which 8 were waited for; matrix products, arithmetic and copies ran while one was open for 1% of the time, Pallas kernels for 4%

profile of v3, /device:TPU:6, one launch (start us, length us, event | category | flops | bytes accessed | tf_op | source)
XLA Modules:
  0.0 155.3 jit_solution(9602976475043040220)
XLA Ops:
  0.7 0.8 copy.19
  1.5 32.9 %all_to_all.24 = s32[64,1,8]{2,1,0:T(1,128)S(1)} all-to-all(s32[64,1,8]{2,1,0:T(1,128)S(1)} %bitcast.38), channel_id=1, replica_groups=mesh['dom'=64,'edge'=8] {'dom'}, dimensions={0} | all-to-all | bytes 4096 | tf_op jit(solution)/shard_map/all_to_all | solution.py:243
  34.9 0.7 reduce.3
  35.8 0.9 copy-done.4
  36.7 1.1 answer.1
  37.9 4.6 %all-to-all-start.1 = ((bf16[64,8,512]{2,1,0:T(8,128)(2,1)}), bf16[64,8,512]{2,1,0:T(8,128)(2,1)S(1)}, u32[]{:S(2)}, u32[]{:S(2)}) async-start(bf16[64,8,512]{2,1,0:T(8,128)(2,1)} %bitcast.4), calls=%async_computation.1 | async-start | bytes 1048576 | tf_op jit(solution)/shard_map/all_to_all | solution.py:253
  43.4 29.7 %all-to-all-done.1 = bf16[64,8,512]{2,1,0:T(8,128)(2,1)S(1)} async-done(((bf16[64,8,512]{2,1,0:T(8,128)(2,1)}), bf16[64,8,512]{2,1,0:T(8,128)(2,1)S(1)}, u32[]{:S(2)}, u32[]{:S(2)}) %all-to-all-start.1) | async-done | bytes 524320 | tf_op jit(solution)/shard_map/all_to_all | solution.py:253
  73.2 1.4 copy-done
  74.6 8.2 %pair.1 = (bf16[512,512]{1,0:T(8,128)(2,1)}, bf16[1024,512]{1,0:T(8,128)(2,1)S(1)}, bf16[1024,512]{1,0:T(8,128)(2,1)S(1)}, bf16[1024,128]{1,0:T(8,128)(2,1)S(1)}, f32[8,512]{1,0:T(8,128)S(1)}) custom-call(s32[1]{0:T(128)S(6)} %copy.22.live_ref, s32[1024,3]{1,0:T(8,128)S(1)} %copy.20.cols_ref, s32[1,1024]{1,0:T(1,128)S(1)} %bitcast.35, ...), custom_call_target="tpu_custom_call" | custom-call | flops 6000000000 | bytes 8388608 | tf_op jit(solution)/shard_map/pair/pallas_call | solution.py:263
  82.7 1.0 copy-done.2
  83.8 6.8 %all-to-all-start.3 = ((bf16[64,8,512]{2,1,0:T(8,128)(2,1)}), bf16[64,8,512]{2,1,0:T(8,128)(2,1)S(1)}, u32[]{:S(2)}, u32[]{:S(2)}) async-start(bf16[64,8,512]{2,1,0:T(8,128)(2,1)} %bitcast.14), calls=%async_computation.3 | async-start | bytes 1048576 | tf_op jit(solution)/shard_map/all_to_all | solution.py:299
  90.5 1.2 copy-done.3
  91.8 3.0 %weights.1 = (f32[4,216,512]{2,1,0:T(8,128)S(1)}, f32[4,216,512]{2,1,0:T(8,128)S(1)}) custom-call(s32[1]{0:T(128)} %bitcast.edge_ref, s32[2,1024]{1,0:T(2,128)S(1)} %pad_add_fusion.1.lines_ref, bf16[256,512]{1,0:T(8,128)(2,1)S(1)} %copy-done.5, bf16[512,512]{1,0:T(8,128)(2,1)S(1)} %bitcast.31, bf16[1024,512]{1,0:T(8,128)(2,1)S(1)} %copy-done.3, ...), custom_call_target="tpu_custom_call" | custom-call | tf_op jit(solution)/shard_map/weights/pallas_call | solution.py:304
  94.7 1.9 %collective-permute-start = (f32[4,216,512]{2,1,0:T(8,128)S(1)}, f32[4,216,512]{2,1,0:T(8,128)S(1)}, u32[]{:S(2)}, u32[]{:S(2)}) collective-permute-start(f32[4,216,512]{2,1,0:T(8,128)S(1)} %get-tuple-element.27), channel_id=1, source_target_pairs={{0,1},{1,0},{2,3},{3,2},{4,5},{5,4},{6,7},{7,6},{8,9},{9,8},{10,11... | collective-permute-start | bytes 5308424 | tf_op jit(solution)/shard_map/ppermute | solution.py:323
  96.7 3.7 %collective-permute-done.got_ref = f32[4,216,512]{2,1,0:T(8,128)S(1)} collective-permute-done((f32[4,216,512]{2,1,0:T(8,128)S(1)}, f32[4,216,512]{2,1,0:T(8,128)S(1)}, u32[]{:S(2)}, u32[]{:S(2)}) %collective-permute-start) | collective-permute-done | bytes 1769504 | tf_op jit(solution)/shard_map/ppermute | solution.py:323
  100.5 2.5 %collective-permute-start.1 = (bf16[224,512]{1,0:T(8,128)(2,1)S(1)}, bf16[224,512]{1,0:T(8,128)(2,1)S(1)}, u32[]{:S(2)}, u32[]{:S(2)}) collective-permute-start(bf16[224,512]{1,0:T(8,128)(2,1)S(1)} %get-tuple-element.29), channel_id=1, source_target_pairs={{0,2},{1,3},{2,4},{3,5},{4,6},{5,7},{6,0},{7,1},{8,10},{9,11},{10,... | collective-permute-start | bytes 688136 | tf_op jit(solution)/shard_map/ppermute | solution.py:324
  103.0 3.5 %collective-permute-start.2 = (bf16[224,512]{1,0:T(8,128)(2,1)S(1)}, bf16[224,512]{1,0:T(8,128)(2,1)S(1)}, u32[]{:S(2)}, u32[]{:S(2)}) collective-permute-start(bf16[224,512]{1,0:T(8,128)(2,1)S(1)} %get-tuple-element.30), channel_id=1, source_target_pairs={{0,6},{1,7},{2,0},{3,1},{4,2},{5,3},{6,4},{7,5},{8,14},{9,15},{10,... | collective-permute-start | bytes 688136 | tf_op jit(solution)/shard_map/ppermute | solution.py:324
  106.5 3.3 %collective-permute-start.3 = (bf16[224,512]{1,0:T(8,128)(2,1)S(1)}, bf16[224,512]{1,0:T(8,128)(2,1)S(1)}, u32[]{:S(2)}, u32[]{:S(2)}) collective-permute-start(bf16[224,512]{1,0:T(8,128)(2,1)S(1)} %get-tuple-element.31), channel_id=1, source_target_pairs={{0,4},{1,5},{2,6},{3,7},{4,0},{5,1},{6,2},{7,3},{8,12},{9,13},{10,... | collective-permute-start | bytes 688136 | tf_op jit(solution)/shard_map/ppermute | solution.py:324
  109.8 2.5 %near.1.refs_4_.near_ref = f32[256,512]{1,0:T(8,128)S(1)} custom-call(s32[2,1024]{1,0:T(2,128)S(1)} %pad_add_fusion.1.lines_ref, s32[1024,3]{1,0:T(8,128)S(1)} %copy.20.cols_ref, bf16[512,512]{1,0:T(8,128)(2,1)S(1)} %bitcast.32, bf16[1024,512]{1,0:T(8,128)(2,1)S(1)} %get-tuple-element.23.bfirst_ref, bf16[1536,512]{1,0:T(8,128)(2,1)S(1)} %copy-done.1), custom_call_target="tpu_custom_call" | custom-call | tf_op jit(solution)/shard_map/near/pallas_call | solution.py:326
  112.3 6.1 %collective-permute-done.2.refs_2_ = bf16[224,512]{1,0:T(8,128)(2,1)S(1)} collective-permute-done((bf16[224,512]{1,0:T(8,128)(2,1)S(1)}, bf16[224,512]{1,0:T(8,128)(2,1)S(1)}, u32[]{:S(2)}, u32[]{:S(2)}) %collective-permute-start.2) | collective-permute-done | bytes 229408 | tf_op jit(solution)/shard_map/ppermute | solution.py:324
  118.4 1.0 total.1
  119.4 1.3 all-to-all-done.3
  120.8 13.8 %all-to-all-start.2 = ((bf16[64,8,256]{2,1,0:T(8,128)(2,1)}), bf16[64,8,256]{2,1,0:T(8,128)(2,1)S(1)}, u32[]{:S(2)}, u32[]{:S(2)}) async-start(bf16[64,8,256]{2,1,0:T(8,128)(2,1)} %bitcast.10), calls=%async_computation.2 | async-start | bytes 524288 | tf_op jit(solution)/shard_map/all_to_all | solution.py:347
  134.9 1.9 %collective-permute-start.4 = (f32[4,32,512]{2,1,0:T(8,128)S(1)}, f32[4,32,512]{2,1,0:T(8,128)S(1)}, u32[]{:S(2)}, u32[]{:S(2)}) collective-permute-start(f32[4,32,512]{2,1,0:T(8,128)S(1)} %get-tuple-element.38), channel_id=1, source_target_pairs={{0,1},{1,0},{2,3},{3,2},{4,5},{5,4},{6,7},{7,6},{8,9},{9,8},{10,11... | collective-permute-start | bytes 786440 | tf_op jit(solution)/shard_map/ppermute | solution.py:376
  136.9 1.5 collective-permute-done.4
  138.4 2.2 %collective-permute-start.5 = (f32[32,512]{1,0:T(8,128)S(1)}, f32[32,512]{1,0:T(8,128)S(1)}, u32[]{:S(2)}, u32[]{:S(2)}) collective-permute-start(f32[32,512]{1,0:T(8,128)S(1)} %get-tuple-element.39), channel_id=1, source_target_pairs={{0,2},{1,3},{2,4},{3,5},{4,6},{5,7},{6,0},{7,1},{8,10},{9,11},{10,... | collective-permute-start | bytes 196616 | tf_op jit(solution)/shard_map/ppermute | solution.py:379
  140.6 3.5 %collective-permute-start.7 = (f32[32,512]{1,0:T(8,128)S(1)}, f32[32,512]{1,0:T(8,128)S(1)}, u32[]{:S(2)}, u32[]{:S(2)}) collective-permute-start(f32[32,512]{1,0:T(8,128)S(1)} %get-tuple-element.40), channel_id=1, source_target_pairs={{0,4},{1,5},{2,6},{3,7},{4,0},{5,1},{6,2},{7,3},{8,12},{9,13},{10,... | collective-permute-start | bytes 196616 | tf_op jit(solution)/shard_map/ppermute | solution.py:379
  144.1 3.3 %collective-permute-start.6 = (f32[32,512]{1,0:T(8,128)S(1)}, f32[32,512]{1,0:T(8,128)S(1)}, u32[]{:S(2)}, u32[]{:S(2)}) collective-permute-start(f32[32,512]{1,0:T(8,128)S(1)} %get-tuple-element.41), channel_id=1, source_target_pairs={{0,6},{1,7},{2,0},{3,1},{4,2},{5,3},{6,4},{7,5},{8,14},{9,15},{10,... | collective-permute-start | bytes 196616 | tf_op jit(solution)/shard_map/ppermute | solution.py:379
  147.4 0.8 collective-permute-done.7
  148.3 3.2 %collective-permute-done.6 = f32[32,512]{1,0:T(8,128)S(1)} collective-permute-done((f32[32,512]{1,0:T(8,128)S(1)}, f32[32,512]{1,0:T(8,128)S(1)}, u32[]{:S(2)}, u32[]{:S(2)}) %collective-permute-start.6) | collective-permute-done | bytes 65568 | tf_op jit(solution)/shard_map/ppermute | solution.py:379
  152.1 2.4 %all-to-all-done.2.got_ref = bf16[64,8,256]{2,1,0:T(8,128)(2,1)S(1)} async-done(((bf16[64,8,256]{2,1,0:T(8,128)(2,1)}), bf16[64,8,256]{2,1,0:T(8,128)(2,1)S(1)}, u32[]{:S(2)}, u32[]{:S(2)}) %all-to-all-start.2) | async-done | bytes 262176 | tf_op jit(solution)/shard_map/all_to_all | solution.py:347
  154.5 0.8 final.1
  (31 shorter events, 2.1 us)
Async XLA Ops:
  0.6 42.5 %copy-start.9 = (s32[1024]{0:T(1024)S(1)}, s32[1024]{0:T(1024)}, u32[]{:S(2)}) copy-start(s32[1024]{0:T(1024)} %param.13) | copy-start | bytes 12292
  0.6 42.5 %copy-start.6 = (s32[1024]{0:T(1024)S(1)}, s32[1024]{0:T(1024)}, u32[]{:S(2)}) copy-start(s32[1024]{0:T(1024)} %param.15) | copy-start | bytes 12292
  0.7 42.5 %copy-start.10 = (s32[1024]{0:T(1024)S(1)}, s32[1024]{0:T(1024)}, u32[]{:S(2)}) copy-start(s32[1024]{0:T(1024)} %param.16) | copy-start | bytes 12292
  0.7 72.5 %copy-start.8 = (bf16[128]{0:T(256)(128)(2,1)S(1)}, bf16[128]{0:T(256)(128)(2,1)}, u32[]{:S(2)}) copy-start(bf16[128]{0:T(256)(128)(2,1)} %param.12) | copy-start | bytes 772
  0.7 72.5 %copy-start.7 = (bf16[512,128]{1,0:T(8,128)(2,1)S(1)}, bf16[512,128]{1,0:T(8,128)(2,1)}, u32[]{:S(2)}) copy-start(bf16[512,128]{1,0:T(8,128)(2,1)} %ws_ref.1) | copy-start | bytes 393220
  35.8 1.0 copy-start.4
  36.7 36.4 %copy-start.5 = (bf16[256,512]{1,0:T(8,128)(2,1)S(1)}, bf16[256,512]{1,0:T(8,128)(2,1)}, u32[]{:S(2)}) copy-start(bf16[256,512]{1,0:T(8,128)(2,1)} %node_ref.5) | copy-start | bytes 786436
  37.9 35.3 %all-to-all-start.1 = ((bf16[64,8,512]{2,1,0:T(8,128)(2,1)}), bf16[64,8,512]{2,1,0:T(8,128)(2,1)S(1)}, u32[]{:S(2)}, u32[]{:S(2)}) async-start(bf16[64,8,512]{2,1,0:T(8,128)(2,1)} %bitcast.4), calls=%async_computation.1 | async-start | bytes 1048576 | tf_op jit(solution)/shard_map/all_to_all | solution.py:253
  73.2 1.4 copy-start
  82.7 1.0 copy-start.2
  83.8 37.0 %all-to-all-start.3 = ((bf16[64,8,512]{2,1,0:T(8,128)(2,1)}), bf16[64,8,512]{2,1,0:T(8,128)(2,1)S(1)}, u32[]{:S(2)}, u32[]{:S(2)}) async-start(bf16[64,8,512]{2,1,0:T(8,128)(2,1)} %bitcast.14), calls=%async_computation.3 | async-start | bytes 1048576 | tf_op jit(solution)/shard_map/all_to_all | solution.py:299
  90.5 1.2 copy-start.3
  94.7 5.6 %collective-permute-start = (f32[4,216,512]{2,1,0:T(8,128)S(1)}, f32[4,216,512]{2,1,0:T(8,128)S(1)}, u32[]{:S(2)}, u32[]{:S(2)}) collective-permute-start(f32[4,216,512]{2,1,0:T(8,128)S(1)} %get-tuple-element.27), channel_id=1, source_target_pairs={{0,1},{1,0},{2,3},{3,2},{4,5},{5,4},{6,7},{7,6},{8,9},{9,8},{10,11... | collective-permute-start | bytes 5308424 | tf_op jit(solution)/shard_map/ppermute | solution.py:323
  100.3 9.5 %copy-start.1 = (bf16[1536,512]{1,0:T(8,128)(2,1)S(1)}, bf16[1536,512]{1,0:T(8,128)(2,1)}, u32[]{:S(2)}) copy-start(bf16[1536,512]{1,0:T(8,128)(2,1)} %wf_ref.3) | copy-start | bytes 4718596
  100.5 11.8 %collective-permute-start.1 = (bf16[224,512]{1,0:T(8,128)(2,1)S(1)}, bf16[224,512]{1,0:T(8,128)(2,1)S(1)}, u32[]{:S(2)}, u32[]{:S(2)}) collective-permute-start(bf16[224,512]{1,0:T(8,128)(2,1)S(1)} %get-tuple-element.29), channel_id=1, source_target_pairs={{0,2},{1,3},{2,4},{3,5},{4,6},{5,7},{6,0},{7,1},{8,10},{9,11},{10,... | collective-permute-start | bytes 688136 | tf_op jit(solution)/shard_map/ppermute | solution.py:324
  103.0 15.4 %collective-permute-start.2 = (bf16[224,512]{1,0:T(8,128)(2,1)S(1)}, bf16[224,512]{1,0:T(8,128)(2,1)S(1)}, u32[]{:S(2)}, u32[]{:S(2)}) collective-permute-start(bf16[224,512]{1,0:T(8,128)(2,1)S(1)} %get-tuple-element.30), channel_id=1, source_target_pairs={{0,6},{1,7},{2,0},{3,1},{4,2},{5,3},{6,4},{7,5},{8,14},{9,15},{10,... | collective-permute-start | bytes 688136 | tf_op jit(solution)/shard_map/ppermute | solution.py:324
  106.5 11.9 %collective-permute-start.3 = (bf16[224,512]{1,0:T(8,128)(2,1)S(1)}, bf16[224,512]{1,0:T(8,128)(2,1)S(1)}, u32[]{:S(2)}, u32[]{:S(2)}) collective-permute-start(bf16[224,512]{1,0:T(8,128)(2,1)S(1)} %get-tuple-element.31), channel_id=1, source_target_pairs={{0,4},{1,5},{2,6},{3,7},{4,0},{5,1},{6,2},{7,3},{8,12},{9,13},{10,... | collective-permute-start | bytes 688136 | tf_op jit(solution)/shard_map/ppermute | solution.py:324
  120.8 33.7 %all-to-all-start.2 = ((bf16[64,8,256]{2,1,0:T(8,128)(2,1)}), bf16[64,8,256]{2,1,0:T(8,128)(2,1)S(1)}, u32[]{:S(2)}, u32[]{:S(2)}) async-start(bf16[64,8,256]{2,1,0:T(8,128)(2,1)} %bitcast.10), calls=%async_computation.2 | async-start | bytes 524288 | tf_op jit(solution)/shard_map/all_to_all | solution.py:347
  134.9 3.4 %collective-permute-start.4 = (f32[4,32,512]{2,1,0:T(8,128)S(1)}, f32[4,32,512]{2,1,0:T(8,128)S(1)}, u32[]{:S(2)}, u32[]{:S(2)}) collective-permute-start(f32[4,32,512]{2,1,0:T(8,128)S(1)} %get-tuple-element.38), channel_id=1, source_target_pairs={{0,1},{1,0},{2,3},{3,2},{4,5},{5,4},{6,7},{7,6},{8,9},{9,8},{10,11... | collective-permute-start | bytes 786440 | tf_op jit(solution)/shard_map/ppermute | solution.py:376
  138.4 9.0 %collective-permute-start.5 = (f32[32,512]{1,0:T(8,128)S(1)}, f32[32,512]{1,0:T(8,128)S(1)}, u32[]{:S(2)}, u32[]{:S(2)}) collective-permute-start(f32[32,512]{1,0:T(8,128)S(1)} %get-tuple-element.39), channel_id=1, source_target_pairs={{0,2},{1,3},{2,4},{3,5},{4,6},{5,7},{6,0},{7,1},{8,10},{9,11},{10,... | collective-permute-start | bytes 196616 | tf_op jit(solution)/shard_map/ppermute | solution.py:379
  140.6 7.7 %collective-permute-start.7 = (f32[32,512]{1,0:T(8,128)S(1)}, f32[32,512]{1,0:T(8,128)S(1)}, u32[]{:S(2)}, u32[]{:S(2)}) collective-permute-start(f32[32,512]{1,0:T(8,128)S(1)} %get-tuple-element.40), channel_id=1, source_target_pairs={{0,4},{1,5},{2,6},{3,7},{4,0},{5,1},{6,2},{7,3},{8,12},{9,13},{10,... | collective-permute-start | bytes 196616 | tf_op jit(solution)/shard_map/ppermute | solution.py:379
  144.1 7.4 %collective-permute-start.6 = (f32[32,512]{1,0:T(8,128)S(1)}, f32[32,512]{1,0:T(8,128)S(1)}, u32[]{:S(2)}, u32[]{:S(2)}) collective-permute-start(f32[32,512]{1,0:T(8,128)S(1)} %get-tuple-element.41), channel_id=1, source_target_pairs={{0,6},{1,7},{2,0},{3,1},{4,2},{5,3},{6,4},{7,5},{8,14},{9,15},{10,... | collective-permute-start | bytes 196616 | tf_op jit(solution)/shard_map/ppermute | solution.py:379

commit v4 on v3

--- a/solution.py
+++ b/solution.py
@@ -13,8 +13,11 @@
 I32 = jnp.int32
 MIB = 1 << 20
 TILE = 512
+LAST = 0
 WHOLE = pl.BlockSpec(memory_space=pltpu.VMEM)
 FREE = pl.CostEstimate(flops=0, bytes_accessed=0, transcendentals=0)
+ANYWHERE = pl.BlockSpec(memory_space=pl.ANY)
+FAR = pl.BlockSpec(memory_space=pltpu.HBM)
 SCALARS = pl.BlockSpec(memory_space=pltpu.SMEM)
 
 
@@ -29,6 +32,10 @@
     return high, (values - high.astype(F32)).astype(BF)
 
 
+def ring_mask(j):
+    return (0, 3, 1, 2)[j]
+
+
 def onehot(index, shape, axis):
     return jnp.where(index == lax.broadcasted_iota(I32, shape, axis), 1.0, 0.0).astype(BF)
 
@@ -41,15 +48,26 @@
     return pl.CostEstimate(flops=flops, bytes_accessed=nbytes, transcendentals=0)
 
 
-def answer_kernel(asked_ref, node_ref, out_ref):
-    own_count, slots = node_ref.shape[0], asked_ref.shape[1]
-    pick = onehot(asked_ref[...], (own_count, slots), 0)
+def answer_kernel(asked_ref, node_any, out_ref, line_out, node_ref, sem):
+    fetch = pltpu.make_async_copy(node_any, node_ref, sem)
+    fetch.start()
+    parts, cap = asked_ref.shape
+    own_count, slots = node_ref.shape[0], line_out.shape[1]
+    spread = lax.broadcasted_iota(I32, (parts, slots), 0)
+    spread = spread == lax.broadcasted_iota(I32, (parts, slots), 1) // cap
+    lines = dot(asked_ref[...].astype(F32).astype(BF), jnp.where(spread, 1.0, 0.0).astype(BF), 0, 0)
+    mine = lax.broadcasted_iota(I32, (cap, slots), 0)
+    mine = mine == lax.broadcasted_iota(I32, (cap, slots), 1) % cap
+    line = jnp.sum(jnp.where(mine, lines, 0.0), axis=0, keepdims=True).astype(I32)
+    line_out[...] = line
+    pick = onehot(line, (own_count, slots), 0)
+    fetch.wait()
     out_ref[...] = dot(pick, node_ref[...], 0, 0).astype(BF)
 
 
 def pair_kernel(
-    scale, live_ref, cols_ref, slots_ref, node_ref, rep_ref, wf_ref, ws_ref, wt_ref,
-    slot_out, first_out, bfirst_out, bsecond_out, extra_out, acc,
+    scale, live_ref, cols_ref, slots_ref, node_ref, rep_ref, wf_any, ws_ref, wt_ref,
+    slot_out, first_out, bfirst_out, bsecond_out, extra_out, acc, wf_ref, sem,
 ):
     step = pl.program_id(0)
     tile = cols_ref.shape[0]
@@ -57,8 +75,20 @@
     slots = rep_ref.shape[0]
     hidden2 = ws_ref.shape[1]
 
+    fetch = [
+        pltpu.make_async_copy(wf_any.at[pl.ds(i * width, width)], wf_ref.at[pl.ds(i * width, width)], sem.at[i])
+        for i in range(3)
+    ]
+
+    def arrive(i):
+        @pl.when(step == 0)
+        def _():
+            fetch[i].wait()
+
     @pl.when(step == 0)
     def _():
+        for copy in fetch:
+            copy.start()
         acc[...] = jnp.zeros_like(acc)
         extra_out[...] = jnp.zeros_like(extra_out)
 
@@ -67,11 +97,12 @@
     target = cols_ref[:, 2:3].astype(F32)
     product = (near * far).astype(BF)
     near_b = near.astype(BF)
-    pre_first = (
-        dot(near_b, wf_ref[:width])
-        + dot(far.astype(BF), wf_ref[width : 2 * width])
-        + dot(product, wf_ref[2 * width :])
-    )
+    arrive(0)
+    pre_first = dot(near_b, wf_ref[:width])
+    arrive(1)
+    pre_first = pre_first + dot(far.astype(BF), wf_ref[width : 2 * width])
+    arrive(2)
+    pre_first = pre_first + dot(product, wf_ref[2 * width :])
     sig = jax.nn.sigmoid(pre_first)
     first = (pre_first * sig).astype(BF)
     slope_first = sig * (1.0 + pre_first * (1.0 - sig))
@@ -105,31 +136,49 @@
 
 
 def weight_kernel(
-    scale, n_edge, edge_ref, lines_ref, node_ref, rep_ref, first_ref, bfirst_ref, bsecond_ref, extra_ref,
-    kept_out, sent_out, grads, grads2,
+    scale, n_edge, edge_ref, lines_ref, node_any, rep_any, first_any, bfirst_any, bsecond_any, extra_ref,
+    kept_out, sent_out, grads, grads2, node_ref, rep_ref, first_ref, bfirst_ref, bsecond_ref, sems,
 ):
+    pairs = (
+        (node_any, node_ref), (rep_any, rep_ref), (bfirst_any, bfirst_ref), (bsecond_any, bsecond_ref),
+        (first_any, first_ref),
+    )
+    fetch = [pltpu.make_async_copy(src, dst, sems.at[i]) for i, (src, dst) in enumerate(pairs)]
+    for copy in fetch:
+        copy.start()
     own_count, width = node_ref.shape
     slots = rep_ref.shape[0]
     edges = lines_ref.shape[1]
-    chips = n_edge // 2
     rows1 = 3 * width // n_edge
     rows2 = grads2.shape[0] // n_edge
+    rows = rows1 + rows2
+    fetch[0].wait()
+    near = dot(node_ref[...], onehot(lines_ref[0:1, :], (own_count, edges), 0), 0, 0)
+    fetch[1].wait()
+    far = dot(rep_ref[...], onehot(lines_ref[1:2, :], (slots, edges), 0), 0, 0)
+    fetch[2].wait()
     bfirst = bfirst_ref[...]
-    near = dot(node_ref[...], onehot(lines_ref[0:1, :], (own_count, edges), 0), 0, 0)
     grads[:width] = scale * dot(near.astype(BF), bfirst)
-    far = dot(rep_ref[...], onehot(lines_ref[1:2, :], (slots, edges), 0), 0, 0)
     grads[width : 2 * width] = scale * dot(far.astype(BF), bfirst)
     grads[2 * width :] = scale * dot((near * far).astype(BF), bfirst)
+    fetch[3].wait()
+    fetch[4].wait()
     grads2[...] = scale * dot(bsecond_ref[...], first_ref[...], 0, 0)
     edge = edge_ref[0]
     chip = edge // 2
     core = edge % 2
+    chips = n_edge // 2
+    extra = extra_ref[...]
+    extra_high, extra_low = halves(extra)
     for j in range(chips):
-        there = 2 * ((chip + j) % chips)
-        for out, owner in ((kept_out, there + core), (sent_out, there + 1 - core)):
-            out[j, :rows1] = grads[pl.ds(pl.multiple_of(owner * rows1, 8), rows1), :]
-            out[j, rows1 : rows1 + rows2] = grads2[pl.ds(pl.multiple_of(owner * rows2, 8), rows2), :]
-            out[j, rows1 + rows2 :] = extra_ref[...]
+        owner = 2 * ((chip + j) % chips) + core
+        kept_out[j, :rows1] = grads[pl.ds(pl.multiple_of(owner * rows1, 8), rows1), :]
+        kept_out[j, rows1:rows] = grads2[pl.ds(pl.multiple_of(owner * rows2, 8), rows2), :]
+        kept_out[j, rows:] = extra
+        owner = 2 * ((chip + j) % chips) + 1 - core
+        sent_out[j, :rows1] = grads[pl.ds(pl.multiple_of(owner * rows1, 8), rows1), :].astype(BF)
+        sent_out[j, rows1:rows] = grads2[pl.ds(pl.multiple_of(owner * rows2, 8), rows2), :].astype(BF)
+        sent_out[j, rows:] = jnp.concatenate([extra_high, extra_low], axis=0)
 
 
 def near_kernel(lines_ref, cols_ref, rep_ref, bfirst_ref, wf_ref, out_ref):
@@ -144,25 +193,38 @@
     out_ref[...] = dot(place, high) + dot(place, low)
 
 
-def owned_kernel(n_edge, edge_ref, asked_ref, near_ref, back_ref, kept_out, sent_out, total):
+def owned_kernel(n_edge, edge_ref, asked_ref, near_ref, back_ref, packed_ref, kept_out, sent_out, packed_out, total):
     own_count = near_ref.shape[0]
-    chips = n_edge // 2
     rows = own_count // n_edge
     place = onehot(asked_ref[...], (own_count, asked_ref.shape[1]), 0)
     total[...] = near_ref[...] + dot(place, back_ref[...])
     edge = edge_ref[0]
-    chip = edge // 2
-    core = edge % 2
-    for j in range(chips):
-        there = 2 * ((chip + j) % chips)
-        for out, owner in ((kept_out, there + core), (sent_out, there + 1 - core)):
-            out[j] = total[pl.ds(pl.multiple_of(owner * rows, 8), rows), :]
+    for j in range(n_edge // 2):
+        mask = ring_mask(j)
+        owner = edge ^ (2 * mask)
+        for out, who in ((kept_out, owner), (sent_out, owner ^ 1)):
+            out[j] = total[pl.ds(pl.multiple_of(who * rows, 8), rows), :]
+
+
+def add_kernel(kept_ref, got_ref, kept_out, sent_out):
+    half = kept_out.shape[0]
+    kept_out[...] = kept_ref[:half] + got_ref[:half].astype(F32)
+    sent_out[...] = (kept_ref[half:] + got_ref[half:].astype(F32)).astype(BF)
+
+
+def last_kernel(kept_ref, got_ref, out_ref):
+    out_ref[...] = kept_ref[0] + got_ref[0].astype(F32)
+
+
+def widen(packed, rows):
+    values = packed.astype(F32)
+    return jnp.concatenate([values[:rows], values[rows : rows + 8] + values[rows + 8 :]], axis=0)
 
 
 def chip_kernel(rows, kept_ref, got_ref, own_out, *packs):
-    own_out[...] = kept_ref[0] + got_ref[0]
+    own_out[...] = kept_ref[0] + widen(got_ref[0], rows)
     for j, out in enumerate(packs):
-        high, low = halves(kept_ref[j + 1] + got_ref[j + 1])
+        high, low = halves(kept_ref[j + 1] + widen(got_ref[j + 1], rows))
         out[: rows + 8] = high
         out[rows + 8 :] = low[rows:]
 
@@ -174,8 +236,7 @@
     lanes = out_ref.shape[1]
     total = own_ref[...]
     for ref in gots:
-        got = ref[...].astype(F32)
-        total = total + jnp.concatenate([got[:rows], got[rows : rows + 8] + got[rows + 8 :]], axis=0)
+        total = total + widen(ref[...], rows)
     hidden = total.shape[1]
     turned = jnp.concatenate([total[:rows], jnp.zeros((lanes - rows, hidden), F32)], axis=0).T
     third = total[rows : rows + 1, :n_second]
@@ -233,7 +294,7 @@
     def ahead(step):
         return [(i, (i + 2 * step) % n_edge) for i in range(n_edge)]
 
-    steps = (1, chips - 1) + tuple(range(2, chips - 1))
+    steps = tuple(range(2, chips - 1)) + (1, chips - 1)
     rows1 = 3 * width // n_edge
     rows2 = hidden2 // n_edge
     rows = rows1 + rows2
@@ -241,15 +302,18 @@
     lines = jnp.stack([src_row, slot_index], axis=0)
 
     asked_here = lax.all_to_all(requests, "dom", split_axis=0, concat_axis=0, tiled=True)
-    asked_line = asked_here.reshape(1, slots)
-    answer = pl.pallas_call(
+    answer, asked_line = pl.pallas_call(
         answer_kernel,
-        out_shape=jax.ShapeDtypeStruct((slots, width), BF),
-        in_specs=[WHOLE, WHOLE],
-        out_specs=WHOLE,
+        out_shape=(
+            jax.ShapeDtypeStruct((slots, width), BF),
+            jax.ShapeDtypeStruct((1, slots), I32),
+        ),
+        in_specs=[WHOLE, FAR],
+        out_specs=(WHOLE, WHOLE),
+        scratch_shapes=[pltpu.VMEM((own_count, width), BF), pltpu.SemaphoreType.DMA],
         compiler_params=params(8),
         name="answer",
-    )(asked_line, node_rows)
+    )(asked_here, node_rows)
     replies = lax.all_to_all(
         answer.reshape(parts, cap, width), "dom", split_axis=0, concat_axis=0, tiled=True
     ).reshape(slots, width)
@@ -264,10 +328,10 @@
         functools.partial(pair_kernel, scale),
         grid=(edges // TILE,),
         out_shape=(
-            jax.ShapeDtypeStruct((slots, width), BF),
-            jax.ShapeDtypeStruct((edges, hidden), BF),
-            jax.ShapeDtypeStruct((edges, hidden), BF),
-            jax.ShapeDtypeStruct((edges, hidden2), BF),
+            pltpu.HBM((slots, width), BF),
+            pltpu.HBM((edges, hidden), BF),
+            pltpu.HBM((edges, hidden), BF),
+            pltpu.HBM((edges, hidden2), BF),
             jax.ShapeDtypeStruct((8, hidden), F32),
         ),
         in_specs=[
@@ -276,7 +340,7 @@
             pl.BlockSpec((1, TILE), lambda i: (0, i)),
             fixed((own_count, width)),
             fixed((slots, width)),
-            fixed((3 * width, hidden)),
+            FAR,
             fixed((hidden, hidden2)),
             fixed((1, hidden2)),
         ],
@@ -287,7 +351,11 @@
             tiles(hidden2),
             pl.BlockSpec((8, hidden), lambda i: (0, 0)),
         ),
-        scratch_shapes=[pltpu.VMEM((slots, width), F32)],
+        scratch_shapes=[
+            pltpu.VMEM((slots, width), F32),
+            pltpu.VMEM((3 * width, hidden), BF),
+            pltpu.SemaphoreType.DMA((3,)),
+        ],
         compiler_params=params(32),
         cost_estimate=cost(6 * 10**9, 8 * MIB),
         name="pair",
@@ -300,17 +368,38 @@
         slot_grad.reshape(parts, cap, width), "dom", split_axis=0, concat_axis=0, tiled=True
     ).reshape(slots, width)
 
-    block = jax.ShapeDtypeStruct((chips, rows + 8, hidden), F32)
     kept, sent = pl.pallas_call(
         functools.partial(weight_kernel, scale, n_edge),
-        out_shape=(block, block),
-        in_specs=[SCALARS] + [WHOLE] * 7,
+        out_shape=(
+            jax.ShapeDtypeStruct((chips, rows + 8, hidden), F32),
+            jax.ShapeDtypeStruct((chips, rows + 16, hidden), BF),
+        ),
+        in_specs=[SCALARS, WHOLE] + [FAR] * 5 + [WHOLE],
         out_specs=(WHOLE, WHOLE),
-        scratch_shapes=[pltpu.VMEM((3 * width, hidden), F32), pltpu.VMEM((hidden2, hidden), F32)],
+        scratch_shapes=[
+            pltpu.VMEM((3 * width, hidden), F32),
+            pltpu.VMEM((hidden2, hidden), F32),
+            pltpu.VMEM((own_count, width), BF),
+            pltpu.VMEM((slots, width), BF),
+            pltpu.VMEM((edges, hidden), BF),
+            pltpu.VMEM((edges, hidden), BF),
+            pltpu.VMEM((edges, hidden2), BF),
+            pltpu.SemaphoreType.DMA((5,)),
+        ],
         compiler_params=params(32),
         cost_estimate=FREE,
         name="weights",
     )(edge, lines, node_rows, replies, first, back_first, back_second, extra)
+    near_part = pl.pallas_call(
+        near_kernel,
+        out_shape=jax.ShapeDtypeStruct((own_count, width), F32),
+        in_specs=[WHOLE] * 5,
+        out_specs=WHOLE,
+        compiler_params=params(32),
+        cost_estimate=FREE,
+        name="near",
+    )(lines, cols, replies, back_first, w_first)
+
     pack = jax.ShapeDtypeStruct((rows + 16, hidden), BF)
     own, *packs = pl.pallas_call(
         functools.partial(chip_kernel, rows),
@@ -323,27 +412,29 @@
     )(kept, lax.ppermute(sent, "edge", sibling))
     gots = [lax.ppermute(packs[step - 1], "edge", ahead(step)) for step in steps]
 
-    near_part = pl.pallas_call(
-        near_kernel,
-        out_shape=jax.ShapeDtypeStruct((own_count, width), F32),
-        in_specs=[WHOLE] * 5,
-        out_specs=WHOLE,
-        compiler_params=params(32),
-        cost_estimate=FREE,
-        name="near",
-    )(lines, cols, replies, back_first, w_first)
-
     share = hidden // parts
     lanes = -(-(rows + 2 * (hidden2 // share) + 2) // 128) * 128
     packed = pl.pallas_call(
         functools.partial(total_kernel, parts, hidden2),
         out_shape=jax.ShapeDtypeStruct((hidden, lanes), BF),
-        in_specs=[WHOLE] * chips + [pl.BlockSpec(memory_space=pl.ANY)],
+        in_specs=[WHOLE] * chips + [ANYWHERE],
         out_specs=WHOLE,
         compiler_params=params(16),
         cost_estimate=FREE,
         name="total",
     )(own, *gots, near_part)
+    block = jax.ShapeDtypeStruct((chips, own_count // n_edge, width), F32)
+    kept, sent, packed = pl.pallas_call(
+        functools.partial(owned_kernel, n_edge),
+        out_shape=(block, block, jax.ShapeDtypeStruct(packed.shape, BF)),
+        in_specs=[SCALARS] + [WHOLE] * 3 + [ANYWHERE],
+        out_specs=(WHOLE, WHOLE, ANYWHERE),
+        input_output_aliases={4: 2},
+        scratch_shapes=[pltpu.VMEM((own_count, width), F32)],
+        compiler_params=params(8),
+        cost_estimate=FREE,
+        name="owned",
+    )(edge, asked_line, near_part, returned, packed)
     got = lax.all_to_all(
         packed.reshape(parts, share, lanes), "dom", split_axis=0, concat_axis=0, tiled=True
     )
@@ -362,21 +453,30 @@
         name="final",
     )(got)
 
-    block = jax.ShapeDtypeStruct((chips, own_count // n_edge, width), F32)
-    kept, sent = pl.pallas_call(
-        functools.partial(owned_kernel, n_edge),
-        out_shape=(block, block),
-        in_specs=[SCALARS] + [WHOLE] * 3,
-        out_specs=(WHOLE, WHOLE),
-        scratch_shapes=[pltpu.VMEM((own_count, width), F32)],
+    for mask in (0, 1, 3):
+        partner = sibling if mask == 0 else [(i, i ^ (2 * mask)) for i in range(n_edge)]
+        got = lax.ppermute(sent, "edge", partner)
+        if mask == 3:
+            break
+        half = (kept.shape[0] // 2,) + kept.shape[1:]
+        kept, sent = pl.pallas_call(
+            add_kernel,
+            out_shape=(jax.ShapeDtypeStruct(half, F32), jax.ShapeDtypeStruct(half, BF)),
+            in_specs=[WHOLE] * 2,
+            out_specs=(WHOLE,) * 2,
+            compiler_params=params(8),
+            cost_estimate=FREE,
+            name="add",
+        )(kept, got)
+    node_share = pl.pallas_call(
+        last_kernel,
+        out_shape=jax.ShapeDtypeStruct(kept.shape[1:], F32),
+        in_specs=[WHOLE] * 2,
+        out_specs=WHOLE,
         compiler_params=params(8),
-        cost_estimate=FREE,
-        name="owned",
-    )(edge, asked_line, near_part, returned)
-    node_chip = kept + lax.ppermute(sent, "edge", sibling)
-    node_share = node_chip[0]
-    for step in steps:
-        node_share = node_share + lax.ppermute(node_chip[step], "edge", ahead(step))
+        cost_estimate=cost(LAST, 0),
+        name="last",
+    )(kept, got)
     return (
         first_t.T, second_share, third_total.reshape(hidden2), loss_total.reshape(()), node_share
     )

time: 157 us -> 155 us (0.987)
  starting transfers between devices: 47.3 us -> 42.9 us
  Pallas kernels: 17.1 us -> 20 us
  waiting for transfers between devices: 48.7 us -> 51.4 us
  local copies, waits for them, and re-layouts: 6.25 us -> 4.26 us
    ppermute x4 -> x3, waiting for transfers between devices: 5.54 us -> 10.8 us  [body(): got = lax.ppermute(sent, 'edge', partner)]
    ppermute x4 -> x3, starting transfers between devices: 10.9 us -> 5.76 us  [body(): got = lax.ppermute(sent, 'edge', partner)]
  transfers between devices with their start and end apart: 11 -> 10, of which waited for: 8 -> 9; matrix products, arithmetic and copies ran while one was open for 1% -> 1% of each run, Pallas kernels for 4% -> 5%
where the time goes in v4:
time: 155 us; the launch traced here: 154 us
  waiting for transfers between devices  51.4 us (33%)
  starting transfers between devices  42.9 us (28%)
  blocking collectives  32.9 us (21%)
  Pallas kernels  20 us (13%)
  local copies, waits for them, and re-layouts  4.26 us (3%)
    all_to_all x1, blocking collectives, body(): lax.all_to_all(requests, 'dom', split_axis=0, concat_axis=0, tiled=True)  32.9 us
    all_to_all x1, waiting for transfers between devices, body(): lax.all_to_all(answer.reshape(parts, cap, width), 'dom', split_axis=0, co...  29 us
    all_to_all x1, starting transfers between devices, body(): lax.all_to_all(packed.reshape(parts, share, lanes), 'dom', split_axis=0,...  14.1 us
    ppermute x3, waiting for transfers between devices, body(): got = lax.ppermute(sent, 'edge', partner)  10.8 us
    ppermute x3, starting transfers between devices, body(): lax.ppermute(packs[step - 1], 'edge', ahead(step))  9.41 us
    pallas_call x1, Pallas kernels, body(): pl.pallas_call(functools.partial(pair_kernel, scale), grid=(edges // TILE...  9.35 us
    all_to_all x1, starting transfers between devices, body(): lax.all_to_all(slot_grad.reshape(parts, cap, width), 'dom', split_axis=0,...  6.9 us
    ppermute x3, starting transfers between devices, body(): got = lax.ppermute(sent, 'edge', partner)  5.76 us
  transfers between devices with their start and end apart: 10, of which 9 were waited for; matrix products, arithmetic and copies ran while one was open for 1% of the time, Pallas kernels for 5%

profile of v4, /device:TPU:6, one launch (start us, length us, event | category | flops | bytes accessed | tf_op | source)
XLA Modules:
  0.0 153.8 jit_solution(10081893029848800006)
XLA Ops:
  0.6 0.9 copy.20
  1.5 32.9 %all_to_all.26 = s32[64,1,8]{2,1,0:T(1,128)S(1)} all-to-all(s32[64,1,8]{2,1,0:T(1,128)S(1)} %bitcast.27), channel_id=1, replica_groups=mesh['dom'=64,'edge'=8] {'dom'}, dimensions={0} | all-to-all | bytes 4096 | tf_op jit(solution)/shard_map/all_to_all | solution.py:304
  34.5 0.9 copy-done.4
  35.4 1.4 answer.1
  36.9 4.6 %all-to-all-start.1 = ((bf16[64,8,512]{2,1,0:T(8,128)(2,1)}), bf16[64,8,512]{2,1,0:T(8,128)(2,1)S(1)}, u32[]{:S(2)}, u32[]{:S(2)}) async-start(bf16[64,8,512]{2,1,0:T(8,128)(2,1)} %bitcast.8), calls=%async_computation.1 | async-start | bytes 1048576 | tf_op jit(solution)/shard_map/all_to_all | solution.py:317
  42.1 0.7 pad_add_fusion
  43.1 29.0 %all-to-all-done.1 = bf16[64,8,512]{2,1,0:T(8,128)(2,1)S(1)} async-done(((bf16[64,8,512]{2,1,0:T(8,128)(2,1)}), bf16[64,8,512]{2,1,0:T(8,128)(2,1)S(1)}, u32[]{:S(2)}, u32[]{:S(2)}) %all-to-all-start.1) | async-done | bytes 524320 | tf_op jit(solution)/shard_map/all_to_all | solution.py:317
  72.2 9.3 %pair.1 = (bf16[512,512]{1,0:T(8,128)(2,1)}, bf16[1024,512]{1,0:T(8,128)(2,1)}, bf16[1024,512]{1,0:T(8,128)(2,1)}, bf16[1024,128]{1,0:T(8,128)(2,1)}, f32[8,512]{1,0:T(8,128)S(1)}) custom-call(s32[1]{0:T(128)S(6)} %copy.24.live_ref, s32[1024,3]{1,0:T(8,128)S(1)} %copy.22.cols_ref, s32[1,1024]{1,0:T(1,128)S(1)} %bitcast.23, bf16[256,512]{1,0:T(8,128)(2,1)S(1)} %copy-done.5, ...), custom_call_target="tpu_custom_call" | custom-call | flops 6000000000 | bytes 8388608 | tf_op jit(solution)/shard_map/pair/pallas_call | solution.py:327
  81.6 6.9 %all-to-all-start.2 = ((bf16[64,8,512]{2,1,0:T(8,128)(2,1)}), bf16[64,8,512]{2,1,0:T(8,128)(2,1)S(1)}, u32[]{:S(2)}, u32[]{:S(2)}) async-start(bf16[64,8,512]{2,1,0:T(8,128)(2,1)} %bitcast.26), calls=%async_computation.2 | async-start | bytes 1048576 | tf_op jit(solution)/shard_map/all_to_all | solution.py:367
  88.5 1.2 copy-done.3
  89.7 0.9 copy-done.6
  90.7 3.8 %weights.1 = (f32[4,216,512]{2,1,0:T(8,128)S(1)}, bf16[4,224,512]{2,1,0:T(8,128)(2,1)S(1)}) custom-call(s32[1]{0:T(128)} %bitcast.edge_ref, s32[2,1024]{1,0:T(2,128)S(1)} %pad_add_fusion.1.lines_ref, bf16[256,512]{1,0:T(8,128)(2,1)S(1)} %copy-done.5, bf16[512,512]{1,0:T(8,128)(2,1)S(1)} %bitcast.18, bf16[1024,512]{1,0:T(8,128)(2,1)S(1)} %copy-done.3, ...), custom_call_target="tpu_custom_call" | custom-call | tf_op jit(solution)/shard_map/weights/pallas_call | solution.py:371
  94.5 2.1 %collective-permute-start = (bf16[4,224,512]{2,1,0:T(8,128)(2,1)S(1)}, bf16[4,224,512]{2,1,0:T(8,128)(2,1)S(1)}, u32[]{:S(2)}, u32[]{:S(2)}) collective-permute-start(bf16[4,224,512]{2,1,0:T(8,128)(2,1)S(1)} %get-tuple-element.37), channel_id=1, source_target_pairs={{0,1},{1,0},{2,3},{3,2},{4,5},{5,4},{6,7},{7,6},{8,9},{9,8},{10,11... | collective-permute-start | bytes 2752520 | tf_op jit(solution)/shard_map/ppermute | solution.py:412
  96.5 2.4 %collective-permute-done.got_ref = bf16[4,224,512]{2,1,0:T(8,128)(2,1)S(1)} collective-permute-done((bf16[4,224,512]{2,1,0:T(8,128)(2,1)S(1)}, bf16[4,224,512]{2,1,0:T(8,128)(2,1)S(1)}, u32[]{:S(2)}, u32[]{:S(2)}) %collective-permute-start) | collective-permute-done | bytes 917536 | tf_op jit(solution)/shard_map/ppermute | solution.py:412
  99.2 3.3 %collective-permute-start.1 = (bf16[224,512]{1,0:T(8,128)(2,1)S(1)}, bf16[224,512]{1,0:T(8,128)(2,1)S(1)}, u32[]{:S(2)}, u32[]{:S(2)}) collective-permute-start(bf16[224,512]{1,0:T(8,128)(2,1)S(1)} %get-tuple-element.39), channel_id=1, source_target_pairs={{0,4},{1,5},{2,6},{3,7},{4,0},{5,1},{6,2},{7,3},{8,12},{9,13},{10,... | collective-permute-start | bytes 688136 | tf_op jit(solution)/shard_map/ppermute | solution.py:413
  102.5 4.0 %collective-permute-start.2 = (bf16[224,512]{1,0:T(8,128)(2,1)S(1)}, bf16[224,512]{1,0:T(8,128)(2,1)S(1)}, u32[]{:S(2)}, u32[]{:S(2)}) collective-permute-start(bf16[224,512]{1,0:T(8,128)(2,1)S(1)} %get-tuple-element.40), channel_id=1, source_target_pairs={{0,2},{1,3},{2,4},{3,5},{4,6},{5,7},{6,0},{7,1},{8,10},{9,11},{10,... | collective-permute-start | bytes 688136 | tf_op jit(solution)/shard_map/ppermute | solution.py:413
  106.5 2.1 %collective-permute-start.3 = (bf16[224,512]{1,0:T(8,128)(2,1)S(1)}, bf16[224,512]{1,0:T(8,128)(2,1)S(1)}, u32[]{:S(2)}, u32[]{:S(2)}) collective-permute-start(bf16[224,512]{1,0:T(8,128)(2,1)S(1)} %get-tuple-element.41), channel_id=1, source_target_pairs={{0,6},{1,7},{2,0},{3,1},{4,2},{5,3},{6,4},{7,5},{8,14},{9,15},{10,... | collective-permute-start | bytes 688136 | tf_op jit(solution)/shard_map/ppermute | solution.py:413
  108.6 2.5 %near.1.refs_4_.near_ref = f32[256,512]{1,0:T(8,128)S(1)} custom-call(s32[2,1024]{1,0:T(2,128)S(1)} %pad_add_fusion.1.lines_ref, s32[1024,3]{1,0:T(8,128)S(1)} %copy.22.cols_ref, bf16[512,512]{1,0:T(8,128)(2,1)S(1)} %bitcast.19, bf16[1024,512]{1,0:T(8,128)(2,1)S(1)} %copy-done, bf16[1536,512]{1,0:T(8,128)(2,1)S(1)} %copy-done.2), custom_call_target="tpu_custom_call" | custom-call | tf_op jit(solution)/shard_map/near/pallas_call | solution.py:393
  111.1 1.8 %collective-permute-done.2.refs_2_ = bf16[224,512]{1,0:T(8,128)(2,1)S(1)} collective-permute-done((bf16[224,512]{1,0:T(8,128)(2,1)S(1)}, bf16[224,512]{1,0:T(8,128)(2,1)S(1)}, u32[]{:S(2)}, u32[]{:S(2)}) %collective-permute-start.2) | collective-permute-done | bytes 229408 | tf_op jit(solution)/shard_map/ppermute | solution.py:413
  112.9 3.8 %collective-permute-done.3.refs_3_ = bf16[224,512]{1,0:T(8,128)(2,1)S(1)} collective-permute-done((bf16[224,512]{1,0:T(8,128)(2,1)S(1)}, bf16[224,512]{1,0:T(8,128)(2,1)S(1)}, u32[]{:S(2)}, u32[]{:S(2)}) %collective-permute-start.3) | collective-permute-done | bytes 229408 | tf_op jit(solution)/shard_map/ppermute | solution.py:413
  116.7 1.0 total.1.packed_ref
  117.7 1.0 all-to-all-done.2
  119.1 14.1 %all-to-all-start.3 = ((bf16[64,8,256]{2,1,0:T(8,128)(2,1)}), bf16[64,8,256]{2,1,0:T(8,128)(2,1)S(1)}, u32[]{:S(2)}, u32[]{:S(2)}) async-start(bf16[64,8,256]{2,1,0:T(8,128)(2,1)} %bitcast.13), calls=%async_computation.3 | async-start | bytes 524288 | tf_op jit(solution)/shard_map/all_to_all | solution.py:438
  133.2 1.9 %collective-permute-start.4 = (f32[4,32,512]{2,1,0:T(8,128)S(1)}, f32[4,32,512]{2,1,0:T(8,128)S(1)}, u32[]{:S(2)}, u32[]{:S(2)}) collective-permute-start(f32[4,32,512]{2,1,0:T(8,128)S(1)} %get-tuple-element.48), channel_id=1, source_target_pairs={{0,1},{1,0},{2,3},{3,2},{4,5},{5,4},{6,7},{7,6},{8,9},{9,8},{10,11... | collective-permute-start | bytes 786440 | tf_op jit(solution)/shard_map/ppermute | solution.py:458
  135.1 1.5 collective-permute-done.4.got_ref
  136.7 1.9 %collective-permute-start.5 = (bf16[2,32,512]{2,1,0:T(8,128)(2,1)S(1)}, bf16[2,32,512]{2,1,0:T(8,128)(2,1)S(1)}, u32[]{:S(2)}, u32[]{:S(2)}) collective-permute-start(bf16[2,32,512]{2,1,0:T(8,128)(2,1)S(1)} %get-tuple-element.50), channel_id=1, source_target_pairs={{0,2},{1,3},{2,0},{3,1},{4,6},{5,7},{6,4},{7,5},{8,10},{9,11},{10,... | collective-permute-start | bytes 196616 | tf_op jit(solution)/shard_map/ppermute | solution.py:458
  138.6 4.2 %collective-permute-done.5.got_ref = bf16[2,32,512]{2,1,0:T(8,128)(2,1)S(1)} collective-permute-done((bf16[2,32,512]{2,1,0:T(8,128)(2,1)S(1)}, bf16[2,32,512]{2,1,0:T(8,128)(2,1)S(1)}, u32[]{:S(2)}, u32[]{:S(2)}) %collective-permute-start.5) | collective-permute-done | bytes 65568 | tf_op jit(solution)/shard_map/ppermute | solution.py:458
  142.8 1.9 %collective-permute-start.6 = (bf16[1,32,512]{2,1,0:T(8,128)(2,1)S(1)}, bf16[1,32,512]{2,1,0:T(8,128)(2,1)S(1)}, u32[]{:S(2)}, u32[]{:S(2)}) collective-permute-start(bf16[1,32,512]{2,1,0:T(8,128)(2,1)S(1)} %get-tuple-element.52), channel_id=1, source_target_pairs={{0,6},{1,7},{2,4},{3,5},{4,2},{5,3},{6,0},{7,1},{8,14},{9,15},{10,... | collective-permute-start | bytes 98312 | tf_op jit(solution)/shard_map/ppermute | solution.py:458
  144.8 5.1 %collective-permute-done.6.got_ref = bf16[1,32,512]{2,1,0:T(8,128)(2,1)S(1)} collective-permute-done((bf16[1,32,512]{2,1,0:T(8,128)(2,1)S(1)}, bf16[1,32,512]{2,1,0:T(8,128)(2,1)S(1)}, u32[]{:S(2)}, u32[]{:S(2)}) %collective-permute-start.6) | collective-permute-done | bytes 32800 | tf_op jit(solution)/shard_map/ppermute | solution.py:458
  149.8 0.6 last.1
  150.5 2.5 %all-to-all-done.3.got_ref = bf16[64,8,256]{2,1,0:T(8,128)(2,1)S(1)} async-done(((bf16[64,8,256]{2,1,0:T(8,128)(2,1)}), bf16[64,8,256]{2,1,0:T(8,128)(2,1)S(1)}, u32[]{:S(2)}, u32[]{:S(2)}) %all-to-all-start.3) | async-done | bytes 262176 | tf_op jit(solution)/shard_map/all_to_all | solution.py:438
  153.0 0.8 final.1
  (26 shorter events, 0.8 us)
Async XLA Ops:
  0.6 71.5 %copy-start.1 = (bf16[1536,512]{1,0:T(8,128)(2,1)S(1)}, bf16[1536,512]{1,0:T(8,128)(2,1)}, u32[]{:S(2)}) copy-start(bf16[1536,512]{1,0:T(8,128)(2,1)} %wf_ref.1) | copy-start | bytes 4718596
  34.5 1.0 copy-start.4
  35.4 36.7 %copy-start.5 = (bf16[256,512]{1,0:T(8,128)(2,1)S(1)}, bf16[256,512]{1,0:T(8,128)(2,1)}, u32[]{:S(2)}) copy-start(bf16[256,512]{1,0:T(8,128)(2,1)} %node_any.3) | copy-start | bytes 786436
  35.4 36.7 %copy-start.7 = (s32[1024]{0:T(1024)S(1)}, s32[1024]{0:T(1024)}, u32[]{:S(2)}) copy-start(s32[1024]{0:T(1024)} %param.15) | copy-start | bytes 12292
  35.4 36.7 %copy-start.8 = (bf16[512,128]{1,0:T(8,128)(2,1)S(1)}, bf16[512,128]{1,0:T(8,128)(2,1)}, u32[]{:S(2)}) copy-start(bf16[512,128]{1,0:T(8,128)(2,1)} %ws_ref.1) | copy-start | bytes 393220
  35.4 36.7 %copy-start.9 = (bf16[128]{0:T(256)(128)(2,1)S(1)}, bf16[128]{0:T(256)(128)(2,1)}, u32[]{:S(2)}) copy-start(bf16[128]{0:T(256)(128)(2,1)} %param.12) | copy-start | bytes 772
  36.9 35.3 %all-to-all-start.1 = ((bf16[64,8,512]{2,1,0:T(8,128)(2,1)}), bf16[64,8,512]{2,1,0:T(8,128)(2,1)S(1)}, u32[]{:S(2)}, u32[]{:S(2)}) async-start(bf16[64,8,512]{2,1,0:T(8,128)(2,1)} %bitcast.8), calls=%async_computation.1 | async-start | bytes 1048576 | tf_op jit(solution)/shard_map/all_to_all | solution.py:317
  72.2 16.3 %copy-start.10 = (s32[1024]{0:T(1024)S(1)}, s32[1024]{0:T(1024)}, u32[]{:S(2)}) copy-start(s32[1024]{0:T(1024)} %param.13) | copy-start | bytes 12292
  81.5 7.0 %copy-start = (bf16[1024,512]{1,0:T(8,128)(2,1)S(1)}, bf16[1024,512]{1,0:T(8,128)(2,1)}, u32[]{:S(2)}) copy-start(bf16[1024,512]{1,0:T(8,128)(2,1)} %get-tuple-element.31.bfirst_ref.bfirst_any) | copy-start | bytes 3145732
  81.6 37.2 %all-to-all-start.2 = ((bf16[64,8,512]{2,1,0:T(8,128)(2,1)}), bf16[64,8,512]{2,1,0:T(8,128)(2,1)S(1)}, u32[]{:S(2)}, u32[]{:S(2)}) async-start(bf16[64,8,512]{2,1,0:T(8,128)(2,1)} %bitcast.26), calls=%async_computation.2 | async-start | bytes 1048576 | tf_op jit(solution)/shard_map/all_to_all | solution.py:367
  88.5 1.2 copy-start.3
  89.7 0.9 copy-start.6
  94.5 14.1 %copy-start.2 = (bf16[1536,512]{1,0:T(8,128)(2,1)S(1)}, bf16[1536,512]{1,0:T(8,128)(2,1)}, u32[]{:S(2)}) copy-start(bf16[1536,512]{1,0:T(8,128)(2,1)} %wf_ref.1) | copy-start | bytes 4718596
  94.5 4.5 %collective-permute-start = (bf16[4,224,512]{2,1,0:T(8,128)(2,1)S(1)}, bf16[4,224,512]{2,1,0:T(8,128)(2,1)S(1)}, u32[]{:S(2)}, u32[]{:S(2)}) collective-permute-start(bf16[4,224,512]{2,1,0:T(8,128)(2,1)S(1)} %get-tuple-element.37), channel_id=1, source_target_pairs={{0,1},{1,0},{2,3},{3,2},{4,5},{5,4},{6,7},{7,6},{8,9},{9,8},{10,11... | collective-permute-start | bytes 2752520 | tf_op jit(solution)/shard_map/ppermute | solution.py:412
  99.2 11.9 %collective-permute-start.1 = (bf16[224,512]{1,0:T(8,128)(2,1)S(1)}, bf16[224,512]{1,0:T(8,128)(2,1)S(1)}, u32[]{:S(2)}, u32[]{:S(2)}) collective-permute-start(bf16[224,512]{1,0:T(8,128)(2,1)S(1)} %get-tuple-element.39), channel_id=1, source_target_pairs={{0,4},{1,5},{2,6},{3,7},{4,0},{5,1},{6,2},{7,3},{8,12},{9,13},{10,... | collective-permute-start | bytes 688136 | tf_op jit(solution)/shard_map/ppermute | solution.py:413
  102.5 10.4 %collective-permute-start.2 = (bf16[224,512]{1,0:T(8,128)(2,1)S(1)}, bf16[224,512]{1,0:T(8,128)(2,1)S(1)}, u32[]{:S(2)}, u32[]{:S(2)}) collective-permute-start(bf16[224,512]{1,0:T(8,128)(2,1)S(1)} %get-tuple-element.40), channel_id=1, source_target_pairs={{0,2},{1,3},{2,4},{3,5},{4,6},{5,7},{6,0},{7,1},{8,10},{9,11},{10,... | collective-permute-start | bytes 688136 | tf_op jit(solution)/shard_map/ppermute | solution.py:413
  106.5 10.2 %collective-permute-start.3 = (bf16[224,512]{1,0:T(8,128)(2,1)S(1)}, bf16[224,512]{1,0:T(8,128)(2,1)S(1)}, u32[]{:S(2)}, u32[]{:S(2)}) collective-permute-start(bf16[224,512]{1,0:T(8,128)(2,1)S(1)} %get-tuple-element.41), channel_id=1, source_target_pairs={{0,6},{1,7},{2,0},{3,1},{4,2},{5,3},{6,4},{7,5},{8,14},{9,15},{10,... | collective-permute-start | bytes 688136 | tf_op jit(solution)/shard_map/ppermute | solution.py:413
  119.1 34.0 %all-to-all-start.3 = ((bf16[64,8,256]{2,1,0:T(8,128)(2,1)}), bf16[64,8,256]{2,1,0:T(8,128)(2,1)S(1)}, u32[]{:S(2)}, u32[]{:S(2)}) async-start(bf16[64,8,256]{2,1,0:T(8,128)(2,1)} %bitcast.13), calls=%async_computation.3 | async-start | bytes 524288 | tf_op jit(solution)/shard_map/all_to_all | solution.py:438
  133.2 3.4 %collective-permute-start.4 = (f32[4,32,512]{2,1,0:T(8,128)S(1)}, f32[4,32,512]{2,1,0:T(8,128)S(1)}, u32[]{:S(2)}, u32[]{:S(2)}) collective-permute-start(f32[4,32,512]{2,1,0:T(8,128)S(1)} %get-tuple-element.48), channel_id=1, source_target_pairs={{0,1},{1,0},{2,3},{3,2},{4,5},{5,4},{6,7},{7,6},{8,9},{9,8},{10,11... | collective-permute-start | bytes 786440 | tf_op jit(solution)/shard_map/ppermute | solution.py:458
  136.7 6.2 %collective-permute-start.5 = (bf16[2,32,512]{2,1,0:T(8,128)(2,1)S(1)}, bf16[2,32,512]{2,1,0:T(8,128)(2,1)S(1)}, u32[]{:S(2)}, u32[]{:S(2)}) collective-permute-start(bf16[2,32,512]{2,1,0:T(8,128)(2,1)S(1)} %get-tuple-element.50), channel_id=1, source_target_pairs={{0,2},{1,3},{2,0},{3,1},{4,6},{5,7},{6,4},{7,5},{8,10},{9,11},{10,... | collective-permute-start | bytes 196616 | tf_op jit(solution)/shard_map/ppermute | solution.py:458
  142.8 7.0 %collective-permute-start.6 = (bf16[1,32,512]{2,1,0:T(8,128)(2,1)S(1)}, bf16[1,32,512]{2,1,0:T(8,128)(2,1)S(1)}, u32[]{:S(2)}, u32[]{:S(2)}) collective-permute-start(bf16[1,32,512]{2,1,0:T(8,128)(2,1)S(1)} %get-tuple-element.52), channel_id=1, source_target_pairs={{0,6},{1,7},{2,4},{3,5},{4,2},{5,3},{6,0},{7,1},{8,14},{9,15},{10,... | collective-permute-start | bytes 98312 | tf_op jit(solution)/shard_map/ppermute | solution.py:458

commit v5 on v4

--- a/solution.py
+++ b/solution.py
@@ -42,6 +42,10 @@
 
 def params(mib):
     return pltpu.CompilerParams(vmem_limit_bytes=mib * MIB)
+
+
+def in_hbm(array):
+    return pltpu.with_memory_space_constraint(array, pltpu.HBM)
 
 
 def cost(flops, nbytes):
@@ -67,72 +71,78 @@
 
 def pair_kernel(
     scale, live_ref, cols_ref, slots_ref, node_ref, rep_ref, wf_any, ws_ref, wt_ref,
-    slot_out, first_out, bfirst_out, bsecond_out, extra_out, acc, wf_ref, sem,
+    slot_out, first_out, bfirst_out, bsecond_out, extra_out,
+    wf_ref, slot_ref, first_ref, bfirst_ref, bsecond_ref, fetch_sems, store_sems,
 ):
-    step = pl.program_id(0)
-    tile = cols_ref.shape[0]
+    edges = cols_ref.shape[0]
     own_count, width = node_ref.shape
     slots = rep_ref.shape[0]
     hidden2 = ws_ref.shape[1]
-
-    fetch = [
-        pltpu.make_async_copy(wf_any.at[pl.ds(i * width, width)], wf_ref.at[pl.ds(i * width, width)], sem.at[i])
-        for i in range(3)
-    ]
-
-    def arrive(i):
-        @pl.when(step == 0)
-        def _():
-            fetch[i].wait()
-
-    @pl.when(step == 0)
-    def _():
-        for copy in fetch:
-            copy.start()
-        acc[...] = jnp.zeros_like(acc)
-        extra_out[...] = jnp.zeros_like(extra_out)
-
-    near = dot(onehot(cols_ref[:, 0:1], (tile, own_count), 1), node_ref[...])
-    far = dot(onehot(cols_ref[:, 1:2], (tile, slots), 1), rep_ref[...])
-    target = cols_ref[:, 2:3].astype(F32)
-    product = (near * far).astype(BF)
-    near_b = near.astype(BF)
-    arrive(0)
-    pre_first = dot(near_b, wf_ref[:width])
-    arrive(1)
-    pre_first = pre_first + dot(far.astype(BF), wf_ref[width : 2 * width])
-    arrive(2)
-    pre_first = pre_first + dot(product, wf_ref[2 * width :])
-    sig = jax.nn.sigmoid(pre_first)
-    first = (pre_first * sig).astype(BF)
-    slope_first = sig * (1.0 + pre_first * (1.0 - sig))
-    first_out[...] = first
-    pre_second = dot(first, ws_ref[...])
-    sig = jax.nn.sigmoid(pre_second)
-    second = (pre_second * sig).astype(BF).astype(F32)
-    slope_second = sig * (1.0 + pre_second * (1.0 - sig))
+    fetch = []
+    for i in range(3):
+        part = pl.ds(i * width, width)
+        fetch.append(pltpu.make_async_copy(wf_any.at[part], wf_ref.at[part], fetch_sems.at[i]))
+        fetch[-1].start()
+    stores = []
+
+    def store(src, dst):
+        copy = pltpu.make_async_copy(src, dst, store_sems.at[len(stores)])
+        copy.start()
+        stores.append(copy)
+
     w_third = wt_ref[...].astype(F32)
-    logits = jnp.sum(second * w_third, axis=1, keepdims=True)
-    place = step * tile + lax.broadcasted_iota(I32, (tile, 1), 0)
-    live = jnp.where(place < live_ref[0], 1.0, 0.0)
-    slope = live * (jax.nn.sigmoid(logits) - target)
-    softplus = jnp.maximum(logits, 0.0) + jnp.log1p(jnp.exp(-jnp.abs(logits)))
-    loss = jnp.sum(live * (softplus - target * logits), axis=0, keepdims=True)
-    extra_out[0:1, :hidden2] += scale * jnp.sum(slope * second, axis=0, keepdims=True)
-    extra_out[1:2, :hidden2] += jnp.broadcast_to(scale * loss, (1, hidden2))
-    back_second = (slope * w_third * slope_second).astype(BF)
-    bsecond_out[...] = back_second
-    back_first = (dot(back_second, ws_ref[...], 1, 1) * slope_first).astype(BF)
-    bfirst_out[...] = back_first
-    block_b = dot(back_first, wf_ref[width : 2 * width], 1, 1)
-    block_c = dot(back_first, wf_ref[2 * width :], 1, 1)
-    high, low = halves(block_b + block_c * near)
-    place = onehot(slots_ref[...], (slots, tile), 0)
-    acc[...] += dot(place, high) + dot(place, low)
-
-    @pl.when(step == pl.num_programs(0) - 1)
-    def _():
-        slot_out[...] = acc[...].astype(BF)
+    total = None
+    third = None
+    loss = None
+    for tile in range(edges // TILE):
+        part = pl.ds(tile * TILE, TILE)
+        near = dot(onehot(cols_ref[part, 0:1], (TILE, own_count), 1), node_ref[...])
+        far = dot(onehot(cols_ref[part, 1:2], (TILE, slots), 1), rep_ref[...])
+        target = cols_ref[part, 2:3].astype(F32)
+        blocks = (near.astype(BF), far.astype(BF), (near * far).astype(BF))
+        pre_first = None
+        for i, block in enumerate(blocks):
+            if tile == 0:
+                fetch[i].wait()
+            term = dot(block, wf_ref[i * width : (i + 1) * width])
+            pre_first = term if pre_first is None else pre_first + term
+        sig = jax.nn.sigmoid(pre_first)
+        first = (pre_first * sig).astype(BF)
+        slope_first = sig * (1.0 + pre_first * (1.0 - sig))
+        first_ref[part] = first
+        store(first_ref.at[part], first_out.at[part])
+        pre_second = dot(first, ws_ref[...])
+        sig = jax.nn.sigmoid(pre_second)
+        second = (pre_second * sig).astype(BF).astype(F32)
+        slope_second = sig * (1.0 + pre_second * (1.0 - sig))
+        logits = jnp.sum(second * w_third, axis=1, keepdims=True)
+        place = tile * TILE + lax.broadcasted_iota(I32, (TILE, 1), 0)
+        live = jnp.where(place < live_ref[0], 1.0, 0.0)
+        slope = live * (jax.nn.sigmoid(logits) - target)
+        back_second = (slope * w_third * slope_second).astype(BF)
+        bsecond_ref[part] = back_second
+        store(bsecond_ref.at[part], bsecond_out.at[part])
+        back_first = (dot(back_second, ws_ref[...], 1, 1) * slope_first).astype(BF)
+        bfirst_ref[part] = back_first
+        store(bfirst_ref.at[part], bfirst_out.at[part])
+        block_b = dot(back_first, wf_ref[width : 2 * width], 1, 1)
+        block_c = dot(back_first, wf_ref[2 * width :], 1, 1)
+        high, low = halves(block_b + block_c * near)
+        place = onehot(slots_ref[:, part], (slots, TILE), 0)
+        term = dot(place, high) + dot(place, low)
+        total = term if total is None else total + term
+        softplus = jnp.maximum(logits, 0.0) + jnp.log1p(jnp.exp(-jnp.abs(logits)))
+        term = jnp.sum(live * (softplus - target * logits), axis=0, keepdims=True)
+        loss = term if loss is None else loss + term
+        term = jnp.sum(slope * second, axis=0, keepdims=True)
+        third = term if third is None else third + term
+    slot_ref[...] = total.astype(BF)
+    store(slot_ref, slot_out)
+    extra_out[...] = jnp.zeros_like(extra_out)
+    extra_out[0:1, :hidden2] = scale * third
+    extra_out[1:2, :hidden2] = jnp.broadcast_to(scale * loss, (1, hidden2))
+    for copy in stores:
+        copy.wait()
 
 
 def weight_kernel(
@@ -152,10 +162,12 @@
     rows1 = 3 * width // n_edge
     rows2 = grads2.shape[0] // n_edge
     rows = rows1 + rows2
+    near_pick = onehot(lines_ref[0:1, :], (own_count, edges), 0)
+    far_pick = onehot(lines_ref[1:2, :], (slots, edges), 0)
     fetch[0].wait()
-    near = dot(node_ref[...], onehot(lines_ref[0:1, :], (own_count, edges), 0), 0, 0)
+    near = dot(node_ref[...], near_pick, 0, 0)
     fetch[1].wait()
-    far = dot(rep_ref[...], onehot(lines_ref[1:2, :], (slots, edges), 0), 0, 0)
+    far = dot(rep_ref[...], far_pick, 0, 0)
     fetch[2].wait()
     bfirst = bfirst_ref[...]
     grads[:width] = scale * dot(near.astype(BF), bfirst)
@@ -313,54 +325,26 @@
         scratch_shapes=[pltpu.VMEM((own_count, width), BF), pltpu.SemaphoreType.DMA],
         compiler_params=params(8),
         name="answer",
-    )(asked_here, node_rows)
+    )(asked_here, in_hbm(node_rows))
     replies = lax.all_to_all(
         answer.reshape(parts, cap, width), "dom", split_axis=0, concat_axis=0, tiled=True
     ).reshape(slots, width)
 
-    def fixed(shape):
-        return pl.BlockSpec(shape, lambda i: (0,) * len(shape), pipeline_mode=pl.Buffered(1))
-
-    def tiles(count):
-        return pl.BlockSpec((TILE, count), lambda i: (i, 0))
-
+    outs = [(slots, width), (edges, hidden), (edges, hidden), (edges, hidden2)]
     slot_grad, first, back_first, back_second, extra = pl.pallas_call(
         functools.partial(pair_kernel, scale),
-        grid=(edges // TILE,),
-        out_shape=(
-            pltpu.HBM((slots, width), BF),
-            pltpu.HBM((edges, hidden), BF),
-            pltpu.HBM((edges, hidden), BF),
-            pltpu.HBM((edges, hidden2), BF),
-            jax.ShapeDtypeStruct((8, hidden), F32),
-        ),
-        in_specs=[
-            SCALARS,
-            tiles(3),
-            pl.BlockSpec((1, TILE), lambda i: (0, i)),
-            fixed((own_count, width)),
-            fixed((slots, width)),
-            FAR,
-            fixed((hidden, hidden2)),
-            fixed((1, hidden2)),
-        ],
-        out_specs=(
-            pl.BlockSpec((slots, width), lambda i: (0, 0)),
-            tiles(hidden),
-            tiles(hidden),
-            tiles(hidden2),
-            pl.BlockSpec((8, hidden), lambda i: (0, 0)),
-        ),
-        scratch_shapes=[
-            pltpu.VMEM((slots, width), F32),
-            pltpu.VMEM((3 * width, hidden), BF),
-            pltpu.SemaphoreType.DMA((3,)),
-        ],
+        out_shape=tuple(pltpu.HBM(shape, BF) for shape in outs)
+        + (jax.ShapeDtypeStruct((8, hidden), F32),),
+        in_specs=[SCALARS] + [WHOLE] * 4 + [FAR] + [WHOLE] * 2,
+        out_specs=(FAR,) * 4 + (WHOLE,),
+        scratch_shapes=[pltpu.VMEM((3 * width, hidden), BF)]
+        + [pltpu.VMEM(shape, BF) for shape in outs]
+        + [pltpu.SemaphoreType.DMA((3,)), pltpu.SemaphoreType.DMA((3 * edges // TILE + 1,))],
         compiler_params=params(32),
         cost_estimate=cost(6 * 10**9, 8 * MIB),
         name="pair",
     )(
-        live_count, cols, slot_index.reshape(1, edges), node_rows, replies, w_first, w_second,
+        live_count, cols, slot_index.reshape(1, edges), node_rows, replies, in_hbm(w_first), w_second,
         w_third.reshape(1, hidden2),
     )
 
@@ -389,7 +373,10 @@
         compiler_params=params(32),
         cost_estimate=FREE,
         name="weights",
-    )(edge, lines, node_rows, replies, first, back_first, back_second, extra)
+    )(
+        edge, lines, in_hbm(node_rows), in_hbm(replies), in_hbm(first), in_hbm(back_first),
+        in_hbm(back_second), extra,
+    )
     near_part = pl.pallas_call(
         near_kernel,
         out_shape=jax.ShapeDtypeStruct((own_count, width), F32),

time: 155 us -> 152 us (0.981)
  local copies, waits for them, and re-layouts: 4.26 us -> 1.08 us
    unnamed x23 -> x19, local copies, waits for them, and re-layouts: 4.04 us -> 0.86 us
  transfers between devices with their start and end apart: 10 -> 10, of which waited for: 9 -> 9; matrix products, arithmetic and copies ran while one was open for 1% -> 1% of each run, Pallas kernels for 5% -> 6%
where the time goes in v5:
time: 152 us; the launch traced here: 151 us
  waiting for transfers between devices  52.6 us (35%)
  starting transfers between devices  41.5 us (27%)
  blocking collectives  32.9 us (22%)
  Pallas kernels  21 us (14%)
  between operations  1.56 us (1%)
    all_to_all x1, blocking collectives, body(): lax.all_to_all(requests, 'dom', split_axis=0, concat_axis=0, tiled=True)  32.9 us
    all_to_all x1, waiting for transfers between devices, body(): lax.all_to_all(answer.reshape(parts, cap, width), 'dom', split_axis=0, co...  29 us
    all_to_all x1, starting transfers between devices, body(): lax.all_to_all(packed.reshape(parts, share, lanes), 'dom', split_axis=0,...  12.8 us
    ppermute x3, waiting for transfers between devices, body(): got = lax.ppermute(sent, 'edge', partner)  10.8 us
    ppermute x3, starting transfers between devices, body(): lax.ppermute(packs[step - 1], 'edge', ahead(step))  9.23 us
    pallas_call x1, Pallas kernels, body(): pl.pallas_call(functools.partial(pair_kernel, scale), out_shape=tuple((pl...  8.72 us
    all_to_all x1, starting transfers between devices, body(): lax.all_to_all(slot_grad.reshape(parts, cap, width), 'dom', split_axis=0,...  6.94 us
    ppermute x3, starting transfers between devices, body(): got = lax.ppermute(sent, 'edge', partner)  5.76 us
  transfers between devices with their start and end apart: 10, of which 9 were waited for; matrix products, arithmetic and copies ran while one was open for 1% of the time, Pallas kernels for 6%

profile of v5, /device:TPU:6, one launch (start us, length us, event | category | flops | bytes accessed | tf_op | source)
XLA Modules:
  0.0 151.5 jit_solution(14885132748198133344)
XLA Ops:
  0.7 0.8 copy.20
  1.5 32.9 %all_to_all.26 = s32[64,1,8]{2,1,0:T(1,128)S(1)} all-to-all(s32[64,1,8]{2,1,0:T(1,128)S(1)} %bitcast.27), channel_id=1, replica_groups=mesh['dom'=64,'edge'=8] {'dom'}, dimensions={0} | all-to-all | bytes 4096 | tf_op jit(solution)/shard_map/all_to_all | solution.py:316
  34.4 2.1 %answer.1 = (bf16[512,512]{1,0:T(8,128)(2,1)}, s32[1,512]{1,0:T(1,128)S(1)}) custom-call(s32[64,8]{1,0:T(8,128)S(1)} %bitcast.21, bf16[256,512]{1,0:T(8,128)(2,1)} %node_any.3), custom_call_target="tpu_custom_call" | custom-call | tf_op jit(solution)/shard_map/answer/pallas_call | solution.py:317
  36.5 4.6 %all-to-all-start.1 = ((bf16[64,8,512]{2,1,0:T(8,128)(2,1)}), bf16[64,8,512]{2,1,0:T(8,128)(2,1)S(1)}, u32[]{:S(2)}, u32[]{:S(2)}) async-start(bf16[64,8,512]{2,1,0:T(8,128)(2,1)} %bitcast.8), calls=%async_computation.1 | async-start | bytes 1048576 | tf_op jit(solution)/shard_map/all_to_all | solution.py:329
  41.8 0.7 pad_add_fusion
  42.6 0.2 copy.22.cols_ref
  42.8 29.0 %all-to-all-done.1 = bf16[64,8,512]{2,1,0:T(8,128)(2,1)S(1)} async-done(((bf16[64,8,512]{2,1,0:T(8,128)(2,1)}), bf16[64,8,512]{2,1,0:T(8,128)(2,1)S(1)}, u32[]{:S(2)}, u32[]{:S(2)}) %all-to-all-start.1) | async-done | bytes 524320 | tf_op jit(solution)/shard_map/all_to_all | solution.py:329
  71.9 8.7 %pair.1 = (bf16[512,512]{1,0:T(8,128)(2,1)}, bf16[1024,512]{1,0:T(8,128)(2,1)}, bf16[1024,512]{1,0:T(8,128)(2,1)}, bf16[1024,128]{1,0:T(8,128)(2,1)}, f32[8,512]{1,0:T(8,128)S(1)}) custom-call(s32[1]{0:T(128)S(6)} %copy.24.live_ref, s32[1024,3]{1,0:T(8,128)S(1)} %copy.22.cols_ref, s32[1,1024]{1,0:T(1,128)S(1)} %bitcast.23, bf16[256,512]{1,0:T(8,128)(2,1)S(1)} %copy-done.4, ...), custom_call_target="tpu_custom_call" | custom-call | flops 6000000000 | bytes 8388608 | tf_op jit(solution)/shard_map/pair/pallas_call | solution.py:334
  80.6 6.9 %all-to-all-start.2 = ((bf16[64,8,512]{2,1,0:T(8,128)(2,1)}), bf16[64,8,512]{2,1,0:T(8,128)(2,1)S(1)}, u32[]{:S(2)}, u32[]{:S(2)}) async-start(bf16[64,8,512]{2,1,0:T(8,128)(2,1)} %bitcast.26), calls=%async_computation.2 | async-start | bytes 1048576 | tf_op jit(solution)/shard_map/all_to_all | solution.py:351
  87.6 4.6 %weights.1 = (f32[4,216,512]{2,1,0:T(8,128)S(1)}, bf16[4,224,512]{2,1,0:T(8,128)(2,1)S(1)}) custom-call(s32[1]{0:T(128)} %bitcast.edge_ref, s32[2,1024]{1,0:T(2,128)S(1)} %pad_add_fusion.1.lines_ref, bf16[256,512]{1,0:T(8,128)(2,1)} %node_any.3, bf16[512,512]{1,0:T(8,128)(2,1)} %bitcast.18, bf16[1024,512]{1,0:T(8,128)(2,1)} %get-tuple-element.33.first_any, ...), custom_call_target="tpu_custom_call" | custom-call | tf_op jit(solution)/shard_map/weights/pallas_call | solution.py:355
  92.3 2.1 %collective-permute-start = (bf16[4,224,512]{2,1,0:T(8,128)(2,1)S(1)}, bf16[4,224,512]{2,1,0:T(8,128)(2,1)S(1)}, u32[]{:S(2)}, u32[]{:S(2)}) collective-permute-start(bf16[4,224,512]{2,1,0:T(8,128)(2,1)S(1)} %get-tuple-element.37), channel_id=1, source_target_pairs={{0,1},{1,0},{2,3},{3,2},{4,5},{5,4},{6,7},{7,6},{8,9},{9,8},{10,11... | collective-permute-start | bytes 2752520 | tf_op jit(solution)/shard_map/ppermute | solution.py:399
  94.3 2.4 %collective-permute-done.got_ref = bf16[4,224,512]{2,1,0:T(8,128)(2,1)S(1)} collective-permute-done((bf16[4,224,512]{2,1,0:T(8,128)(2,1)S(1)}, bf16[4,224,512]{2,1,0:T(8,128)(2,1)S(1)}, u32[]{:S(2)}, u32[]{:S(2)}) %collective-permute-start) | collective-permute-done | bytes 917536 | tf_op jit(solution)/shard_map/ppermute | solution.py:399
  96.8 0.2 chip.1
  97.0 3.3 %collective-permute-start.1 = (bf16[224,512]{1,0:T(8,128)(2,1)S(1)}, bf16[224,512]{1,0:T(8,128)(2,1)S(1)}, u32[]{:S(2)}, u32[]{:S(2)}) collective-permute-start(bf16[224,512]{1,0:T(8,128)(2,1)S(1)} %get-tuple-element.39), channel_id=1, source_target_pairs={{0,4},{1,5},{2,6},{3,7},{4,0},{5,1},{6,2},{7,3},{8,12},{9,13},{10,... | collective-permute-start | bytes 688136 | tf_op jit(solution)/shard_map/ppermute | solution.py:400
  100.3 4.0 %collective-permute-start.2 = (bf16[224,512]{1,0:T(8,128)(2,1)S(1)}, bf16[224,512]{1,0:T(8,128)(2,1)S(1)}, u32[]{:S(2)}, u32[]{:S(2)}) collective-permute-start(bf16[224,512]{1,0:T(8,128)(2,1)S(1)} %get-tuple-element.40), channel_id=1, source_target_pairs={{0,2},{1,3},{2,4},{3,5},{4,6},{5,7},{6,0},{7,1},{8,10},{9,11},{10,... | collective-permute-start | bytes 688136 | tf_op jit(solution)/shard_map/ppermute | solution.py:400
  104.3 1.9 %collective-permute-start.3 = (bf16[224,512]{1,0:T(8,128)(2,1)S(1)}, bf16[224,512]{1,0:T(8,128)(2,1)S(1)}, u32[]{:S(2)}, u32[]{:S(2)}) collective-permute-start(bf16[224,512]{1,0:T(8,128)(2,1)S(1)} %get-tuple-element.41), channel_id=1, source_target_pairs={{0,6},{1,7},{2,0},{3,1},{4,2},{5,3},{6,4},{7,5},{8,14},{9,15},{10,... | collective-permute-start | bytes 688136 | tf_op jit(solution)/shard_map/ppermute | solution.py:400
  106.3 2.5 %near.1.refs_4_.near_ref = f32[256,512]{1,0:T(8,128)S(1)} custom-call(s32[2,1024]{1,0:T(2,128)S(1)} %pad_add_fusion.1.lines_ref, s32[1024,3]{1,0:T(8,128)S(1)} %copy.22.cols_ref, bf16[512,512]{1,0:T(8,128)(2,1)S(1)} %bitcast.19, bf16[1024,512]{1,0:T(8,128)(2,1)S(1)} %copy-done.2, bf16[1536,512]{1,0:T(8,128)(2,1)S(1)} %copy-done.3), custom_call_target="tpu_custom_call" | custom-call | tf_op jit(solution)/shard_map/near/pallas_call | solution.py:380
  108.8 1.9 %collective-permute-done.2.refs_2_ = bf16[224,512]{1,0:T(8,128)(2,1)S(1)} collective-permute-done((bf16[224,512]{1,0:T(8,128)(2,1)S(1)}, bf16[224,512]{1,0:T(8,128)(2,1)S(1)}, u32[]{:S(2)}, u32[]{:S(2)}) %collective-permute-start.2) | collective-permute-done | bytes 229408 | tf_op jit(solution)/shard_map/ppermute | solution.py:400
  110.7 3.8 %collective-permute-done.3.refs_3_ = bf16[224,512]{1,0:T(8,128)(2,1)S(1)} collective-permute-done((bf16[224,512]{1,0:T(8,128)(2,1)S(1)}, bf16[224,512]{1,0:T(8,128)(2,1)S(1)}, u32[]{:S(2)}, u32[]{:S(2)}) %collective-permute-start.3) | collective-permute-done | bytes 229408 | tf_op jit(solution)/shard_map/ppermute | solution.py:400
  114.5 1.0 total.1.packed_ref
  115.5 2.1 %all-to-all-done.2 = bf16[64,8,512]{2,1,0:T(8,128)(2,1)S(1)} async-done(((bf16[64,8,512]{2,1,0:T(8,128)(2,1)}), bf16[64,8,512]{2,1,0:T(8,128)(2,1)S(1)}, u32[]{:S(2)}, u32[]{:S(2)}) %all-to-all-start.2) | async-done | bytes 524320 | tf_op jit(solution)/shard_map/all_to_all | solution.py:351
  117.7 0.3 owned.1
  118.0 12.8 %all-to-all-start.3 = ((bf16[64,8,256]{2,1,0:T(8,128)(2,1)}), bf16[64,8,256]{2,1,0:T(8,128)(2,1)S(1)}, u32[]{:S(2)}, u32[]{:S(2)}) async-start(bf16[64,8,256]{2,1,0:T(8,128)(2,1)} %bitcast.13), calls=%async_computation.3 | async-start | bytes 524288 | tf_op jit(solution)/shard_map/all_to_all | solution.py:425
  130.8 1.9 %collective-permute-start.4 = (f32[4,32,512]{2,1,0:T(8,128)S(1)}, f32[4,32,512]{2,1,0:T(8,128)S(1)}, u32[]{:S(2)}, u32[]{:S(2)}) collective-permute-start(f32[4,32,512]{2,1,0:T(8,128)S(1)} %get-tuple-element.48), channel_id=1, source_target_pairs={{0,1},{1,0},{2,3},{3,2},{4,5},{5,4},{6,7},{7,6},{8,9},{9,8},{10,11... | collective-permute-start | bytes 786440 | tf_op jit(solution)/shard_map/ppermute | solution.py:445
  132.8 1.5 collective-permute-done.4.got_ref
  134.3 1.9 %collective-permute-start.5 = (bf16[2,32,512]{2,1,0:T(8,128)(2,1)S(1)}, bf16[2,32,512]{2,1,0:T(8,128)(2,1)S(1)}, u32[]{:S(2)}, u32[]{:S(2)}) collective-permute-start(bf16[2,32,512]{2,1,0:T(8,128)(2,1)S(1)} %get-tuple-element.50), channel_id=1, source_target_pairs={{0,2},{1,3},{2,0},{3,1},{4,6},{5,7},{6,4},{7,5},{8,10},{9,11},{10,... | collective-permute-start | bytes 196616 | tf_op jit(solution)/shard_map/ppermute | solution.py:445
  136.2 4.2 %collective-permute-done.5.got_ref = bf16[2,32,512]{2,1,0:T(8,128)(2,1)S(1)} collective-permute-done((bf16[2,32,512]{2,1,0:T(8,128)(2,1)S(1)}, bf16[2,32,512]{2,1,0:T(8,128)(2,1)S(1)}, u32[]{:S(2)}, u32[]{:S(2)}) %collective-permute-start.5) | collective-permute-done | bytes 65568 | tf_op jit(solution)/shard_map/ppermute | solution.py:445
  140.5 1.9 %collective-permute-start.6 = (bf16[1,32,512]{2,1,0:T(8,128)(2,1)S(1)}, bf16[1,32,512]{2,1,0:T(8,128)(2,1)S(1)}, u32[]{:S(2)}, u32[]{:S(2)}) collective-permute-start(bf16[1,32,512]{2,1,0:T(8,128)(2,1)S(1)} %get-tuple-element.52), channel_id=1, source_target_pairs={{0,6},{1,7},{2,4},{3,5},{4,2},{5,3},{6,0},{7,1},{8,14},{9,15},{10,... | collective-permute-start | bytes 98312 | tf_op jit(solution)/shard_map/ppermute | solution.py:445
  142.4 5.1 %collective-permute-done.6.got_ref = bf16[1,32,512]{2,1,0:T(8,128)(2,1)S(1)} collective-permute-done((bf16[1,32,512]{2,1,0:T(8,128)(2,1)S(1)}, bf16[1,32,512]{2,1,0:T(8,128)(2,1)S(1)}, u32[]{:S(2)}, u32[]{:S(2)}) %collective-permute-start.6) | collective-permute-done | bytes 32800 | tf_op jit(solution)/shard_map/ppermute | solution.py:445
  147.5 0.6 last.1
  148.1 2.5 %all-to-all-done.3.got_ref = bf16[64,8,256]{2,1,0:T(8,128)(2,1)S(1)} async-done(((bf16[64,8,256]{2,1,0:T(8,128)(2,1)}), bf16[64,8,256]{2,1,0:T(8,128)(2,1)S(1)}, u32[]{:S(2)}, u32[]{:S(2)}) %all-to-all-start.3) | async-done | bytes 262176 | tf_op jit(solution)/shard_map/all_to_all | solution.py:425
  150.7 0.8 final.1
  (22 shorter events, 0.1 us)
Async XLA Ops:
  0.6 71.2 %copy-start.4 = (bf16[256,512]{1,0:T(8,128)(2,1)S(1)}, bf16[256,512]{1,0:T(8,128)(2,1)}, u32[]{:S(2)}) copy-start(bf16[256,512]{1,0:T(8,128)(2,1)} %node_any.3) | copy-start | bytes 786436
  0.6 71.2 %copy-start.5 = (s32[1024]{0:T(1024)S(1)}, s32[1024]{0:T(1024)}, u32[]{:S(2)}) copy-start(s32[1024]{0:T(1024)} %param.15) | copy-start | bytes 12292
  0.7 71.2 %copy-start.7 = (bf16[128]{0:T(256)(128)(2,1)S(1)}, bf16[128]{0:T(256)(128)(2,1)}, u32[]{:S(2)}) copy-start(bf16[128]{0:T(256)(128)(2,1)} %param.12) | copy-start | bytes 772
  0.7 71.2 %copy-start.6 = (bf16[512,128]{1,0:T(8,128)(2,1)S(1)}, bf16[512,128]{1,0:T(8,128)(2,1)}, u32[]{:S(2)}) copy-start(bf16[512,128]{1,0:T(8,128)(2,1)} %ws_ref.1) | copy-start | bytes 393220
  36.5 35.3 %all-to-all-start.1 = ((bf16[64,8,512]{2,1,0:T(8,128)(2,1)}), bf16[64,8,512]{2,1,0:T(8,128)(2,1)S(1)}, u32[]{:S(2)}, u32[]{:S(2)}) async-start(bf16[64,8,512]{2,1,0:T(8,128)(2,1)} %bitcast.8), calls=%async_computation.1 | async-start | bytes 1048576 | tf_op jit(solution)/shard_map/all_to_all | solution.py:329
  71.8 8.8 %copy-start = (bf16[64,8,512]{2,1,0:T(8,128)(2,1)}, bf16[64,8,512]{2,1,0:T(8,128)(2,1)S(1)}, u32[]{:S(2)}) copy-start(bf16[64,8,512]{2,1,0:T(8,128)(2,1)S(1)} %all-to-all-done.1) | copy-start | bytes 1572868
  71.8 15.7 %copy-start.8 = (s32[1024]{0:T(1024)S(1)}, s32[1024]{0:T(1024)}, u32[]{:S(2)}) copy-start(s32[1024]{0:T(1024)} %param.13) | copy-start | bytes 12292
  80.6 37.1 %all-to-all-start.2 = ((bf16[64,8,512]{2,1,0:T(8,128)(2,1)}), bf16[64,8,512]{2,1,0:T(8,128)(2,1)S(1)}, u32[]{:S(2)}, u32[]{:S(2)}) async-start(bf16[64,8,512]{2,1,0:T(8,128)(2,1)} %bitcast.26), calls=%async_computation.2 | async-start | bytes 1048576 | tf_op jit(solution)/shard_map/all_to_all | solution.py:351
  87.6 18.7 %copy-start.3 = (bf16[1536,512]{1,0:T(8,128)(2,1)S(1)}, bf16[1536,512]{1,0:T(8,128)(2,1)}, u32[]{:S(2)}) copy-start(bf16[1536,512]{1,0:T(8,128)(2,1)} %wf_ref.1) | copy-start | bytes 4718596
  92.2 14.0 %copy-start.1 = (bf16[64,8,512]{2,1,0:T(8,128)(2,1)S(1)}, bf16[64,8,512]{2,1,0:T(8,128)(2,1)}, u32[]{:S(2)}) copy-start(bf16[64,8,512]{2,1,0:T(8,128)(2,1)} %copy-done) | copy-start | bytes 1572868
  92.3 14.0 %copy-start.2 = (bf16[1024,512]{1,0:T(8,128)(2,1)S(1)}, bf16[1024,512]{1,0:T(8,128)(2,1)}, u32[]{:S(2)}) copy-start(bf16[1024,512]{1,0:T(8,128)(2,1)} %get-tuple-element.31.bfirst_ref.bfirst_any) | copy-start | bytes 3145732
  92.3 4.5 %collective-permute-start = (bf16[4,224,512]{2,1,0:T(8,128)(2,1)S(1)}, bf16[4,224,512]{2,1,0:T(8,128)(2,1)S(1)}, u32[]{:S(2)}, u32[]{:S(2)}) collective-permute-start(bf16[4,224,512]{2,1,0:T(8,128)(2,1)S(1)} %get-tuple-element.37), channel_id=1, source_target_pairs={{0,1},{1,0},{2,3},{3,2},{4,5},{5,4},{6,7},{7,6},{8,9},{9,8},{10,11... | collective-permute-start | bytes 2752520 | tf_op jit(solution)/shard_map/ppermute | solution.py:399
  97.0 11.8 %collective-permute-start.1 = (bf16[224,512]{1,0:T(8,128)(2,1)S(1)}, bf16[224,512]{1,0:T(8,128)(2,1)S(1)}, u32[]{:S(2)}, u32[]{:S(2)}) collective-permute-start(bf16[224,512]{1,0:T(8,128)(2,1)S(1)} %get-tuple-element.39), channel_id=1, source_target_pairs={{0,4},{1,5},{2,6},{3,7},{4,0},{5,1},{6,2},{7,3},{8,12},{9,13},{10,... | collective-permute-start | bytes 688136 | tf_op jit(solution)/shard_map/ppermute | solution.py:400
  100.3 10.4 %collective-permute-start.2 = (bf16[224,512]{1,0:T(8,128)(2,1)S(1)}, bf16[224,512]{1,0:T(8,128)(2,1)S(1)}, u32[]{:S(2)}, u32[]{:S(2)}) collective-permute-start(bf16[224,512]{1,0:T(8,128)(2,1)S(1)} %get-tuple-element.40), channel_id=1, source_target_pairs={{0,2},{1,3},{2,4},{3,5},{4,6},{5,7},{6,0},{7,1},{8,10},{9,11},{10,... | collective-permute-start | bytes 688136 | tf_op jit(solution)/shard_map/ppermute | solution.py:400
  104.3 10.2 %collective-permute-start.3 = (bf16[224,512]{1,0:T(8,128)(2,1)S(1)}, bf16[224,512]{1,0:T(8,128)(2,1)S(1)}, u32[]{:S(2)}, u32[]{:S(2)}) collective-permute-start(bf16[224,512]{1,0:T(8,128)(2,1)S(1)} %get-tuple-element.41), channel_id=1, source_target_pairs={{0,6},{1,7},{2,0},{3,1},{4,2},{5,3},{6,4},{7,5},{8,14},{9,15},{10,... | collective-permute-start | bytes 688136 | tf_op jit(solution)/shard_map/ppermute | solution.py:400
  118.0 32.7 %all-to-all-start.3 = ((bf16[64,8,256]{2,1,0:T(8,128)(2,1)}), bf16[64,8,256]{2,1,0:T(8,128)(2,1)S(1)}, u32[]{:S(2)}, u32[]{:S(2)}) async-start(bf16[64,8,256]{2,1,0:T(8,128)(2,1)} %bitcast.13), calls=%async_computation.3 | async-start | bytes 524288 | tf_op jit(solution)/shard_map/all_to_all | solution.py:425
  130.8 3.4 %collective-permute-start.4 = (f32[4,32,512]{2,1,0:T(8,128)S(1)}, f32[4,32,512]{2,1,0:T(8,128)S(1)}, u32[]{:S(2)}, u32[]{:S(2)}) collective-permute-start(f32[4,32,512]{2,1,0:T(8,128)S(1)} %get-tuple-element.48), channel_id=1, source_target_pairs={{0,1},{1,0},{2,3},{3,2},{4,5},{5,4},{6,7},{7,6},{8,9},{9,8},{10,11... | collective-permute-start | bytes 786440 | tf_op jit(solution)/shard_map/ppermute | solution.py:445
  134.3 6.2 %collective-permute-start.5 = (bf16[2,32,512]{2,1,0:T(8,128)(2,1)S(1)}, bf16[2,32,512]{2,1,0:T(8,128)(2,1)S(1)}, u32[]{:S(2)}, u32[]{:S(2)}) collective-permute-start(bf16[2,32,512]{2,1,0:T(8,128)(2,1)S(1)} %get-tuple-element.50), channel_id=1, source_target_pairs={{0,2},{1,3},{2,0},{3,1},{4,6},{5,7},{6,4},{7,5},{8,10},{9,11},{10,... | collective-permute-start | bytes 196616 | tf_op jit(solution)/shard_map/ppermute | solution.py:445
  140.5 7.0 %collective-permute-start.6 = (bf16[1,32,512]{2,1,0:T(8,128)(2,1)S(1)}, bf16[1,32,512]{2,1,0:T(8,128)(2,1)S(1)}, u32[]{:S(2)}, u32[]{:S(2)}) collective-permute-start(bf16[1,32,512]{2,1,0:T(8,128)(2,1)S(1)} %get-tuple-element.52), channel_id=1, source_target_pairs={{0,6},{1,7},{2,4},{3,5},{4,2},{5,3},{6,0},{7,1},{8,14},{9,15},{10,... | collective-permute-start | bytes 98312 | tf_op jit(solution)/shard_map/ppermute | solution.py:445

commit v6 on v5

--- a/solution.py
+++ b/solution.py
@@ -12,7 +12,7 @@
 F32 = jnp.float32
 I32 = jnp.int32
 MIB = 1 << 20
-TILE = 512
+TILE = 1024
 LAST = 0
 WHOLE = pl.BlockSpec(memory_space=pltpu.VMEM)
 FREE = pl.CostEstimate(flops=0, bytes_accessed=0, transcendentals=0)
@@ -70,9 +70,10 @@
 
 
 def pair_kernel(
-    scale, live_ref, cols_ref, slots_ref, node_ref, rep_ref, wf_any, ws_ref, wt_ref,
-    slot_out, first_out, bfirst_out, bsecond_out, extra_out,
-    wf_ref, slot_ref, first_ref, bfirst_ref, bsecond_ref, fetch_sems, store_sems,
+    scale, n_edge, live_ref, edge_ref, cols_ref, lines_ref, node_ref, rep_ref, wf_any, ws_ref, wt_ref,
+    slot_out, bfirst_out, kept_out, sent_out,
+    wf_ref, slot_ref, first_ref, bfirst_ref, bsecond_ref, grads, grads2, extra_ref, sent_ref,
+    feat_ref, fetch_sems, store_sems,
 ):
     edges = cols_ref.shape[0]
     own_count, width = node_ref.shape
@@ -91,7 +92,6 @@
         stores.append(copy)
 
     w_third = wt_ref[...].astype(F32)
-    total = None
     third = None
     loss = None
     for tile in range(edges // TILE):
@@ -102,6 +102,7 @@
         blocks = (near.astype(BF), far.astype(BF), (near * far).astype(BF))
         pre_first = None
         for i, block in enumerate(blocks):
+            feat_ref[i, part] = block
             if tile == 0:
                 fetch[i].wait()
             term = dot(block, wf_ref[i * width : (i + 1) * width])
@@ -110,7 +111,6 @@
         first = (pre_first * sig).astype(BF)
         slope_first = sig * (1.0 + pre_first * (1.0 - sig))
         first_ref[part] = first
-        store(first_ref.at[part], first_out.at[part])
         pre_second = dot(first, ws_ref[...])
         sig = jax.nn.sigmoid(pre_second)
         second = (pre_second * sig).astype(BF).astype(F32)
@@ -121,61 +121,25 @@
         slope = live * (jax.nn.sigmoid(logits) - target)
         back_second = (slope * w_third * slope_second).astype(BF)
         bsecond_ref[part] = back_second
-        store(bsecond_ref.at[part], bsecond_out.at[part])
         back_first = (dot(back_second, ws_ref[...], 1, 1) * slope_first).astype(BF)
         bfirst_ref[part] = back_first
         store(bfirst_ref.at[part], bfirst_out.at[part])
-        block_b = dot(back_first, wf_ref[width : 2 * width], 1, 1)
-        block_c = dot(back_first, wf_ref[2 * width :], 1, 1)
-        high, low = halves(block_b + block_c * near)
-        place = onehot(slots_ref[:, part], (slots, TILE), 0)
-        term = dot(place, high) + dot(place, low)
-        total = term if total is None else total + term
         softplus = jnp.maximum(logits, 0.0) + jnp.log1p(jnp.exp(-jnp.abs(logits)))
         term = jnp.sum(live * (softplus - target * logits), axis=0, keepdims=True)
         loss = term if loss is None else loss + term
         term = jnp.sum(slope * second, axis=0, keepdims=True)
         third = term if third is None else third + term
-    slot_ref[...] = total.astype(BF)
-    store(slot_ref, slot_out)
-    extra_out[...] = jnp.zeros_like(extra_out)
-    extra_out[0:1, :hidden2] = scale * third
-    extra_out[1:2, :hidden2] = jnp.broadcast_to(scale * loss, (1, hidden2))
-    for copy in stores:
-        copy.wait()
-
-
-def weight_kernel(
-    scale, n_edge, edge_ref, lines_ref, node_any, rep_any, first_any, bfirst_any, bsecond_any, extra_ref,
-    kept_out, sent_out, grads, grads2, node_ref, rep_ref, first_ref, bfirst_ref, bsecond_ref, sems,
-):
-    pairs = (
-        (node_any, node_ref), (rep_any, rep_ref), (bfirst_any, bfirst_ref), (bsecond_any, bsecond_ref),
-        (first_any, first_ref),
-    )
-    fetch = [pltpu.make_async_copy(src, dst, sems.at[i]) for i, (src, dst) in enumerate(pairs)]
-    for copy in fetch:
-        copy.start()
-    own_count, width = node_ref.shape
-    slots = rep_ref.shape[0]
-    edges = lines_ref.shape[1]
+    extra_ref[...] = jnp.zeros_like(extra_ref)
+    extra_ref[0:1, :hidden2] = scale * third
+    extra_ref[1:2, :hidden2] = jnp.broadcast_to(scale * loss, (1, hidden2))
+
     rows1 = 3 * width // n_edge
-    rows2 = grads2.shape[0] // n_edge
+    rows2 = hidden2 // n_edge
     rows = rows1 + rows2
-    near_pick = onehot(lines_ref[0:1, :], (own_count, edges), 0)
-    far_pick = onehot(lines_ref[1:2, :], (slots, edges), 0)
-    fetch[0].wait()
-    near = dot(node_ref[...], near_pick, 0, 0)
-    fetch[1].wait()
-    far = dot(rep_ref[...], far_pick, 0, 0)
-    fetch[2].wait()
     bfirst = bfirst_ref[...]
-    grads[:width] = scale * dot(near.astype(BF), bfirst)
-    grads[width : 2 * width] = scale * dot(far.astype(BF), bfirst)
-    grads[2 * width :] = scale * dot((near * far).astype(BF), bfirst)
-    fetch[3].wait()
-    fetch[4].wait()
     grads2[...] = scale * dot(bsecond_ref[...], first_ref[...], 0, 0)
+    for i in range(3):
+        grads[i * width : (i + 1) * width] = scale * dot(feat_ref[i], bfirst, 0, 0)
     edge = edge_ref[0]
     chip = edge // 2
     core = edge % 2
@@ -183,14 +147,33 @@
     extra = extra_ref[...]
     extra_high, extra_low = halves(extra)
     for j in range(chips):
-        owner = 2 * ((chip + j) % chips) + core
-        kept_out[j, :rows1] = grads[pl.ds(pl.multiple_of(owner * rows1, 8), rows1), :]
-        kept_out[j, rows1:rows] = grads2[pl.ds(pl.multiple_of(owner * rows2, 8), rows2), :]
-        kept_out[j, rows:] = extra
-        owner = 2 * ((chip + j) % chips) + 1 - core
-        sent_out[j, :rows1] = grads[pl.ds(pl.multiple_of(owner * rows1, 8), rows1), :].astype(BF)
-        sent_out[j, rows1:rows] = grads2[pl.ds(pl.multiple_of(owner * rows2, 8), rows2), :].astype(BF)
-        sent_out[j, rows:] = jnp.concatenate([extra_high, extra_low], axis=0)
+        there = 2 * ((chip + j) % chips)
+        part1 = pl.ds(pl.multiple_of((there + core) * rows1, 8), rows1)
+        part2 = pl.ds(pl.multiple_of((there + core) * rows2, 8), rows2)
+        store(grads.at[part1], kept_out.at[j, pl.ds(0, rows1)])
+        store(grads2.at[part2], kept_out.at[j, pl.ds(rows1, rows2)])
+        store(extra_ref, kept_out.at[j, pl.ds(rows, 8)])
+        part1 = pl.ds(pl.multiple_of((there + 1 - core) * rows1, 8), rows1)
+        part2 = pl.ds(pl.multiple_of((there + 1 - core) * rows2, 8), rows2)
+        sent_ref[j, :rows1] = grads[part1, :].astype(BF)
+        sent_ref[j, rows1:rows] = grads2[part2, :].astype(BF)
+        sent_ref[j, rows:] = jnp.concatenate([extra_high, extra_low], axis=0)
+        store(sent_ref.at[j], sent_out.at[j])
+
+    total = None
+    for tile in range(edges // TILE):
+        part = pl.ds(tile * TILE, TILE)
+        back_first = bfirst_ref[part]
+        block_b = dot(back_first, wf_ref[width : 2 * width], 1, 1)
+        block_c = dot(back_first, wf_ref[2 * width :], 1, 1)
+        high, low = halves(block_b + block_c * feat_ref[0, part].astype(F32))
+        place = onehot(lines_ref[1:2, part], (slots, TILE), 0)
+        term = dot(place, high) + dot(place, low)
+        total = term if total is None else total + term
+    slot_ref[...] = total.astype(BF)
+    store(slot_ref, slot_out)
+    for copy in stores:
+        copy.wait()
 
 
 def near_kernel(lines_ref, cols_ref, rep_ref, bfirst_ref, wf_ref, out_ref):
@@ -330,53 +313,35 @@
         answer.reshape(parts, cap, width), "dom", split_axis=0, concat_axis=0, tiled=True
     ).reshape(slots, width)
 
-    outs = [(slots, width), (edges, hidden), (edges, hidden), (edges, hidden2)]
-    slot_grad, first, back_first, back_second, extra = pl.pallas_call(
-        functools.partial(pair_kernel, scale),
-        out_shape=tuple(pltpu.HBM(shape, BF) for shape in outs)
-        + (jax.ShapeDtypeStruct((8, hidden), F32),),
-        in_specs=[SCALARS] + [WHOLE] * 4 + [FAR] + [WHOLE] * 2,
-        out_specs=(FAR,) * 4 + (WHOLE,),
-        scratch_shapes=[pltpu.VMEM((3 * width, hidden), BF)]
-        + [pltpu.VMEM(shape, BF) for shape in outs]
-        + [pltpu.SemaphoreType.DMA((3,)), pltpu.SemaphoreType.DMA((3 * edges // TILE + 1,))],
-        compiler_params=params(32),
-        cost_estimate=cost(6 * 10**9, 8 * MIB),
-        name="pair",
-    )(
-        live_count, cols, slot_index.reshape(1, edges), node_rows, replies, in_hbm(w_first), w_second,
-        w_third.reshape(1, hidden2),
-    )
-
-    returned = lax.all_to_all(
-        slot_grad.reshape(parts, cap, width), "dom", split_axis=0, concat_axis=0, tiled=True
-    ).reshape(slots, width)
-
-    kept, sent = pl.pallas_call(
-        functools.partial(weight_kernel, scale, n_edge),
-        out_shape=(
-            jax.ShapeDtypeStruct((chips, rows + 8, hidden), F32),
-            jax.ShapeDtypeStruct((chips, rows + 16, hidden), BF),
-        ),
-        in_specs=[SCALARS, WHOLE] + [FAR] * 5 + [WHOLE],
-        out_specs=(WHOLE, WHOLE),
+    outs = [(slots, width), (edges, hidden), (chips, rows + 8, hidden), (chips, rows + 16, hidden)]
+    slot_grad, back_first, kept, sent = pl.pallas_call(
+        functools.partial(pair_kernel, scale, n_edge),
+        out_shape=tuple(pltpu.HBM(shape, dtype) for shape, dtype in zip(outs, (BF, BF, F32, BF))),
+        in_specs=[SCALARS] * 2 + [WHOLE] * 4 + [FAR] + [WHOLE] * 2,
+        out_specs=(FAR,) * 4,
         scratch_shapes=[
-            pltpu.VMEM((3 * width, hidden), F32),
-            pltpu.VMEM((hidden2, hidden), F32),
-            pltpu.VMEM((own_count, width), BF),
+            pltpu.VMEM((3 * width, hidden), BF),
             pltpu.VMEM((slots, width), BF),
             pltpu.VMEM((edges, hidden), BF),
             pltpu.VMEM((edges, hidden), BF),
             pltpu.VMEM((edges, hidden2), BF),
-            pltpu.SemaphoreType.DMA((5,)),
+            pltpu.VMEM((3 * width, hidden), F32),
+            pltpu.VMEM((hidden2, hidden), F32),
+            pltpu.VMEM((8, hidden), F32),
+            pltpu.VMEM((chips, rows + 16, hidden), BF),
+            pltpu.VMEM((3, edges, width), BF),
+            pltpu.SemaphoreType.DMA((3,)),
+            pltpu.SemaphoreType.DMA((edges // TILE + 1 + 4 * chips,)),
         ],
-        compiler_params=params(32),
-        cost_estimate=FREE,
-        name="weights",
-    )(
-        edge, lines, in_hbm(node_rows), in_hbm(replies), in_hbm(first), in_hbm(back_first),
-        in_hbm(back_second), extra,
-    )
+        compiler_params=params(48),
+        cost_estimate=cost(6 * 10**9, 8 * MIB),
+        name="pair",
+    )(live_count, edge, cols, lines, node_rows, replies, in_hbm(w_first), w_second, w_third.reshape(1, hidden2))
+
+    returned = lax.all_to_all(
+        slot_grad.reshape(parts, cap, width), "dom", split_axis=0, concat_axis=0, tiled=True
+    ).reshape(slots, width)
+
     near_part = pl.pallas_call(
         near_kernel,
         out_shape=jax.ShapeDtypeStruct((own_count, width), F32),

time: 152 us -> 151 us (level)
  starting transfers between devices: 41.5 us -> 38.3 us
  Pallas kernels: 21 us -> 18.1 us
  local copies, waits for them, and re-layouts: 1.08 us -> 3.96 us
  waiting for transfers between devices: 52.6 us -> 54.7 us
    all_to_all x1, waiting for transfers between devices: 2.15 us -> 5.53 us  [body(): lax.all_to_all(slot_grad.reshape(parts, cap, width), 'dom', split_axis=0,...]
    all_to_all x1, starting transfers between devices: 12.8 us -> 9.62 us  [body(): lax.all_to_all(packed.reshape(parts, share, lanes), 'dom', split_axis=0,...]
    unnamed x19 -> x17, local copies, waits for them, and re-layouts: 0.86 us -> 3.74 us
    pallas_call x2 -> x1, Pallas kernels: 13.4 us -> 10.6 us  [body(): pl.pallas_call(functools.partial(pair_kernel, scale, n_edge), out_shape=t...]
  transfers between devices with their start and end apart: 10 -> 10, of which waited for: 9 -> 9; matrix products, arithmetic and copies ran while one was open for 1% -> 1% of each run, Pallas kernels for 6% -> 3%
where the time goes in v6:
time: 151 us; the launch traced here: 150 us
  waiting for transfers between devices  54.7 us (36%)
  starting transfers between devices  38.3 us (25%)
  blocking collectives  32.9 us (22%)
  Pallas kernels  18.1 us (12%)
  local copies, waits for them, and re-layouts  3.96 us (3%)
  between operations  1.52 us (1%)
    all_to_all x1, blocking collectives, body(): lax.all_to_all(requests, 'dom', split_axis=0, concat_axis=0, tiled=True)  32.9 us
    all_to_all x1, waiting for transfers between devices, body(): lax.all_to_all(answer.reshape(parts, cap, width), 'dom', split_axis=0, co...  29 us
    ppermute x3, waiting for transfers between devices, body(): got = lax.ppermute(sent, 'edge', partner)  10.8 us
    pallas_call x1, Pallas kernels, body(): pl.pallas_call(functools.partial(pair_kernel, scale, n_edge), out_shape=t...  10.6 us
    all_to_all x1, starting transfers between devices, body(): lax.all_to_all(packed.reshape(parts, share, lanes), 'dom', split_axis=0,...  9.62 us
    ppermute x3, starting transfers between devices, body(): lax.ppermute(packs[step - 1], 'edge', ahead(step))  9.42 us
    all_to_all x1, starting transfers between devices, body(): lax.all_to_all(slot_grad.reshape(parts, cap, width), 'dom', split_axis=0,...  6.9 us
    ppermute x3, starting transfers between devices, body(): got = lax.ppermute(sent, 'edge', partner)  5.76 us
  transfers between devices with their start and end apart: 10, of which 9 were waited for; matrix products, arithmetic and copies ran while one was open for 1% of the time, Pallas kernels for 3%

profile of v6, /device:TPU:6, one launch (start us, length us, event | category | flops | bytes accessed | tf_op | source)
XLA Modules:
  0.0 150.2 jit_solution(6150651576437029164)
XLA Ops:
  0.7 0.8 copy.20
  1.5 32.9 %all_to_all.26 = s32[64,1,8]{2,1,0:T(1,128)S(1)} all-to-all(s32[64,1,8]{2,1,0:T(1,128)S(1)} %bitcast.23), channel_id=1, replica_groups=mesh['dom'=64,'edge'=8] {'dom'}, dimensions={0} | all-to-all | bytes 4096 | tf_op jit(solution)/shard_map/all_to_all | solution.py:299
  34.5 2.1 %answer.1 = (bf16[512,512]{1,0:T(8,128)(2,1)}, s32[1,512]{1,0:T(1,128)S(1)}) custom-call(s32[64,8]{1,0:T(8,128)S(1)} %bitcast.20, bf16[256,512]{1,0:T(8,128)(2,1)} %node_ref.1), custom_call_target="tpu_custom_call" | custom-call | tf_op jit(solution)/shard_map/answer/pallas_call | solution.py:300
  36.6 4.6 %all-to-all-start.1 = ((bf16[64,8,512]{2,1,0:T(8,128)(2,1)}), bf16[64,8,512]{2,1,0:T(8,128)(2,1)S(1)}, u32[]{:S(2)}, u32[]{:S(2)}) async-start(bf16[64,8,512]{2,1,0:T(8,128)(2,1)} %bitcast.8), calls=%async_computation.1 | async-start | bytes 1048576 | tf_op jit(solution)/shard_map/all_to_all | solution.py:312
  41.9 0.7 pad_add_fusion
  42.6 0.2 copy.22.cols_ref
  42.9 29.0 %all-to-all-done.1 = bf16[64,8,512]{2,1,0:T(8,128)(2,1)S(1)} async-done(((bf16[64,8,512]{2,1,0:T(8,128)(2,1)}), bf16[64,8,512]{2,1,0:T(8,128)(2,1)S(1)}, u32[]{:S(2)}, u32[]{:S(2)}) %all-to-all-start.1) | async-done | bytes 524320 | tf_op jit(solution)/shard_map/all_to_all | solution.py:312
  71.9 10.6 %pair.1 = (bf16[512,512]{1,0:T(8,128)(2,1)}, bf16[1024,512]{1,0:T(8,128)(2,1)}, f32[4,216,512]{2,1,0:T(8,128)}, bf16[4,224,512]{2,1,0:T(8,128)(2,1)}) custom-call(s32[1]{0:T(128)S(6)} %copy.24.live_ref, s32[1]{0:T(128)} %bitcast.edge_ref, s32[1024,3]{1,0:T(8,128)S(1)} %copy.22.cols_ref, s32[2,1024]{1,0:T(2,128)S(1)} %pad_add_fusion.1.lines_ref, ...), custom_call_target="tpu_custom_call" | custom-call | flops 6000000000 | bytes 8388608 | tf_op jit(solution)/shard_map/pair/pallas_call | solution.py:317
  82.4 6.9 %all-to-all-start.2 = ((bf16[64,8,512]{2,1,0:T(8,128)(2,1)}), bf16[64,8,512]{2,1,0:T(8,128)(2,1)S(1)}, u32[]{:S(2)}, u32[]{:S(2)}) async-start(bf16[64,8,512]{2,1,0:T(8,128)(2,1)} %bitcast.22), calls=%async_computation.2 | async-start | bytes 1048576 | tf_op jit(solution)/shard_map/all_to_all | solution.py:341
  89.3 1.9 %collective-permute-start = (bf16[4,224,512]{2,1,0:T(8,128)(2,1)}, bf16[4,224,512]{2,1,0:T(8,128)(2,1)S(1)}, u32[]{:S(2)}, u32[]{:S(2)}) collective-permute-start(bf16[4,224,512]{2,1,0:T(8,128)(2,1)} %get-tuple-element.31), channel_id=1, source_target_pairs={{0,1},{1,0},{2,3},{3,2},{4,5},{5,4},{6,7},{7,6},{8,9},{9,8},{10,11... | collective-permute-start | bytes 2752520 | tf_op jit(solution)/shard_map/ppermute | solution.py:364
  91.3 2.6 %collective-permute-done.got_ref = bf16[4,224,512]{2,1,0:T(8,128)(2,1)S(1)} collective-permute-done((bf16[4,224,512]{2,1,0:T(8,128)(2,1)}, bf16[4,224,512]{2,1,0:T(8,128)(2,1)S(1)}, u32[]{:S(2)}, u32[]{:S(2)}) %collective-permute-start) | collective-permute-done | bytes 917536 | tf_op jit(solution)/shard_map/ppermute | solution.py:364
  93.9 1.5 copy-done
  95.6 3.3 %collective-permute-start.1 = (bf16[224,512]{1,0:T(8,128)(2,1)S(1)}, bf16[224,512]{1,0:T(8,128)(2,1)S(1)}, u32[]{:S(2)}, u32[]{:S(2)}) collective-permute-start(bf16[224,512]{1,0:T(8,128)(2,1)S(1)} %get-tuple-element.33), channel_id=1, source_target_pairs={{0,4},{1,5},{2,6},{3,7},{4,0},{5,1},{6,2},{7,3},{8,12},{9,13},{10,... | collective-permute-start | bytes 688136 | tf_op jit(solution)/shard_map/ppermute | solution.py:365
  98.9 4.0 %collective-permute-start.2 = (bf16[224,512]{1,0:T(8,128)(2,1)S(1)}, bf16[224,512]{1,0:T(8,128)(2,1)S(1)}, u32[]{:S(2)}, u32[]{:S(2)}) collective-permute-start(bf16[224,512]{1,0:T(8,128)(2,1)S(1)} %get-tuple-element.34), channel_id=1, source_target_pairs={{0,2},{1,3},{2,4},{3,5},{4,6},{5,7},{6,0},{7,1},{8,10},{9,11},{10,... | collective-permute-start | bytes 688136 | tf_op jit(solution)/shard_map/ppermute | solution.py:365
  102.9 2.1 %collective-permute-start.3 = (bf16[224,512]{1,0:T(8,128)(2,1)S(1)}, bf16[224,512]{1,0:T(8,128)(2,1)S(1)}, u32[]{:S(2)}, u32[]{:S(2)}) collective-permute-start(bf16[224,512]{1,0:T(8,128)(2,1)S(1)} %get-tuple-element.35), channel_id=1, source_target_pairs={{0,6},{1,7},{2,0},{3,1},{4,2},{5,3},{6,4},{7,5},{8,14},{9,15},{10,... | collective-permute-start | bytes 688136 | tf_op jit(solution)/shard_map/ppermute | solution.py:365
  105.0 1.4 copy-done.1
  106.4 2.5 %near.1.refs_4_.near_ref = f32[256,512]{1,0:T(8,128)S(1)} custom-call(s32[2,1024]{1,0:T(2,128)S(1)} %pad_add_fusion.1.lines_ref, s32[1024,3]{1,0:T(8,128)S(1)} %copy.22.cols_ref, bf16[512,512]{1,0:T(8,128)(2,1)S(1)} %bitcast.19, bf16[1024,512]{1,0:T(8,128)(2,1)S(1)} %copy-done.2, bf16[1536,512]{1,0:T(8,128)(2,1)S(1)} %copy-done.1), custom_call_target="tpu_custom_call" | custom-call | tf_op jit(solution)/shard_map/near/pallas_call | solution.py:345
  108.9 0.4 collective-permute-done.2.refs_2_
  109.3 3.8 %collective-permute-done.3.refs_3_ = bf16[224,512]{1,0:T(8,128)(2,1)S(1)} collective-permute-done((bf16[224,512]{1,0:T(8,128)(2,1)S(1)}, bf16[224,512]{1,0:T(8,128)(2,1)S(1)}, u32[]{:S(2)}, u32[]{:S(2)}) %collective-permute-start.3) | collective-permute-done | bytes 229408 | tf_op jit(solution)/shard_map/ppermute | solution.py:365
  113.1 1.0 total.1.packed_ref
  114.1 5.5 %all-to-all-done.2 = bf16[64,8,512]{2,1,0:T(8,128)(2,1)S(1)} async-done(((bf16[64,8,512]{2,1,0:T(8,128)(2,1)}), bf16[64,8,512]{2,1,0:T(8,128)(2,1)S(1)}, u32[]{:S(2)}, u32[]{:S(2)}) %all-to-all-start.2) | async-done | bytes 524320 | tf_op jit(solution)/shard_map/all_to_all | solution.py:341
  119.6 0.3 owned.1
  120.0 9.6 %all-to-all-start.3 = ((bf16[64,8,256]{2,1,0:T(8,128)(2,1)}), bf16[64,8,256]{2,1,0:T(8,128)(2,1)S(1)}, u32[]{:S(2)}, u32[]{:S(2)}) async-start(bf16[64,8,256]{2,1,0:T(8,128)(2,1)} %bitcast.13), calls=%async_computation.3 | async-start | bytes 524288 | tf_op jit(solution)/shard_map/all_to_all | solution.py:390
  129.6 1.9 %collective-permute-start.4 = (f32[4,32,512]{2,1,0:T(8,128)S(1)}, f32[4,32,512]{2,1,0:T(8,128)S(1)}, u32[]{:S(2)}, u32[]{:S(2)}) collective-permute-start(f32[4,32,512]{2,1,0:T(8,128)S(1)} %get-tuple-element.42), channel_id=1, source_target_pairs={{0,1},{1,0},{2,3},{3,2},{4,5},{5,4},{6,7},{7,6},{8,9},{9,8},{10,11... | collective-permute-start | bytes 786440 | tf_op jit(solution)/shard_map/ppermute | solution.py:410
  131.5 1.5 collective-permute-done.4.got_ref
  133.1 1.9 %collective-permute-start.5 = (bf16[2,32,512]{2,1,0:T(8,128)(2,1)S(1)}, bf16[2,32,512]{2,1,0:T(8,128)(2,1)S(1)}, u32[]{:S(2)}, u32[]{:S(2)}) collective-permute-start(bf16[2,32,512]{2,1,0:T(8,128)(2,1)S(1)} %get-tuple-element.44), channel_id=1, source_target_pairs={{0,2},{1,3},{2,0},{3,1},{4,6},{5,7},{6,4},{7,5},{8,10},{9,11},{10,... | collective-permute-start | bytes 196616 | tf_op jit(solution)/shard_map/ppermute | solution.py:410
  135.0 4.2 %collective-permute-done.5.got_ref = bf16[2,32,512]{2,1,0:T(8,128)(2,1)S(1)} collective-permute-done((bf16[2,32,512]{2,1,0:T(8,128)(2,1)S(1)}, bf16[2,32,512]{2,1,0:T(8,128)(2,1)S(1)}, u32[]{:S(2)}, u32[]{:S(2)}) %collective-permute-start.5) | collective-permute-done | bytes 65568 | tf_op jit(solution)/shard_map/ppermute | solution.py:410
  139.2 1.9 %collective-permute-start.6 = (bf16[1,32,512]{2,1,0:T(8,128)(2,1)S(1)}, bf16[1,32,512]{2,1,0:T(8,128)(2,1)S(1)}, u32[]{:S(2)}, u32[]{:S(2)}) collective-permute-start(bf16[1,32,512]{2,1,0:T(8,128)(2,1)S(1)} %get-tuple-element.46), channel_id=1, source_target_pairs={{0,6},{1,7},{2,4},{3,5},{4,2},{5,3},{6,0},{7,1},{8,14},{9,15},{10,... | collective-permute-start | bytes 98312 | tf_op jit(solution)/shard_map/ppermute | solution.py:410
  141.2 5.1 %collective-permute-done.6.got_ref = bf16[1,32,512]{2,1,0:T(8,128)(2,1)S(1)} collective-permute-done((bf16[1,32,512]{2,1,0:T(8,128)(2,1)S(1)}, bf16[1,32,512]{2,1,0:T(8,128)(2,1)S(1)}, u32[]{:S(2)}, u32[]{:S(2)}) %collective-permute-start.6) | collective-permute-done | bytes 32800 | tf_op jit(solution)/shard_map/ppermute | solution.py:410
  146.3 0.6 last.1
  146.9 2.5 %all-to-all-done.3.got_ref = bf16[64,8,256]{2,1,0:T(8,128)(2,1)S(1)} async-done(((bf16[64,8,256]{2,1,0:T(8,128)(2,1)}), bf16[64,8,256]{2,1,0:T(8,128)(2,1)S(1)}, u32[]{:S(2)}, u32[]{:S(2)}) %all-to-all-start.3) | async-done | bytes 262176 | tf_op jit(solution)/shard_map/all_to_all | solution.py:390
  149.4 0.8 final.1
  (19 shorter events, 0.3 us)
Async XLA Ops:
  0.6 71.2 %copy-start.3 = (bf16[256,512]{1,0:T(8,128)(2,1)S(1)}, bf16[256,512]{1,0:T(8,128)(2,1)}, u32[]{:S(2)}) copy-start(bf16[256,512]{1,0:T(8,128)(2,1)} %node_ref.1) | copy-start | bytes 786436
  0.6 42.2 %copy-start.7 = (s32[1024]{0:T(1024)S(1)}, s32[1024]{0:T(1024)}, u32[]{:S(2)}) copy-start(s32[1024]{0:T(1024)} %param.13) | copy-start | bytes 12292
  0.7 42.2 %copy-start.6 = (s32[1024]{0:T(1024)S(1)}, s32[1024]{0:T(1024)}, u32[]{:S(2)}) copy-start(s32[1024]{0:T(1024)} %param.15) | copy-start | bytes 12292
  0.7 71.2 %copy-start.5 = (bf16[128]{0:T(256)(128)(2,1)S(1)}, bf16[128]{0:T(256)(128)(2,1)}, u32[]{:S(2)}) copy-start(bf16[128]{0:T(256)(128)(2,1)} %param.12) | copy-start | bytes 772
  0.7 71.2 %copy-start.4 = (bf16[512,128]{1,0:T(8,128)(2,1)S(1)}, bf16[512,128]{1,0:T(8,128)(2,1)}, u32[]{:S(2)}) copy-start(bf16[512,128]{1,0:T(8,128)(2,1)} %ws_ref.1) | copy-start | bytes 393220
  36.6 35.3 %all-to-all-start.1 = ((bf16[64,8,512]{2,1,0:T(8,128)(2,1)}), bf16[64,8,512]{2,1,0:T(8,128)(2,1)S(1)}, u32[]{:S(2)}, u32[]{:S(2)}) async-start(bf16[64,8,512]{2,1,0:T(8,128)(2,1)} %bitcast.8), calls=%async_computation.1 | async-start | bytes 1048576 | tf_op jit(solution)/shard_map/all_to_all | solution.py:312
  82.4 22.6 %copy-start.2 = (bf16[1024,512]{1,0:T(8,128)(2,1)S(1)}, bf16[1024,512]{1,0:T(8,128)(2,1)}, u32[]{:S(2)}) copy-start(bf16[1024,512]{1,0:T(8,128)(2,1)} %get-tuple-element.28.bfirst_ref) | copy-start | bytes 3145732
  82.4 37.2 %all-to-all-start.2 = ((bf16[64,8,512]{2,1,0:T(8,128)(2,1)}), bf16[64,8,512]{2,1,0:T(8,128)(2,1)S(1)}, u32[]{:S(2)}, u32[]{:S(2)}) async-start(bf16[64,8,512]{2,1,0:T(8,128)(2,1)} %bitcast.22), calls=%async_computation.2 | async-start | bytes 1048576 | tf_op jit(solution)/shard_map/all_to_all | solution.py:341
  89.3 4.6 %collective-permute-start = (bf16[4,224,512]{2,1,0:T(8,128)(2,1)}, bf16[4,224,512]{2,1,0:T(8,128)(2,1)S(1)}, u32[]{:S(2)}, u32[]{:S(2)}) collective-permute-start(bf16[4,224,512]{2,1,0:T(8,128)(2,1)} %get-tuple-element.31), channel_id=1, source_target_pairs={{0,1},{1,0},{2,3},{3,2},{4,5},{5,4},{6,7},{7,6},{8,9},{9,8},{10,11... | collective-permute-start | bytes 2752520 | tf_op jit(solution)/shard_map/ppermute | solution.py:364
  93.9 1.5 copy-start
  95.6 13.4 %collective-permute-start.1 = (bf16[224,512]{1,0:T(8,128)(2,1)S(1)}, bf16[224,512]{1,0:T(8,128)(2,1)S(1)}, u32[]{:S(2)}, u32[]{:S(2)}) collective-permute-start(bf16[224,512]{1,0:T(8,128)(2,1)S(1)} %get-tuple-element.33), channel_id=1, source_target_pairs={{0,4},{1,5},{2,6},{3,7},{4,0},{5,1},{6,2},{7,3},{8,12},{9,13},{10,... | collective-permute-start | bytes 688136 | tf_op jit(solution)/shard_map/ppermute | solution.py:365
  98.9 10.4 %collective-permute-start.2 = (bf16[224,512]{1,0:T(8,128)(2,1)S(1)}, bf16[224,512]{1,0:T(8,128)(2,1)S(1)}, u32[]{:S(2)}, u32[]{:S(2)}) collective-permute-start(bf16[224,512]{1,0:T(8,128)(2,1)S(1)} %get-tuple-element.34), channel_id=1, source_target_pairs={{0,2},{1,3},{2,4},{3,5},{4,6},{5,7},{6,0},{7,1},{8,10},{9,11},{10,... | collective-permute-start | bytes 688136 | tf_op jit(solution)/shard_map/ppermute | solution.py:365
  102.9 10.2 %collective-permute-start.3 = (bf16[224,512]{1,0:T(8,128)(2,1)S(1)}, bf16[224,512]{1,0:T(8,128)(2,1)S(1)}, u32[]{:S(2)}, u32[]{:S(2)}) collective-permute-start(bf16[224,512]{1,0:T(8,128)(2,1)S(1)} %get-tuple-element.35), channel_id=1, source_target_pairs={{0,6},{1,7},{2,0},{3,1},{4,2},{5,3},{6,4},{7,5},{8,14},{9,15},{10,... | collective-permute-start | bytes 688136 | tf_op jit(solution)/shard_map/ppermute | solution.py:365
  105.0 1.4 copy-start.1
  120.0 29.5 %all-to-all-start.3 = ((bf16[64,8,256]{2,1,0:T(8,128)(2,1)}), bf16[64,8,256]{2,1,0:T(8,128)(2,1)S(1)}, u32[]{:S(2)}, u32[]{:S(2)}) async-start(bf16[64,8,256]{2,1,0:T(8,128)(2,1)} %bitcast.13), calls=%async_computation.3 | async-start | bytes 524288 | tf_op jit(solution)/shard_map/all_to_all | solution.py:390
  129.6 3.4 %collective-permute-start.4 = (f32[4,32,512]{2,1,0:T(8,128)S(1)}, f32[4,32,512]{2,1,0:T(8,128)S(1)}, u32[]{:S(2)}, u32[]{:S(2)}) collective-permute-start(f32[4,32,512]{2,1,0:T(8,128)S(1)} %get-tuple-element.42), channel_id=1, source_target_pairs={{0,1},{1,0},{2,3},{3,2},{4,5},{5,4},{6,7},{7,6},{8,9},{9,8},{10,11... | collective-permute-start | bytes 786440 | tf_op jit(solution)/shard_map/ppermute | solution.py:410
  133.1 6.2 %collective-permute-start.5 = (bf16[2,32,512]{2,1,0:T(8,128)(2,1)S(1)}, bf16[2,32,512]{2,1,0:T(8,128)(2,1)S(1)}, u32[]{:S(2)}, u32[]{:S(2)}) collective-permute-start(bf16[2,32,512]{2,1,0:T(8,128)(2,1)S(1)} %get-tuple-element.44), channel_id=1, source_target_pairs={{0,2},{1,3},{2,0},{3,1},{4,6},{5,7},{6,4},{7,5},{8,10},{9,11},{10,... | collective-permute-start | bytes 196616 | tf_op jit(solution)/shard_map/ppermute | solution.py:410
  139.2 7.0 %collective-permute-start.6 = (bf16[1,32,512]{2,1,0:T(8,128)(2,1)S(1)}, bf16[1,32,512]{2,1,0:T(8,128)(2,1)S(1)}, u32[]{:S(2)}, u32[]{:S(2)}) collective-permute-start(bf16[1,32,512]{2,1,0:T(8,128)(2,1)S(1)} %get-tuple-element.46), channel_id=1, source_target_pairs={{0,6},{1,7},{2,4},{3,5},{4,2},{5,3},{6,0},{7,1},{8,14},{9,15},{10,... | collective-permute-start | bytes 98312 | tf_op jit(solution)/shard_map/ppermute | solution.py:410

commit v7 on v6

--- a/solution.py
+++ b/solution.py
@@ -113,10 +113,11 @@
         first_ref[part] = first
         pre_second = dot(first, ws_ref[...])
         sig = jax.nn.sigmoid(pre_second)
-        second = (pre_second * sig).astype(BF).astype(F32)
+        second_b = (pre_second * sig).astype(BF)
+        second = second_b.astype(F32)
         slope_second = sig * (1.0 + pre_second * (1.0 - sig))
-        logits = jnp.sum(second * w_third, axis=1, keepdims=True)
-        place = tile * TILE + lax.broadcasted_iota(I32, (TILE, 1), 0)
+        logits = dot(second_b, jnp.broadcast_to(wt_ref[...], (hidden2, hidden2)), 1, 1)
+        place = tile * TILE + lax.broadcasted_iota(I32, (TILE, hidden2), 0)
         live = jnp.where(place < live_ref[0], 1.0, 0.0)
         slope = live * (jax.nn.sigmoid(logits) - target)
         back_second = (slope * w_third * slope_second).astype(BF)
@@ -131,7 +132,7 @@
         third = term if third is None else third + term
     extra_ref[...] = jnp.zeros_like(extra_ref)
     extra_ref[0:1, :hidden2] = scale * third
-    extra_ref[1:2, :hidden2] = jnp.broadcast_to(scale * loss, (1, hidden2))
+    extra_ref[1:2, :hidden2] = scale * loss
 
     rows1 = 3 * width // n_edge
     rows2 = hidden2 // n_edge
@@ -166,9 +167,8 @@
         back_first = bfirst_ref[part]
         block_b = dot(back_first, wf_ref[width : 2 * width], 1, 1)
         block_c = dot(back_first, wf_ref[2 * width :], 1, 1)
-        high, low = halves(block_b + block_c * feat_ref[0, part].astype(F32))
         place = onehot(lines_ref[1:2, part], (slots, TILE), 0)
-        term = dot(place, high) + dot(place, low)
+        term = dot(place, (block_b + block_c * feat_ref[0, part].astype(F32)).astype(BF))
         total = term if total is None else total + term
     slot_ref[...] = total.astype(BF)
     store(slot_ref, slot_out)

time: 151 us -> 150 us (level)
  no operation moved by 1% of the time
where the time goes in v7:
time: 150 us; the launch traced here: 149 us
  waiting for transfers between devices  54.7 us (36%)
  starting transfers between devices  38.3 us (26%)
  blocking collectives  32.9 us (22%)
  Pallas kernels  17.2 us (11%)
  local copies, waits for them, and re-layouts  3.96 us (3%)
  between operations  1.52 us (1%)
    all_to_all x1, blocking collectives, body(): lax.all_to_all(requests, 'dom', split_axis=0, concat_axis=0, tiled=True)  32.9 us
    all_to_all x1, waiting for transfers between devices, body(): lax.all_to_all(answer.reshape(parts, cap, width), 'dom', split_axis=0, co...  29 us
    ppermute x3, waiting for transfers between devices, body(): got = lax.ppermute(sent, 'edge', partner)  10.8 us
    all_to_all x1, starting transfers between devices, body(): lax.all_to_all(packed.reshape(parts, share, lanes), 'dom', split_axis=0,...  9.63 us
    pallas_call x1, Pallas kernels, body(): pl.pallas_call(functools.partial(pair_kernel, scale, n_edge), out_shape=t...  9.6 us
    ppermute x3, starting transfers between devices, body(): lax.ppermute(packs[step - 1], 'edge', ahead(step))  9.41 us
    all_to_all x1, starting transfers between devices, body(): lax.all_to_all(slot_grad.reshape(parts, cap, width), 'dom', split_axis=0,...  6.9 us
    ppermute x3, starting transfers between devices, body(): got = lax.ppermute(sent, 'edge', partner)  5.76 us
  transfers between devices with their start and end apart: 10, of which 9 were waited for; matrix products, arithmetic and copies ran while one was open for 1% of the time, Pallas kernels for 3%

profile of v7, /device:TPU:6, one launch (start us, length us, event | category | flops | bytes accessed | tf_op | source)
XLA Modules:
  0.0 149.3 jit_solution(15633369978006408013)
XLA Ops:
  0.7 0.8 copy.20
  1.5 32.9 %all_to_all.26 = s32[64,1,8]{2,1,0:T(1,128)S(1)} all-to-all(s32[64,1,8]{2,1,0:T(1,128)S(1)} %bitcast.23), channel_id=1, replica_groups=mesh['dom'=64,'edge'=8] {'dom'}, dimensions={0} | all-to-all | bytes 4096 | tf_op jit(solution)/shard_map/all_to_all | solution.py:299
  34.5 2.1 %answer.1 = (bf16[512,512]{1,0:T(8,128)(2,1)}, s32[1,512]{1,0:T(1,128)S(1)}) custom-call(s32[64,8]{1,0:T(8,128)S(1)} %bitcast.20, bf16[256,512]{1,0:T(8,128)(2,1)} %node_ref.1), custom_call_target="tpu_custom_call" | custom-call | tf_op jit(solution)/shard_map/answer/pallas_call | solution.py:300
  36.6 4.6 %all-to-all-start.1 = ((bf16[64,8,512]{2,1,0:T(8,128)(2,1)}), bf16[64,8,512]{2,1,0:T(8,128)(2,1)S(1)}, u32[]{:S(2)}, u32[]{:S(2)}) async-start(bf16[64,8,512]{2,1,0:T(8,128)(2,1)} %bitcast.8), calls=%async_computation.1 | async-start | bytes 1048576 | tf_op jit(solution)/shard_map/all_to_all | solution.py:312
  41.9 0.7 pad_add_fusion
  42.6 0.2 copy.22.cols_ref
  42.9 29.0 %all-to-all-done.1 = bf16[64,8,512]{2,1,0:T(8,128)(2,1)S(1)} async-done(((bf16[64,8,512]{2,1,0:T(8,128)(2,1)}), bf16[64,8,512]{2,1,0:T(8,128)(2,1)S(1)}, u32[]{:S(2)}, u32[]{:S(2)}) %all-to-all-start.1) | async-done | bytes 524320 | tf_op jit(solution)/shard_map/all_to_all | solution.py:312
  71.9 9.6 %pair.1 = (bf16[512,512]{1,0:T(8,128)(2,1)}, bf16[1024,512]{1,0:T(8,128)(2,1)}, f32[4,216,512]{2,1,0:T(8,128)}, bf16[4,224,512]{2,1,0:T(8,128)(2,1)}) custom-call(s32[1]{0:T(128)S(6)} %copy.24.live_ref, s32[1]{0:T(128)} %bitcast.edge_ref, s32[1024,3]{1,0:T(8,128)S(1)} %copy.22.cols_ref, s32[2,1024]{1,0:T(2,128)S(1)} %pad_add_fusion.1.lines_ref, ...), custom_call_target="tpu_custom_call" | custom-call | flops 6000000000 | bytes 8388608 | tf_op jit(solution)/shard_map/pair/pallas_call | solution.py:317
  81.5 6.9 %all-to-all-start.2 = ((bf16[64,8,512]{2,1,0:T(8,128)(2,1)}), bf16[64,8,512]{2,1,0:T(8,128)(2,1)S(1)}, u32[]{:S(2)}, u32[]{:S(2)}) async-start(bf16[64,8,512]{2,1,0:T(8,128)(2,1)} %bitcast.22), calls=%async_computation.2 | async-start | bytes 1048576 | tf_op jit(solution)/shard_map/all_to_all | solution.py:341
  88.4 1.9 %collective-permute-start = (bf16[4,224,512]{2,1,0:T(8,128)(2,1)}, bf16[4,224,512]{2,1,0:T(8,128)(2,1)S(1)}, u32[]{:S(2)}, u32[]{:S(2)}) collective-permute-start(bf16[4,224,512]{2,1,0:T(8,128)(2,1)} %get-tuple-element.31), channel_id=1, source_target_pairs={{0,1},{1,0},{2,3},{3,2},{4,5},{5,4},{6,7},{7,6},{8,9},{9,8},{10,11... | collective-permute-start | bytes 2752520 | tf_op jit(solution)/shard_map/ppermute | solution.py:364
  90.3 2.6 %collective-permute-done.got_ref = bf16[4,224,512]{2,1,0:T(8,128)(2,1)S(1)} collective-permute-done((bf16[4,224,512]{2,1,0:T(8,128)(2,1)}, bf16[4,224,512]{2,1,0:T(8,128)(2,1)S(1)}, u32[]{:S(2)}, u32[]{:S(2)}) %collective-permute-start) | collective-permute-done | bytes 917536 | tf_op jit(solution)/shard_map/ppermute | solution.py:364
  93.0 1.5 copy-done
  94.6 3.3 %collective-permute-start.1 = (bf16[224,512]{1,0:T(8,128)(2,1)S(1)}, bf16[224,512]{1,0:T(8,128)(2,1)S(1)}, u32[]{:S(2)}, u32[]{:S(2)}) collective-permute-start(bf16[224,512]{1,0:T(8,128)(2,1)S(1)} %get-tuple-element.33), channel_id=1, source_target_pairs={{0,4},{1,5},{2,6},{3,7},{4,0},{5,1},{6,2},{7,3},{8,12},{9,13},{10,... | collective-permute-start | bytes 688136 | tf_op jit(solution)/shard_map/ppermute | solution.py:365
  97.9 4.0 %collective-permute-start.2 = (bf16[224,512]{1,0:T(8,128)(2,1)S(1)}, bf16[224,512]{1,0:T(8,128)(2,1)S(1)}, u32[]{:S(2)}, u32[]{:S(2)}) collective-permute-start(bf16[224,512]{1,0:T(8,128)(2,1)S(1)} %get-tuple-element.34), channel_id=1, source_target_pairs={{0,2},{1,3},{2,4},{3,5},{4,6},{5,7},{6,0},{7,1},{8,10},{9,11},{10,... | collective-permute-start | bytes 688136 | tf_op jit(solution)/shard_map/ppermute | solution.py:365
  101.9 2.1 %collective-permute-start.3 = (bf16[224,512]{1,0:T(8,128)(2,1)S(1)}, bf16[224,512]{1,0:T(8,128)(2,1)S(1)}, u32[]{:S(2)}, u32[]{:S(2)}) collective-permute-start(bf16[224,512]{1,0:T(8,128)(2,1)S(1)} %get-tuple-element.35), channel_id=1, source_target_pairs={{0,6},{1,7},{2,0},{3,1},{4,2},{5,3},{6,4},{7,5},{8,14},{9,15},{10,... | collective-permute-start | bytes 688136 | tf_op jit(solution)/shard_map/ppermute | solution.py:365
  104.1 1.4 copy-done.1
  105.5 2.5 %near.1.refs_4_.near_ref = f32[256,512]{1,0:T(8,128)S(1)} custom-call(s32[2,1024]{1,0:T(2,128)S(1)} %pad_add_fusion.1.lines_ref, s32[1024,3]{1,0:T(8,128)S(1)} %copy.22.cols_ref, bf16[512,512]{1,0:T(8,128)(2,1)S(1)} %bitcast.19, bf16[1024,512]{1,0:T(8,128)(2,1)S(1)} %copy-done.2, bf16[1536,512]{1,0:T(8,128)(2,1)S(1)} %copy-done.1), custom_call_target="tpu_custom_call" | custom-call | tf_op jit(solution)/shard_map/near/pallas_call | solution.py:345
  108.0 0.4 collective-permute-done.2.refs_2_
  108.4 3.8 %collective-permute-done.3.refs_3_ = bf16[224,512]{1,0:T(8,128)(2,1)S(1)} collective-permute-done((bf16[224,512]{1,0:T(8,128)(2,1)S(1)}, bf16[224,512]{1,0:T(8,128)(2,1)S(1)}, u32[]{:S(2)}, u32[]{:S(2)}) %collective-permute-start.3) | collective-permute-done | bytes 229408 | tf_op jit(solution)/shard_map/ppermute | solution.py:365
  112.1 1.0 total.1.packed_ref
  113.1 5.5 %all-to-all-done.2 = bf16[64,8,512]{2,1,0:T(8,128)(2,1)S(1)} async-done(((bf16[64,8,512]{2,1,0:T(8,128)(2,1)}), bf16[64,8,512]{2,1,0:T(8,128)(2,1)S(1)}, u32[]{:S(2)}, u32[]{:S(2)}) %all-to-all-start.2) | async-done | bytes 524320 | tf_op jit(solution)/shard_map/all_to_all | solution.py:341
  118.7 0.3 owned.1
  119.0 9.6 %all-to-all-start.3 = ((bf16[64,8,256]{2,1,0:T(8,128)(2,1)}), bf16[64,8,256]{2,1,0:T(8,128)(2,1)S(1)}, u32[]{:S(2)}, u32[]{:S(2)}) async-start(bf16[64,8,256]{2,1,0:T(8,128)(2,1)} %bitcast.13), calls=%async_computation.3 | async-start | bytes 524288 | tf_op jit(solution)/shard_map/all_to_all | solution.py:390
  128.6 1.9 %collective-permute-start.4 = (f32[4,32,512]{2,1,0:T(8,128)S(1)}, f32[4,32,512]{2,1,0:T(8,128)S(1)}, u32[]{:S(2)}, u32[]{:S(2)}) collective-permute-start(f32[4,32,512]{2,1,0:T(8,128)S(1)} %get-tuple-element.42), channel_id=1, source_target_pairs={{0,1},{1,0},{2,3},{3,2},{4,5},{5,4},{6,7},{7,6},{8,9},{9,8},{10,11... | collective-permute-start | bytes 786440 | tf_op jit(solution)/shard_map/ppermute | solution.py:410
  130.6 1.5 %collective-permute-done.4.got_ref = f32[4,32,512]{2,1,0:T(8,128)S(1)} collective-permute-done((f32[4,32,512]{2,1,0:T(8,128)S(1)}, f32[4,32,512]{2,1,0:T(8,128)S(1)}, u32[]{:S(2)}, u32[]{:S(2)}) %collective-permute-start.4) | collective-permute-done | bytes 262176 | tf_op jit(solution)/shard_map/ppermute | solution.py:410
  132.1 1.9 %collective-permute-start.5 = (bf16[2,32,512]{2,1,0:T(8,128)(2,1)S(1)}, bf16[2,32,512]{2,1,0:T(8,128)(2,1)S(1)}, u32[]{:S(2)}, u32[]{:S(2)}) collective-permute-start(bf16[2,32,512]{2,1,0:T(8,128)(2,1)S(1)} %get-tuple-element.44), channel_id=1, source_target_pairs={{0,2},{1,3},{2,0},{3,1},{4,6},{5,7},{6,4},{7,5},{8,10},{9,11},{10,... | collective-permute-start | bytes 196616 | tf_op jit(solution)/shard_map/ppermute | solution.py:410
  134.0 4.2 %collective-permute-done.5.got_ref = bf16[2,32,512]{2,1,0:T(8,128)(2,1)S(1)} collective-permute-done((bf16[2,32,512]{2,1,0:T(8,128)(2,1)S(1)}, bf16[2,32,512]{2,1,0:T(8,128)(2,1)S(1)}, u32[]{:S(2)}, u32[]{:S(2)}) %collective-permute-start.5) | collective-permute-done | bytes 65568 | tf_op jit(solution)/shard_map/ppermute | solution.py:410
  138.3 1.9 %collective-permute-start.6 = (bf16[1,32,512]{2,1,0:T(8,128)(2,1)S(1)}, bf16[1,32,512]{2,1,0:T(8,128)(2,1)S(1)}, u32[]{:S(2)}, u32[]{:S(2)}) collective-permute-start(bf16[1,32,512]{2,1,0:T(8,128)(2,1)S(1)} %get-tuple-element.46), channel_id=1, source_target_pairs={{0,6},{1,7},{2,4},{3,5},{4,2},{5,3},{6,0},{7,1},{8,14},{9,15},{10,... | collective-permute-start | bytes 98312 | tf_op jit(solution)/shard_map/ppermute | solution.py:410
  140.2 5.1 %collective-permute-done.6.got_ref = bf16[1,32,512]{2,1,0:T(8,128)(2,1)S(1)} collective-permute-done((bf16[1,32,512]{2,1,0:T(8,128)(2,1)S(1)}, bf16[1,32,512]{2,1,0:T(8,128)(2,1)S(1)}, u32[]{:S(2)}, u32[]{:S(2)}) %collective-permute-start.6) | collective-permute-done | bytes 32800 | tf_op jit(solution)/shard_map/ppermute | solution.py:410
  145.3 0.6 last.1
  145.9 2.5 %all-to-all-done.3.got_ref = bf16[64,8,256]{2,1,0:T(8,128)(2,1)S(1)} async-done(((bf16[64,8,256]{2,1,0:T(8,128)(2,1)}), bf16[64,8,256]{2,1,0:T(8,128)(2,1)S(1)}, u32[]{:S(2)}, u32[]{:S(2)}) %all-to-all-start.3) | async-done | bytes 262176 | tf_op jit(solution)/shard_map/all_to_all | solution.py:390
  148.5 0.8 final.1
  (19 shorter events, 0.3 us)
Async XLA Ops:
  0.6 71.2 %copy-start.3 = (bf16[256,512]{1,0:T(8,128)(2,1)S(1)}, bf16[256,512]{1,0:T(8,128)(2,1)}, u32[]{:S(2)}) copy-start(bf16[256,512]{1,0:T(8,128)(2,1)} %node_ref.1) | copy-start | bytes 786436
  0.6 42.2 %copy-start.7 = (s32[1024]{0:T(1024)S(1)}, s32[1024]{0:T(1024)}, u32[]{:S(2)}) copy-start(s32[1024]{0:T(1024)} %param.13) | copy-start | bytes 12292
  0.7 42.2 %copy-start.6 = (s32[1024]{0:T(1024)S(1)}, s32[1024]{0:T(1024)}, u32[]{:S(2)}) copy-start(s32[1024]{0:T(1024)} %param.15) | copy-start | bytes 12292
  0.7 71.2 %copy-start.5 = (bf16[128]{0:T(256)(128)(2,1)S(1)}, bf16[128]{0:T(256)(128)(2,1)}, u32[]{:S(2)}) copy-start(bf16[128]{0:T(256)(128)(2,1)} %param.12) | copy-start | bytes 772
  0.7 71.2 %copy-start.4 = (bf16[512,128]{1,0:T(8,128)(2,1)S(1)}, bf16[512,128]{1,0:T(8,128)(2,1)}, u32[]{:S(2)}) copy-start(bf16[512,128]{1,0:T(8,128)(2,1)} %ws_ref.1) | copy-start | bytes 393220
  36.6 35.3 %all-to-all-start.1 = ((bf16[64,8,512]{2,1,0:T(8,128)(2,1)}), bf16[64,8,512]{2,1,0:T(8,128)(2,1)S(1)}, u32[]{:S(2)}, u32[]{:S(2)}) async-start(bf16[64,8,512]{2,1,0:T(8,128)(2,1)} %bitcast.8), calls=%async_computation.1 | async-start | bytes 1048576 | tf_op jit(solution)/shard_map/all_to_all | solution.py:312
  81.5 22.6 %copy-start.2 = (bf16[1024,512]{1,0:T(8,128)(2,1)S(1)}, bf16[1024,512]{1,0:T(8,128)(2,1)}, u32[]{:S(2)}) copy-start(bf16[1024,512]{1,0:T(8,128)(2,1)} %get-tuple-element.28.bfirst_ref) | copy-start | bytes 3145732
  81.5 37.2 %all-to-all-start.2 = ((bf16[64,8,512]{2,1,0:T(8,128)(2,1)}), bf16[64,8,512]{2,1,0:T(8,128)(2,1)S(1)}, u32[]{:S(2)}, u32[]{:S(2)}) async-start(bf16[64,8,512]{2,1,0:T(8,128)(2,1)} %bitcast.22), calls=%async_computation.2 | async-start | bytes 1048576 | tf_op jit(solution)/shard_map/all_to_all | solution.py:341
  88.4 4.6 %collective-permute-start = (bf16[4,224,512]{2,1,0:T(8,128)(2,1)}, bf16[4,224,512]{2,1,0:T(8,128)(2,1)S(1)}, u32[]{:S(2)}, u32[]{:S(2)}) collective-permute-start(bf16[4,224,512]{2,1,0:T(8,128)(2,1)} %get-tuple-element.31), channel_id=1, source_target_pairs={{0,1},{1,0},{2,3},{3,2},{4,5},{5,4},{6,7},{7,6},{8,9},{9,8},{10,11... | collective-permute-start | bytes 2752520 | tf_op jit(solution)/shard_map/ppermute | solution.py:364
  93.0 1.5 copy-start
  94.6 13.4 %collective-permute-start.1 = (bf16[224,512]{1,0:T(8,128)(2,1)S(1)}, bf16[224,512]{1,0:T(8,128)(2,1)S(1)}, u32[]{:S(2)}, u32[]{:S(2)}) collective-permute-start(bf16[224,512]{1,0:T(8,128)(2,1)S(1)} %get-tuple-element.33), channel_id=1, source_target_pairs={{0,4},{1,5},{2,6},{3,7},{4,0},{5,1},{6,2},{7,3},{8,12},{9,13},{10,... | collective-permute-start | bytes 688136 | tf_op jit(solution)/shard_map/ppermute | solution.py:365
  97.9 10.4 %collective-permute-start.2 = (bf16[224,512]{1,0:T(8,128)(2,1)S(1)}, bf16[224,512]{1,0:T(8,128)(2,1)S(1)}, u32[]{:S(2)}, u32[]{:S(2)}) collective-permute-start(bf16[224,512]{1,0:T(8,128)(2,1)S(1)} %get-tuple-element.34), channel_id=1, source_target_pairs={{0,2},{1,3},{2,4},{3,5},{4,6},{5,7},{6,0},{7,1},{8,10},{9,11},{10,... | collective-permute-start | bytes 688136 | tf_op jit(solution)/shard_map/ppermute | solution.py:365
  101.9 10.2 %collective-permute-start.3 = (bf16[224,512]{1,0:T(8,128)(2,1)S(1)}, bf16[224,512]{1,0:T(8,128)(2,1)S(1)}, u32[]{:S(2)}, u32[]{:S(2)}) collective-permute-start(bf16[224,512]{1,0:T(8,128)(2,1)S(1)} %get-tuple-element.35), channel_id=1, source_target_pairs={{0,6},{1,7},{2,0},{3,1},{4,2},{5,3},{6,4},{7,5},{8,14},{9,15},{10,... | collective-permute-start | bytes 688136 | tf_op jit(solution)/shard_map/ppermute | solution.py:365
  104.1 1.4 copy-start.1
  119.0 29.5 %all-to-all-start.3 = ((bf16[64,8,256]{2,1,0:T(8,128)(2,1)}), bf16[64,8,256]{2,1,0:T(8,128)(2,1)S(1)}, u32[]{:S(2)}, u32[]{:S(2)}) async-start(bf16[64,8,256]{2,1,0:T(8,128)(2,1)} %bitcast.13), calls=%async_computation.3 | async-start | bytes 524288 | tf_op jit(solution)/shard_map/all_to_all | solution.py:390
  128.6 3.4 %collective-permute-start.4 = (f32[4,32,512]{2,1,0:T(8,128)S(1)}, f32[4,32,512]{2,1,0:T(8,128)S(1)}, u32[]{:S(2)}, u32[]{:S(2)}) collective-permute-start(f32[4,32,512]{2,1,0:T(8,128)S(1)} %get-tuple-element.42), channel_id=1, source_target_pairs={{0,1},{1,0},{2,3},{3,2},{4,5},{5,4},{6,7},{7,6},{8,9},{9,8},{10,11... | collective-permute-start | bytes 786440 | tf_op jit(solution)/shard_map/ppermute | solution.py:410
  132.1 6.2 %collective-permute-start.5 = (bf16[2,32,512]{2,1,0:T(8,128)(2,1)S(1)}, bf16[2,32,512]{2,1,0:T(8,128)(2,1)S(1)}, u32[]{:S(2)}, u32[]{:S(2)}) collective-permute-start(bf16[2,32,512]{2,1,0:T(8,128)(2,1)S(1)} %get-tuple-element.44), channel_id=1, source_target_pairs={{0,2},{1,3},{2,0},{3,1},{4,6},{5,7},{6,4},{7,5},{8,10},{9,11},{10,... | collective-permute-start | bytes 196616 | tf_op jit(solution)/shard_map/ppermute | solution.py:410
  138.3 7.0 %collective-permute-start.6 = (bf16[1,32,512]{2,1,0:T(8,128)(2,1)S(1)}, bf16[1,32,512]{2,1,0:T(8,128)(2,1)S(1)}, u32[]{:S(2)}, u32[]{:S(2)}) collective-permute-start(bf16[1,32,512]{2,1,0:T(8,128)(2,1)S(1)} %get-tuple-element.46), channel_id=1, source_target_pairs={{0,6},{1,7},{2,4},{3,5},{4,2},{5,3},{6,0},{7,1},{8,14},{9,15},{10,... | collective-permute-start | bytes 98312 | tf_op jit(solution)/shard_map/ppermute | solution.py:410

commit v8 on v7

--- a/solution.py
+++ b/solution.py
@@ -52,8 +52,8 @@
     return pl.CostEstimate(flops=flops, bytes_accessed=nbytes, transcendentals=0)
 
 
-def answer_kernel(asked_ref, node_any, out_ref, line_out, node_ref, sem):
-    fetch = pltpu.make_async_copy(node_any, node_ref, sem)
+def answer_kernel(asked_ref, node_any, out_any, line_out, node_ref, out_ref, sems):
+    fetch = pltpu.make_async_copy(node_any, node_ref, sems.at[0])
     fetch.start()
     parts, cap = asked_ref.shape
     own_count, slots = node_ref.shape[0], line_out.shape[1]
@@ -66,7 +66,15 @@
     line_out[...] = line
     pick = onehot(line, (own_count, slots), 0)
     fetch.wait()
-    out_ref[...] = dot(pick, node_ref[...], 0, 0).astype(BF)
+    half = slots // 2
+    stores = []
+    for h in range(2):
+        part = pl.ds(h * half, half)
+        out_ref[part] = dot(pick[:, h * half : (h + 1) * half], node_ref[...], 0, 0).astype(BF)
+        stores.append(pltpu.make_async_copy(out_ref.at[part], out_any.at[part], sems.at[1 + h]))
+        stores[-1].start()
+    for copy in stores:
+        copy.wait()
 
 
 def pair_kernel(
@@ -145,8 +153,7 @@
     chip = edge // 2
     core = edge % 2
     chips = n_edge // 2
-    extra = extra_ref[...]
-    extra_high, extra_low = halves(extra)
+    extra = paired(extra_ref[...])
     for j in range(chips):
         there = 2 * ((chip + j) % chips)
         part1 = pl.ds(pl.multiple_of((there + core) * rows1, 8), rows1)
@@ -158,7 +165,7 @@
         part2 = pl.ds(pl.multiple_of((there + 1 - core) * rows2, 8), rows2)
         sent_ref[j, :rows1] = grads[part1, :].astype(BF)
         sent_ref[j, rows1:rows] = grads2[part2, :].astype(BF)
-        sent_ref[j, rows:] = jnp.concatenate([extra_high, extra_low], axis=0)
+        sent_ref[j, rows:] = extra
         store(sent_ref.at[j], sent_out.at[j])
 
     total = None
@@ -211,6 +218,11 @@
     out_ref[...] = kept_ref[0] + got_ref[0].astype(F32)
 
 
+def paired(values):
+    high = values.astype(BF).astype(F32)
+    return jnp.concatenate([high, values - high], axis=0).astype(BF)
+
+
 def widen(packed, rows):
     values = packed.astype(F32)
     return jnp.concatenate([values[:rows], values[rows : rows + 8] + values[rows + 8 :]], axis=0)
@@ -219,9 +231,9 @@
 def chip_kernel(rows, kept_ref, got_ref, own_out, *packs):
     own_out[...] = kept_ref[0] + widen(got_ref[0], rows)
     for j, out in enumerate(packs):
-        high, low = halves(kept_ref[j + 1] + widen(got_ref[j + 1], rows))
-        out[: rows + 8] = high
-        out[rows + 8 :] = low[rows:]
+        total = kept_ref[j + 1] + widen(got_ref[j + 1], rows)
+        out[:rows] = total[:rows].astype(BF)
+        out[rows:] = paired(total[rows:])
 
 
 def total_kernel(parts, n_second, *refs):
@@ -300,12 +312,16 @@
     answer, asked_line = pl.pallas_call(
         answer_kernel,
         out_shape=(
-            jax.ShapeDtypeStruct((slots, width), BF),
+            pltpu.HBM((slots, width), BF),
             jax.ShapeDtypeStruct((1, slots), I32),
         ),
         in_specs=[WHOLE, FAR],
-        out_specs=(WHOLE, WHOLE),
-        scratch_shapes=[pltpu.VMEM((own_count, width), BF), pltpu.SemaphoreType.DMA],
+        out_specs=(FAR, WHOLE),
+        scratch_shapes=[
+            pltpu.VMEM((own_count, width), BF),
+            pltpu.VMEM((slots, width), BF),
+            pltpu.SemaphoreType.DMA((3,)),
+        ],
         compiler_params=params(8),
         name="answer",
     )(asked_here, in_hbm(node_rows))

time: 150 us -> 150 us (level)
  no operation moved by 1% of the time
where the time goes in v8:
time: 150 us; the launch traced here: 149 us
  waiting for transfers between devices  54.7 us (36%)
  starting transfers between devices  38.3 us (26%)
  blocking collectives  32.9 us (22%)
  Pallas kernels  17.1 us (11%)
  local copies, waits for them, and re-layouts  3.96 us (3%)
  between operations  1.52 us (1%)
    all_to_all x1, blocking collectives, body(): lax.all_to_all(requests, 'dom', split_axis=0, concat_axis=0, tiled=True)  32.9 us
    all_to_all x1, waiting for transfers between devices, body(): lax.all_to_all(answer.reshape(parts, cap, width), 'dom', split_axis=0, co...  29 us
    ppermute x3, waiting for transfers between devices, body(): got = lax.ppermute(sent, 'edge', partner)  10.8 us
    all_to_all x1, starting transfers between devices, body(): lax.all_to_all(packed.reshape(parts, share, lanes), 'dom', split_axis=0,...  9.63 us
    pallas_call x1, Pallas kernels, body(): pl.pallas_call(functools.partial(pair_kernel, scale, n_edge), out_shape=t...  9.61 us
    ppermute x3, starting transfers between devices, body(): lax.ppermute(packs[step - 1], 'edge', ahead(step))  9.41 us
    all_to_all x1, starting transfers between devices, body(): lax.all_to_all(slot_grad.reshape(parts, cap, width), 'dom', split_axis=0,...  6.9 us
    ppermute x3, starting transfers between devices, body(): got = lax.ppermute(sent, 'edge', partner)  5.76 us
  transfers between devices with their start and end apart: 10, of which 9 were waited for; matrix products, arithmetic and copies ran while one was open for 1% of the time, Pallas kernels for 3%

profile of v8, /device:TPU:6, one launch (start us, length us, event | category | flops | bytes accessed | tf_op | source)
XLA Modules:
  0.0 149.2 jit_solution(17391587555632827549)
XLA Ops:
  0.7 0.8 copy.20
  1.5 32.9 %all_to_all.26 = s32[64,1,8]{2,1,0:T(1,128)S(1)} all-to-all(s32[64,1,8]{2,1,0:T(1,128)S(1)} %bitcast.24), channel_id=1, replica_groups=mesh['dom'=64,'edge'=8] {'dom'}, dimensions={0} | all-to-all | bytes 4096 | tf_op jit(solution)/shard_map/all_to_all | solution.py:311
  34.5 2.0 %answer.1 = (bf16[512,512]{1,0:T(8,128)(2,1)}, s32[1,512]{1,0:T(1,128)S(1)}) custom-call(s32[64,8]{1,0:T(8,128)S(1)} %bitcast.20, bf16[256,512]{1,0:T(8,128)(2,1)} %node_ref.1), custom_call_target="tpu_custom_call" | custom-call | tf_op jit(solution)/shard_map/answer/pallas_call | solution.py:312
  36.5 4.6 %all-to-all-start.1 = ((bf16[64,8,512]{2,1,0:T(8,128)(2,1)}), bf16[64,8,512]{2,1,0:T(8,128)(2,1)S(1)}, u32[]{:S(2)}, u32[]{:S(2)}) async-start(bf16[64,8,512]{2,1,0:T(8,128)(2,1)} %bitcast.23), calls=%async_computation.1 | async-start | bytes 1048576 | tf_op jit(solution)/shard_map/all_to_all | solution.py:328
  41.8 0.7 pad_add_fusion
  42.6 0.2 copy.22.cols_ref
  42.8 29.0 %all-to-all-done.1 = bf16[64,8,512]{2,1,0:T(8,128)(2,1)S(1)} async-done(((bf16[64,8,512]{2,1,0:T(8,128)(2,1)}), bf16[64,8,512]{2,1,0:T(8,128)(2,1)S(1)}, u32[]{:S(2)}, u32[]{:S(2)}) %all-to-all-start.1) | async-done | bytes 524320 | tf_op jit(solution)/shard_map/all_to_all | solution.py:328
  71.8 9.6 %pair.1 = (bf16[512,512]{1,0:T(8,128)(2,1)}, bf16[1024,512]{1,0:T(8,128)(2,1)}, f32[4,216,512]{2,1,0:T(8,128)}, bf16[4,224,512]{2,1,0:T(8,128)(2,1)}) custom-call(s32[1]{0:T(128)S(6)} %copy.24.live_ref, s32[1]{0:T(128)} %bitcast.edge_ref, s32[1024,3]{1,0:T(8,128)S(1)} %copy.22.cols_ref, s32[2,1024]{1,0:T(2,128)S(1)} %pad_add_fusion.1.lines_ref, ...), custom_call_target="tpu_custom_call" | custom-call | flops 6000000000 | bytes 8388608 | tf_op jit(solution)/shard_map/pair/pallas_call | solution.py:333
  81.4 6.9 %all-to-all-start.2 = ((bf16[64,8,512]{2,1,0:T(8,128)(2,1)}), bf16[64,8,512]{2,1,0:T(8,128)(2,1)S(1)}, u32[]{:S(2)}, u32[]{:S(2)}) async-start(bf16[64,8,512]{2,1,0:T(8,128)(2,1)} %bitcast.22), calls=%async_computation.2 | async-start | bytes 1048576 | tf_op jit(solution)/shard_map/all_to_all | solution.py:357
  88.3 1.9 %collective-permute-start = (bf16[4,224,512]{2,1,0:T(8,128)(2,1)}, bf16[4,224,512]{2,1,0:T(8,128)(2,1)S(1)}, u32[]{:S(2)}, u32[]{:S(2)}) collective-permute-start(bf16[4,224,512]{2,1,0:T(8,128)(2,1)} %get-tuple-element.31), channel_id=1, source_target_pairs={{0,1},{1,0},{2,3},{3,2},{4,5},{5,4},{6,7},{7,6},{8,9},{9,8},{10,11... | collective-permute-start | bytes 2752520 | tf_op jit(solution)/shard_map/ppermute | solution.py:380
  90.3 2.6 %collective-permute-done.got_ref = bf16[4,224,512]{2,1,0:T(8,128)(2,1)S(1)} collective-permute-done((bf16[4,224,512]{2,1,0:T(8,128)(2,1)}, bf16[4,224,512]{2,1,0:T(8,128)(2,1)S(1)}, u32[]{:S(2)}, u32[]{:S(2)}) %collective-permute-start) | collective-permute-done | bytes 917536 | tf_op jit(solution)/shard_map/ppermute | solution.py:380
  92.9 1.5 copy-done
  94.6 3.3 %collective-permute-start.1 = (bf16[224,512]{1,0:T(8,128)(2,1)S(1)}, bf16[224,512]{1,0:T(8,128)(2,1)S(1)}, u32[]{:S(2)}, u32[]{:S(2)}) collective-permute-start(bf16[224,512]{1,0:T(8,128)(2,1)S(1)} %get-tuple-element.33), channel_id=1, source_target_pairs={{0,4},{1,5},{2,6},{3,7},{4,0},{5,1},{6,2},{7,3},{8,12},{9,13},{10,... | collective-permute-start | bytes 688136 | tf_op jit(solution)/shard_map/ppermute | solution.py:381
  97.9 4.0 %collective-permute-start.2 = (bf16[224,512]{1,0:T(8,128)(2,1)S(1)}, bf16[224,512]{1,0:T(8,128)(2,1)S(1)}, u32[]{:S(2)}, u32[]{:S(2)}) collective-permute-start(bf16[224,512]{1,0:T(8,128)(2,1)S(1)} %get-tuple-element.34), channel_id=1, source_target_pairs={{0,2},{1,3},{2,4},{3,5},{4,6},{5,7},{6,0},{7,1},{8,10},{9,11},{10,... | collective-permute-start | bytes 688136 | tf_op jit(solution)/shard_map/ppermute | solution.py:381
  101.9 2.1 %collective-permute-start.3 = (bf16[224,512]{1,0:T(8,128)(2,1)S(1)}, bf16[224,512]{1,0:T(8,128)(2,1)S(1)}, u32[]{:S(2)}, u32[]{:S(2)}) collective-permute-start(bf16[224,512]{1,0:T(8,128)(2,1)S(1)} %get-tuple-element.35), channel_id=1, source_target_pairs={{0,6},{1,7},{2,0},{3,1},{4,2},{5,3},{6,4},{7,5},{8,14},{9,15},{10,... | collective-permute-start | bytes 688136 | tf_op jit(solution)/shard_map/ppermute | solution.py:381
  104.0 1.4 copy-done.1
  105.4 2.5 %near.1.refs_4_.near_ref = f32[256,512]{1,0:T(8,128)S(1)} custom-call(s32[2,1024]{1,0:T(2,128)S(1)} %pad_add_fusion.1.lines_ref, s32[1024,3]{1,0:T(8,128)S(1)} %copy.22.cols_ref, bf16[512,512]{1,0:T(8,128)(2,1)S(1)} %bitcast.19, bf16[1024,512]{1,0:T(8,128)(2,1)S(1)} %copy-done.2, bf16[1536,512]{1,0:T(8,128)(2,1)S(1)} %copy-done.1), custom_call_target="tpu_custom_call" | custom-call | tf_op jit(solution)/shard_map/near/pallas_call | solution.py:361
  107.9 0.4 collective-permute-done.2.refs_2_
  108.3 3.8 %collective-permute-done.3.refs_3_ = bf16[224,512]{1,0:T(8,128)(2,1)S(1)} collective-permute-done((bf16[224,512]{1,0:T(8,128)(2,1)S(1)}, bf16[224,512]{1,0:T(8,128)(2,1)S(1)}, u32[]{:S(2)}, u32[]{:S(2)}) %collective-permute-start.3) | collective-permute-done | bytes 229408 | tf_op jit(solution)/shard_map/ppermute | solution.py:381
  112.1 1.0 total.1.packed_ref
  113.1 5.5 %all-to-all-done.2 = bf16[64,8,512]{2,1,0:T(8,128)(2,1)S(1)} async-done(((bf16[64,8,512]{2,1,0:T(8,128)(2,1)}), bf16[64,8,512]{2,1,0:T(8,128)(2,1)S(1)}, u32[]{:S(2)}, u32[]{:S(2)}) %all-to-all-start.2) | async-done | bytes 524320 | tf_op jit(solution)/shard_map/all_to_all | solution.py:357
  118.6 0.3 owned.1
  119.0 9.6 %all-to-all-start.3 = ((bf16[64,8,256]{2,1,0:T(8,128)(2,1)}), bf16[64,8,256]{2,1,0:T(8,128)(2,1)S(1)}, u32[]{:S(2)}, u32[]{:S(2)}) async-start(bf16[64,8,256]{2,1,0:T(8,128)(2,1)} %bitcast.13), calls=%async_computation.3 | async-start | bytes 524288 | tf_op jit(solution)/shard_map/all_to_all | solution.py:406
  128.6 1.9 %collective-permute-start.4 = (f32[4,32,512]{2,1,0:T(8,128)S(1)}, f32[4,32,512]{2,1,0:T(8,128)S(1)}, u32[]{:S(2)}, u32[]{:S(2)}) collective-permute-start(f32[4,32,512]{2,1,0:T(8,128)S(1)} %get-tuple-element.42), channel_id=1, source_target_pairs={{0,1},{1,0},{2,3},{3,2},{4,5},{5,4},{6,7},{7,6},{8,9},{9,8},{10,11... | collective-permute-start | bytes 786440 | tf_op jit(solution)/shard_map/ppermute | solution.py:426
  130.5 1.5 %collective-permute-done.4.got_ref = f32[4,32,512]{2,1,0:T(8,128)S(1)} collective-permute-done((f32[4,32,512]{2,1,0:T(8,128)S(1)}, f32[4,32,512]{2,1,0:T(8,128)S(1)}, u32[]{:S(2)}, u32[]{:S(2)}) %collective-permute-start.4) | collective-permute-done | bytes 262176 | tf_op jit(solution)/shard_map/ppermute | solution.py:426
  132.1 1.9 %collective-permute-start.5 = (bf16[2,32,512]{2,1,0:T(8,128)(2,1)S(1)}, bf16[2,32,512]{2,1,0:T(8,128)(2,1)S(1)}, u32[]{:S(2)}, u32[]{:S(2)}) collective-permute-start(bf16[2,32,512]{2,1,0:T(8,128)(2,1)S(1)} %get-tuple-element.44), channel_id=1, source_target_pairs={{0,2},{1,3},{2,0},{3,1},{4,6},{5,7},{6,4},{7,5},{8,10},{9,11},{10,... | collective-permute-start | bytes 196616 | tf_op jit(solution)/shard_map/ppermute | solution.py:426
  134.0 4.2 %collective-permute-done.5.got_ref = bf16[2,32,512]{2,1,0:T(8,128)(2,1)S(1)} collective-permute-done((bf16[2,32,512]{2,1,0:T(8,128)(2,1)S(1)}, bf16[2,32,512]{2,1,0:T(8,128)(2,1)S(1)}, u32[]{:S(2)}, u32[]{:S(2)}) %collective-permute-start.5) | collective-permute-done | bytes 65568 | tf_op jit(solution)/shard_map/ppermute | solution.py:426
  138.2 1.9 %collective-permute-start.6 = (bf16[1,32,512]{2,1,0:T(8,128)(2,1)S(1)}, bf16[1,32,512]{2,1,0:T(8,128)(2,1)S(1)}, u32[]{:S(2)}, u32[]{:S(2)}) collective-permute-start(bf16[1,32,512]{2,1,0:T(8,128)(2,1)S(1)} %get-tuple-element.46), channel_id=1, source_target_pairs={{0,6},{1,7},{2,4},{3,5},{4,2},{5,3},{6,0},{7,1},{8,14},{9,15},{10,... | collective-permute-start | bytes 98312 | tf_op jit(solution)/shard_map/ppermute | solution.py:426
  140.2 5.1 %collective-permute-done.6.got_ref = bf16[1,32,512]{2,1,0:T(8,128)(2,1)S(1)} collective-permute-done((bf16[1,32,512]{2,1,0:T(8,128)(2,1)S(1)}, bf16[1,32,512]{2,1,0:T(8,128)(2,1)S(1)}, u32[]{:S(2)}, u32[]{:S(2)}) %collective-permute-start.6) | collective-permute-done | bytes 32800 | tf_op jit(solution)/shard_map/ppermute | solution.py:426
  145.3 0.6 last.1
  145.9 2.5 %all-to-all-done.3.got_ref = bf16[64,8,256]{2,1,0:T(8,128)(2,1)S(1)} async-done(((bf16[64,8,256]{2,1,0:T(8,128)(2,1)}), bf16[64,8,256]{2,1,0:T(8,128)(2,1)S(1)}, u32[]{:S(2)}, u32[]{:S(2)}) %all-to-all-start.3) | async-done | bytes 262176 | tf_op jit(solution)/shard_map/all_to_all | solution.py:406
  148.4 0.8 final.1
  (19 shorter events, 0.3 us)
Async XLA Ops:
  0.6 71.2 %copy-start.3 = (bf16[256,512]{1,0:T(8,128)(2,1)S(1)}, bf16[256,512]{1,0:T(8,128)(2,1)}, u32[]{:S(2)}) copy-start(bf16[256,512]{1,0:T(8,128)(2,1)} %node_ref.1) | copy-start | bytes 786436
  0.6 42.1 %copy-start.7 = (s32[1024]{0:T(1024)S(1)}, s32[1024]{0:T(1024)}, u32[]{:S(2)}) copy-start(s32[1024]{0:T(1024)} %param.13) | copy-start | bytes 12292
  0.7 42.1 %copy-start.6 = (s32[1024]{0:T(1024)S(1)}, s32[1024]{0:T(1024)}, u32[]{:S(2)}) copy-start(s32[1024]{0:T(1024)} %param.15) | copy-start | bytes 12292
  0.7 71.1 %copy-start.5 = (bf16[128]{0:T(256)(128)(2,1)S(1)}, bf16[128]{0:T(256)(128)(2,1)}, u32[]{:S(2)}) copy-start(bf16[128]{0:T(256)(128)(2,1)} %param.12) | copy-start | bytes 772
  0.7 71.1 %copy-start.4 = (bf16[512,128]{1,0:T(8,128)(2,1)S(1)}, bf16[512,128]{1,0:T(8,128)(2,1)}, u32[]{:S(2)}) copy-start(bf16[512,128]{1,0:T(8,128)(2,1)} %ws_ref.1) | copy-start | bytes 393220
  36.5 35.3 %all-to-all-start.1 = ((bf16[64,8,512]{2,1,0:T(8,128)(2,1)}), bf16[64,8,512]{2,1,0:T(8,128)(2,1)S(1)}, u32[]{:S(2)}, u32[]{:S(2)}) async-start(bf16[64,8,512]{2,1,0:T(8,128)(2,1)} %bitcast.23), calls=%async_computation.1 | async-start | bytes 1048576 | tf_op jit(solution)/shard_map/all_to_all | solution.py:328
  81.4 22.6 %copy-start.2 = (bf16[1024,512]{1,0:T(8,128)(2,1)S(1)}, bf16[1024,512]{1,0:T(8,128)(2,1)}, u32[]{:S(2)}) copy-start(bf16[1024,512]{1,0:T(8,128)(2,1)} %get-tuple-element.28.bfirst_ref) | copy-start | bytes 3145732
  81.4 37.2 %all-to-all-start.2 = ((bf16[64,8,512]{2,1,0:T(8,128)(2,1)}), bf16[64,8,512]{2,1,0:T(8,128)(2,1)S(1)}, u32[]{:S(2)}, u32[]{:S(2)}) async-start(bf16[64,8,512]{2,1,0:T(8,128)(2,1)} %bitcast.22), calls=%async_computation.2 | async-start | bytes 1048576 | tf_op jit(solution)/shard_map/all_to_all | solution.py:357
  88.3 4.6 %collective-permute-start = (bf16[4,224,512]{2,1,0:T(8,128)(2,1)}, bf16[4,224,512]{2,1,0:T(8,128)(2,1)S(1)}, u32[]{:S(2)}, u32[]{:S(2)}) collective-permute-start(bf16[4,224,512]{2,1,0:T(8,128)(2,1)} %get-tuple-element.31), channel_id=1, source_target_pairs={{0,1},{1,0},{2,3},{3,2},{4,5},{5,4},{6,7},{7,6},{8,9},{9,8},{10,11... | collective-permute-start | bytes 2752520 | tf_op jit(solution)/shard_map/ppermute | solution.py:380
  92.9 1.5 copy-start
  94.6 13.4 %collective-permute-start.1 = (bf16[224,512]{1,0:T(8,128)(2,1)S(1)}, bf16[224,512]{1,0:T(8,128)(2,1)S(1)}, u32[]{:S(2)}, u32[]{:S(2)}) collective-permute-start(bf16[224,512]{1,0:T(8,128)(2,1)S(1)} %get-tuple-element.33), channel_id=1, source_target_pairs={{0,4},{1,5},{2,6},{3,7},{4,0},{5,1},{6,2},{7,3},{8,12},{9,13},{10,... | collective-permute-start | bytes 688136 | tf_op jit(solution)/shard_map/ppermute | solution.py:381
  97.9 10.4 %collective-permute-start.2 = (bf16[224,512]{1,0:T(8,128)(2,1)S(1)}, bf16[224,512]{1,0:T(8,128)(2,1)S(1)}, u32[]{:S(2)}, u32[]{:S(2)}) collective-permute-start(bf16[224,512]{1,0:T(8,128)(2,1)S(1)} %get-tuple-element.34), channel_id=1, source_target_pairs={{0,2},{1,3},{2,4},{3,5},{4,6},{5,7},{6,0},{7,1},{8,10},{9,11},{10,... | collective-permute-start | bytes 688136 | tf_op jit(solution)/shard_map/ppermute | solution.py:381
  101.9 10.2 %collective-permute-start.3 = (bf16[224,512]{1,0:T(8,128)(2,1)S(1)}, bf16[224,512]{1,0:T(8,128)(2,1)S(1)}, u32[]{:S(2)}, u32[]{:S(2)}) collective-permute-start(bf16[224,512]{1,0:T(8,128)(2,1)S(1)} %get-tuple-element.35), channel_id=1, source_target_pairs={{0,6},{1,7},{2,0},{3,1},{4,2},{5,3},{6,4},{7,5},{8,14},{9,15},{10,... | collective-permute-start | bytes 688136 | tf_op jit(solution)/shard_map/ppermute | solution.py:381
  104.0 1.4 copy-start.1
  119.0 29.5 %all-to-all-start.3 = ((bf16[64,8,256]{2,1,0:T(8,128)(2,1)}), bf16[64,8,256]{2,1,0:T(8,128)(2,1)S(1)}, u32[]{:S(2)}, u32[]{:S(2)}) async-start(bf16[64,8,256]{2,1,0:T(8,128)(2,1)} %bitcast.13), calls=%async_computation.3 | async-start | bytes 524288 | tf_op jit(solution)/shard_map/all_to_all | solution.py:406
  128.6 3.4 %collective-permute-start.4 = (f32[4,32,512]{2,1,0:T(8,128)S(1)}, f32[4,32,512]{2,1,0:T(8,128)S(1)}, u32[]{:S(2)}, u32[]{:S(2)}) collective-permute-start(f32[4,32,512]{2,1,0:T(8,128)S(1)} %get-tuple-element.42), channel_id=1, source_target_pairs={{0,1},{1,0},{2,3},{3,2},{4,5},{5,4},{6,7},{7,6},{8,9},{9,8},{10,11... | collective-permute-start | bytes 786440 | tf_op jit(solution)/shard_map/ppermute | solution.py:426
  132.1 6.2 %collective-permute-start.5 = (bf16[2,32,512]{2,1,0:T(8,128)(2,1)S(1)}, bf16[2,32,512]{2,1,0:T(8,128)(2,1)S(1)}, u32[]{:S(2)}, u32[]{:S(2)}) collective-permute-start(bf16[2,32,512]{2,1,0:T(8,128)(2,1)S(1)} %get-tuple-element.44), channel_id=1, source_target_pairs={{0,2},{1,3},{2,0},{3,1},{4,6},{5,7},{6,4},{7,5},{8,10},{9,11},{10,... | collective-permute-start | bytes 196616 | tf_op jit(solution)/shard_map/ppermute | solution.py:426
  138.2 7.0 %collective-permute-start.6 = (bf16[1,32,512]{2,1,0:T(8,128)(2,1)S(1)}, bf16[1,32,512]{2,1,0:T(8,128)(2,1)S(1)}, u32[]{:S(2)}, u32[]{:S(2)}) collective-permute-start(bf16[1,32,512]{2,1,0:T(8,128)(2,1)S(1)} %get-tuple-element.46), channel_id=1, source_target_pairs={{0,6},{1,7},{2,4},{3,5},{4,2},{5,3},{6,0},{7,1},{8,14},{9,15},{10,... | collective-permute-start | bytes 98312 | tf_op jit(solution)/shard_map/ppermute | solution.py:426

commit v9 on v8

--- a/solution.py
+++ b/solution.py
@@ -78,7 +78,7 @@
 
 
 def pair_kernel(
-    scale, n_edge, live_ref, edge_ref, cols_ref, lines_ref, node_ref, rep_ref, wf_any, ws_ref, wt_ref,
+    n_edge, live_ref, edge_ref, cols_ref, lines_ref, node_ref, rep_ref, wf_any, ws_ref, wt_ref,
     slot_out, bfirst_out, kept_out, sent_out,
     wf_ref, slot_ref, first_ref, bfirst_ref, bsecond_ref, grads, grads2, extra_ref, sent_ref,
     feat_ref, fetch_sems, store_sems,
@@ -139,16 +139,16 @@
         term = jnp.sum(slope * second, axis=0, keepdims=True)
         third = term if third is None else third + term
     extra_ref[...] = jnp.zeros_like(extra_ref)
-    extra_ref[0:1, :hidden2] = scale * third
-    extra_ref[1:2, :hidden2] = scale * loss
+    extra_ref[0:1, :hidden2] = third
+    extra_ref[1:2, :hidden2] = loss
 
     rows1 = 3 * width // n_edge
     rows2 = hidden2 // n_edge
     rows = rows1 + rows2
     bfirst = bfirst_ref[...]
-    grads2[...] = scale * dot(bsecond_ref[...], first_ref[...], 0, 0)
+    grads2[...] = dot(bsecond_ref[...], first_ref[...], 0, 0)
     for i in range(3):
-        grads[i * width : (i + 1) * width] = scale * dot(feat_ref[i], bfirst, 0, 0)
+        grads[i * width : (i + 1) * width] = dot(feat_ref[i], bfirst, 0, 0)
     edge = edge_ref[0]
     chip = edge // 2
     core = edge % 2
@@ -202,10 +202,10 @@
     total[...] = near_ref[...] + dot(place, back_ref[...])
     edge = edge_ref[0]
     for j in range(n_edge // 2):
-        mask = ring_mask(j)
-        owner = edge ^ (2 * mask)
-        for out, who in ((kept_out, owner), (sent_out, owner ^ 1)):
-            out[j] = total[pl.ds(pl.multiple_of(who * rows, 8), rows), :]
+        owner = edge ^ (2 * ring_mask(j))
+        kept_out[j] = total[pl.ds(pl.multiple_of(owner * rows, 8), rows), :]
+        part = pl.ds(pl.multiple_of((owner ^ 1) * rows, 8), rows)
+        sent_out[j] = total[part, :].astype(BF)
 
 
 def add_kernel(kept_ref, got_ref, kept_out, sent_out):
@@ -264,8 +264,8 @@
     out_ref[...] = turned.astype(BF)
 
 
-def final_kernel(rows1, rows2, got_ref, first_out, second_out, third_out, loss_out):
-    total = jnp.sum(got_ref[...].astype(F32), axis=0)
+def final_kernel(scale, rows1, rows2, got_ref, first_out, second_out, third_out, loss_out):
+    total = scale * jnp.sum(got_ref[...].astype(F32), axis=0)
     share, lanes = total.shape
     rows = rows1 + rows2
     n_second = third_out.shape[1]
@@ -331,7 +331,7 @@
 
     outs = [(slots, width), (edges, hidden), (chips, rows + 8, hidden), (chips, rows + 16, hidden)]
     slot_grad, back_first, kept, sent = pl.pallas_call(
-        functools.partial(pair_kernel, scale, n_edge),
+        functools.partial(pair_kernel, n_edge),
         out_shape=tuple(pltpu.HBM(shape, dtype) for shape, dtype in zip(outs, (BF, BF, F32, BF))),
         in_specs=[SCALARS] * 2 + [WHOLE] * 4 + [FAR] + [WHOLE] * 2,
         out_specs=(FAR,) * 4,
@@ -394,7 +394,11 @@
     block = jax.ShapeDtypeStruct((chips, own_count // n_edge, width), F32)
     kept, sent, packed = pl.pallas_call(
         functools.partial(owned_kernel, n_edge),
-        out_shape=(block, block, jax.ShapeDtypeStruct(packed.shape, BF)),
+        out_shape=(
+            block,
+            jax.ShapeDtypeStruct(block.shape, BF),
+            jax.ShapeDtypeStruct(packed.shape, BF),
+        ),
         in_specs=[SCALARS] + [WHOLE] * 3 + [ANYWHERE],
         out_specs=(WHOLE, WHOLE, ANYWHERE),
         input_output_aliases={4: 2},
@@ -407,7 +411,7 @@
         packed.reshape(parts, share, lanes), "dom", split_axis=0, concat_axis=0, tiled=True
     )
     first_t, second_share, third_total, loss_total = pl.pallas_call(
-        functools.partial(final_kernel, rows1, rows2),
+        functools.partial(final_kernel, scale, rows1, rows2),
         out_shape=(
             jax.ShapeDtypeStruct((share, rows1), F32),
             jax.ShapeDtypeStruct((share, rows2), F32),

time: 150 us -> 150 us (level)
  no operation moved by 1% of the time
where the time goes in v9:
time: 150 us; the launch traced here: 149 us
  waiting for transfers between devices  54.7 us (36%)
  starting transfers between devices  38.3 us (26%)
  blocking collectives  32.9 us (22%)
  Pallas kernels  17.1 us (11%)
  local copies, waits for them, and re-layouts  3.96 us (3%)
  between operations  1.52 us (1%)
    all_to_all x1, blocking collectives, body(): lax.all_to_all(requests, 'dom', split_axis=0, concat_axis=0, tiled=True)  32.9 us
    all_to_all x1, waiting for transfers between devices, body(): lax.all_to_all(answer.reshape(parts, cap, width), 'dom', split_axis=0, co...  29 us
    ppermute x3, waiting for transfers between devices, body(): got = lax.ppermute(sent, 'edge', partner)  10.6 us
    all_to_all x1, starting transfers between devices, body(): lax.all_to_all(packed.reshape(parts, share, lanes), 'dom', split_axis=0,...  9.63 us
    pallas_call x1, Pallas kernels, body(): pl.pallas_call(functools.partial(pair_kernel, n_edge), out_shape=tuple((p...  9.6 us
    ppermute x3, starting transfers between devices, body(): lax.ppermute(packs[step - 1], 'edge', ahead(step))  9.41 us
    all_to_all x1, starting transfers between devices, body(): lax.all_to_all(slot_grad.reshape(parts, cap, width), 'dom', split_axis=0,...  6.9 us
    ppermute x3, starting transfers between devices, body(): got = lax.ppermute(sent, 'edge', partner)  5.76 us
  transfers between devices with their start and end apart: 10, of which 9 were waited for; matrix products, arithmetic and copies ran while one was open for 1% of the time, Pallas kernels for 3%

profile of v9, /device:TPU:6, one launch (start us, length us, event | category | flops | bytes accessed | tf_op | source)
XLA Modules:
  0.0 149.2 jit_solution(13542491968814007870)
XLA Ops:
  0.7 0.8 copy.20
  1.5 32.9 %all_to_all.26 = s32[64,1,8]{2,1,0:T(1,128)S(1)} all-to-all(s32[64,1,8]{2,1,0:T(1,128)S(1)} %bitcast.24), channel_id=1, replica_groups=mesh['dom'=64,'edge'=8] {'dom'}, dimensions={0} | all-to-all | bytes 4096 | tf_op jit(solution)/shard_map/all_to_all | solution.py:311
  34.5 2.0 %answer.1 = (bf16[512,512]{1,0:T(8,128)(2,1)}, s32[1,512]{1,0:T(1,128)S(1)}) custom-call(s32[64,8]{1,0:T(8,128)S(1)} %bitcast.20, bf16[256,512]{1,0:T(8,128)(2,1)} %node_ref.1), custom_call_target="tpu_custom_call" | custom-call | tf_op jit(solution)/shard_map/answer/pallas_call | solution.py:312
  36.5 4.6 %all-to-all-start.1 = ((bf16[64,8,512]{2,1,0:T(8,128)(2,1)}), bf16[64,8,512]{2,1,0:T(8,128)(2,1)S(1)}, u32[]{:S(2)}, u32[]{:S(2)}) async-start(bf16[64,8,512]{2,1,0:T(8,128)(2,1)} %bitcast.23), calls=%async_computation.1 | async-start | bytes 1048576 | tf_op jit(solution)/shard_map/all_to_all | solution.py:328
  41.8 0.7 pad_add_fusion
  42.6 0.2 copy.22.cols_ref
  42.8 29.0 %all-to-all-done.1 = bf16[64,8,512]{2,1,0:T(8,128)(2,1)S(1)} async-done(((bf16[64,8,512]{2,1,0:T(8,128)(2,1)}), bf16[64,8,512]{2,1,0:T(8,128)(2,1)S(1)}, u32[]{:S(2)}, u32[]{:S(2)}) %all-to-all-start.1) | async-done | bytes 524320 | tf_op jit(solution)/shard_map/all_to_all | solution.py:328
  71.8 9.6 %pair.1 = (bf16[512,512]{1,0:T(8,128)(2,1)}, bf16[1024,512]{1,0:T(8,128)(2,1)}, f32[4,216,512]{2,1,0:T(8,128)}, bf16[4,224,512]{2,1,0:T(8,128)(2,1)}) custom-call(s32[1]{0:T(128)S(6)} %copy.24.live_ref, s32[1]{0:T(128)} %bitcast.edge_ref, s32[1024,3]{1,0:T(8,128)S(1)} %copy.22.cols_ref, s32[2,1024]{1,0:T(2,128)S(1)} %pad_add_fusion.1.lines_ref, ...), custom_call_target="tpu_custom_call" | custom-call | flops 6000000000 | bytes 8388608 | tf_op jit(solution)/shard_map/pair/pallas_call | solution.py:333
  81.4 6.9 %all-to-all-start.2 = ((bf16[64,8,512]{2,1,0:T(8,128)(2,1)}), bf16[64,8,512]{2,1,0:T(8,128)(2,1)S(1)}, u32[]{:S(2)}, u32[]{:S(2)}) async-start(bf16[64,8,512]{2,1,0:T(8,128)(2,1)} %bitcast.22), calls=%async_computation.2 | async-start | bytes 1048576 | tf_op jit(solution)/shard_map/all_to_all | solution.py:357
  88.3 1.9 %collective-permute-start = (bf16[4,224,512]{2,1,0:T(8,128)(2,1)}, bf16[4,224,512]{2,1,0:T(8,128)(2,1)S(1)}, u32[]{:S(2)}, u32[]{:S(2)}) collective-permute-start(bf16[4,224,512]{2,1,0:T(8,128)(2,1)} %get-tuple-element.31), channel_id=1, source_target_pairs={{0,1},{1,0},{2,3},{3,2},{4,5},{5,4},{6,7},{7,6},{8,9},{9,8},{10,11... | collective-permute-start | bytes 2752520 | tf_op jit(solution)/shard_map/ppermute | solution.py:380
  90.3 2.6 %collective-permute-done.got_ref = bf16[4,224,512]{2,1,0:T(8,128)(2,1)S(1)} collective-permute-done((bf16[4,224,512]{2,1,0:T(8,128)(2,1)}, bf16[4,224,512]{2,1,0:T(8,128)(2,1)S(1)}, u32[]{:S(2)}, u32[]{:S(2)}) %collective-permute-start) | collective-permute-done | bytes 917536 | tf_op jit(solution)/shard_map/ppermute | solution.py:380
  92.9 1.5 copy-done
  94.6 3.3 %collective-permute-start.1 = (bf16[224,512]{1,0:T(8,128)(2,1)S(1)}, bf16[224,512]{1,0:T(8,128)(2,1)S(1)}, u32[]{:S(2)}, u32[]{:S(2)}) collective-permute-start(bf16[224,512]{1,0:T(8,128)(2,1)S(1)} %get-tuple-element.33), channel_id=1, source_target_pairs={{0,4},{1,5},{2,6},{3,7},{4,0},{5,1},{6,2},{7,3},{8,12},{9,13},{10,... | collective-permute-start | bytes 688136 | tf_op jit(solution)/shard_map/ppermute | solution.py:381
  97.9 4.0 %collective-permute-start.2 = (bf16[224,512]{1,0:T(8,128)(2,1)S(1)}, bf16[224,512]{1,0:T(8,128)(2,1)S(1)}, u32[]{:S(2)}, u32[]{:S(2)}) collective-permute-start(bf16[224,512]{1,0:T(8,128)(2,1)S(1)} %get-tuple-element.34), channel_id=1, source_target_pairs={{0,2},{1,3},{2,4},{3,5},{4,6},{5,7},{6,0},{7,1},{8,10},{9,11},{10,... | collective-permute-start | bytes 688136 | tf_op jit(solution)/shard_map/ppermute | solution.py:381
  101.9 2.1 %collective-permute-start.3 = (bf16[224,512]{1,0:T(8,128)(2,1)S(1)}, bf16[224,512]{1,0:T(8,128)(2,1)S(1)}, u32[]{:S(2)}, u32[]{:S(2)}) collective-permute-start(bf16[224,512]{1,0:T(8,128)(2,1)S(1)} %get-tuple-element.35), channel_id=1, source_target_pairs={{0,6},{1,7},{2,0},{3,1},{4,2},{5,3},{6,4},{7,5},{8,14},{9,15},{10,... | collective-permute-start | bytes 688136 | tf_op jit(solution)/shard_map/ppermute | solution.py:381
  104.0 1.4 copy-done.1
  105.4 2.5 %near.1.refs_4_.near_ref = f32[256,512]{1,0:T(8,128)S(1)} custom-call(s32[2,1024]{1,0:T(2,128)S(1)} %pad_add_fusion.1.lines_ref, s32[1024,3]{1,0:T(8,128)S(1)} %copy.22.cols_ref, bf16[512,512]{1,0:T(8,128)(2,1)S(1)} %bitcast.19, bf16[1024,512]{1,0:T(8,128)(2,1)S(1)} %copy-done.2, bf16[1536,512]{1,0:T(8,128)(2,1)S(1)} %copy-done.1), custom_call_target="tpu_custom_call" | custom-call | tf_op jit(solution)/shard_map/near/pallas_call | solution.py:361
  107.9 0.4 collective-permute-done.2.refs_2_
  108.3 3.8 %collective-permute-done.3.refs_3_ = bf16[224,512]{1,0:T(8,128)(2,1)S(1)} collective-permute-done((bf16[224,512]{1,0:T(8,128)(2,1)S(1)}, bf16[224,512]{1,0:T(8,128)(2,1)S(1)}, u32[]{:S(2)}, u32[]{:S(2)}) %collective-permute-start.3) | collective-permute-done | bytes 229408 | tf_op jit(solution)/shard_map/ppermute | solution.py:381
  112.1 1.0 total.1.packed_ref
  113.1 5.5 %all-to-all-done.2 = bf16[64,8,512]{2,1,0:T(8,128)(2,1)S(1)} async-done(((bf16[64,8,512]{2,1,0:T(8,128)(2,1)}), bf16[64,8,512]{2,1,0:T(8,128)(2,1)S(1)}, u32[]{:S(2)}, u32[]{:S(2)}) %all-to-all-start.2) | async-done | bytes 524320 | tf_op jit(solution)/shard_map/all_to_all | solution.py:357
  118.6 0.3 owned.1
  118.9 9.6 %all-to-all-start.3 = ((bf16[64,8,256]{2,1,0:T(8,128)(2,1)}), bf16[64,8,256]{2,1,0:T(8,128)(2,1)S(1)}, u32[]{:S(2)}, u32[]{:S(2)}) async-start(bf16[64,8,256]{2,1,0:T(8,128)(2,1)} %bitcast.13), calls=%async_computation.3 | async-start | bytes 524288 | tf_op jit(solution)/shard_map/all_to_all | solution.py:410
  128.6 1.9 %collective-permute-start.4 = (bf16[4,32,512]{2,1,0:T(8,128)(2,1)S(1)}, bf16[4,32,512]{2,1,0:T(8,128)(2,1)S(1)}, u32[]{:S(2)}, u32[]{:S(2)}) collective-permute-start(bf16[4,32,512]{2,1,0:T(8,128)(2,1)S(1)} %get-tuple-element.42), channel_id=1, source_target_pairs={{0,1},{1,0},{2,3},{3,2},{4,5},{5,4},{6,7},{7,6},{8,9},{9,8},{10,11... | collective-permute-start | bytes 393224 | tf_op jit(solution)/shard_map/ppermute | solution.py:430
  130.5 1.3 collective-permute-done.4.got_ref
  131.9 1.9 %collective-permute-start.5 = (bf16[2,32,512]{2,1,0:T(8,128)(2,1)S(1)}, bf16[2,32,512]{2,1,0:T(8,128)(2,1)S(1)}, u32[]{:S(2)}, u32[]{:S(2)}) collective-permute-start(bf16[2,32,512]{2,1,0:T(8,128)(2,1)S(1)} %get-tuple-element.44), channel_id=1, source_target_pairs={{0,2},{1,3},{2,0},{3,1},{4,6},{5,7},{6,4},{7,5},{8,10},{9,11},{10,... | collective-permute-start | bytes 196616 | tf_op jit(solution)/shard_map/ppermute | solution.py:430
  133.8 4.2 %collective-permute-done.5.got_ref = bf16[2,32,512]{2,1,0:T(8,128)(2,1)S(1)} collective-permute-done((bf16[2,32,512]{2,1,0:T(8,128)(2,1)S(1)}, bf16[2,32,512]{2,1,0:T(8,128)(2,1)S(1)}, u32[]{:S(2)}, u32[]{:S(2)}) %collective-permute-start.5) | collective-permute-done | bytes 65568 | tf_op jit(solution)/shard_map/ppermute | solution.py:430
  138.0 1.9 %collective-permute-start.6 = (bf16[1,32,512]{2,1,0:T(8,128)(2,1)S(1)}, bf16[1,32,512]{2,1,0:T(8,128)(2,1)S(1)}, u32[]{:S(2)}, u32[]{:S(2)}) collective-permute-start(bf16[1,32,512]{2,1,0:T(8,128)(2,1)S(1)} %get-tuple-element.46), channel_id=1, source_target_pairs={{0,6},{1,7},{2,4},{3,5},{4,2},{5,3},{6,0},{7,1},{8,14},{9,15},{10,... | collective-permute-start | bytes 98312 | tf_op jit(solution)/shard_map/ppermute | solution.py:430
  140.0 5.1 %collective-permute-done.6.got_ref = bf16[1,32,512]{2,1,0:T(8,128)(2,1)S(1)} collective-permute-done((bf16[1,32,512]{2,1,0:T(8,128)(2,1)S(1)}, bf16[1,32,512]{2,1,0:T(8,128)(2,1)S(1)}, u32[]{:S(2)}, u32[]{:S(2)}) %collective-permute-start.6) | collective-permute-done | bytes 32800 | tf_op jit(solution)/shard_map/ppermute | solution.py:430
  145.0 0.6 last.1
  145.7 2.7 %all-to-all-done.3.got_ref = bf16[64,8,256]{2,1,0:T(8,128)(2,1)S(1)} async-done(((bf16[64,8,256]{2,1,0:T(8,128)(2,1)}), bf16[64,8,256]{2,1,0:T(8,128)(2,1)S(1)}, u32[]{:S(2)}, u32[]{:S(2)}) %all-to-all-start.3) | async-done | bytes 262176 | tf_op jit(solution)/shard_map/all_to_all | solution.py:410
  148.4 0.8 final.1
  (19 shorter events, 0.2 us)
Async XLA Ops:
  0.6 71.2 %copy-start.3 = (bf16[256,512]{1,0:T(8,128)(2,1)S(1)}, bf16[256,512]{1,0:T(8,128)(2,1)}, u32[]{:S(2)}) copy-start(bf16[256,512]{1,0:T(8,128)(2,1)} %node_ref.1) | copy-start | bytes 786436
  0.6 42.1 %copy-start.7 = (s32[1024]{0:T(1024)S(1)}, s32[1024]{0:T(1024)}, u32[]{:S(2)}) copy-start(s32[1024]{0:T(1024)} %param.13) | copy-start | bytes 12292
  0.7 42.1 %copy-start.6 = (s32[1024]{0:T(1024)S(1)}, s32[1024]{0:T(1024)}, u32[]{:S(2)}) copy-start(s32[1024]{0:T(1024)} %param.15) | copy-start | bytes 12292
  0.7 71.1 %copy-start.5 = (bf16[128]{0:T(256)(128)(2,1)S(1)}, bf16[128]{0:T(256)(128)(2,1)}, u32[]{:S(2)}) copy-start(bf16[128]{0:T(256)(128)(2,1)} %param.12) | copy-start | bytes 772
  0.7 71.1 %copy-start.4 = (bf16[512,128]{1,0:T(8,128)(2,1)S(1)}, bf16[512,128]{1,0:T(8,128)(2,1)}, u32[]{:S(2)}) copy-start(bf16[512,128]{1,0:T(8,128)(2,1)} %ws_ref.1) | copy-start | bytes 393220
  36.5 35.3 %all-to-all-start.1 = ((bf16[64,8,512]{2,1,0:T(8,128)(2,1)}), bf16[64,8,512]{2,1,0:T(8,128)(2,1)S(1)}, u32[]{:S(2)}, u32[]{:S(2)}) async-start(bf16[64,8,512]{2,1,0:T(8,128)(2,1)} %bitcast.23), calls=%async_computation.1 | async-start | bytes 1048576 | tf_op jit(solution)/shard_map/all_to_all | solution.py:328
  81.4 22.6 %copy-start.2 = (bf16[1024,512]{1,0:T(8,128)(2,1)S(1)}, bf16[1024,512]{1,0:T(8,128)(2,1)}, u32[]{:S(2)}) copy-start(bf16[1024,512]{1,0:T(8,128)(2,1)} %get-tuple-element.28.bfirst_ref) | copy-start | bytes 3145732
  81.4 37.2 %all-to-all-start.2 = ((bf16[64,8,512]{2,1,0:T(8,128)(2,1)}), bf16[64,8,512]{2,1,0:T(8,128)(2,1)S(1)}, u32[]{:S(2)}, u32[]{:S(2)}) async-start(bf16[64,8,512]{2,1,0:T(8,128)(2,1)} %bitcast.22), calls=%async_computation.2 | async-start | bytes 1048576 | tf_op jit(solution)/shard_map/all_to_all | solution.py:357
  88.3 4.6 %collective-permute-start = (bf16[4,224,512]{2,1,0:T(8,128)(2,1)}, bf16[4,224,512]{2,1,0:T(8,128)(2,1)S(1)}, u32[]{:S(2)}, u32[]{:S(2)}) collective-permute-start(bf16[4,224,512]{2,1,0:T(8,128)(2,1)} %get-tuple-element.31), channel_id=1, source_target_pairs={{0,1},{1,0},{2,3},{3,2},{4,5},{5,4},{6,7},{7,6},{8,9},{9,8},{10,11... | collective-permute-start | bytes 2752520 | tf_op jit(solution)/shard_map/ppermute | solution.py:380
  92.9 1.5 copy-start
  94.6 13.4 %collective-permute-start.1 = (bf16[224,512]{1,0:T(8,128)(2,1)S(1)}, bf16[224,512]{1,0:T(8,128)(2,1)S(1)}, u32[]{:S(2)}, u32[]{:S(2)}) collective-permute-start(bf16[224,512]{1,0:T(8,128)(2,1)S(1)} %get-tuple-element.33), channel_id=1, source_target_pairs={{0,4},{1,5},{2,6},{3,7},{4,0},{5,1},{6,2},{7,3},{8,12},{9,13},{10,... | collective-permute-start | bytes 688136 | tf_op jit(solution)/shard_map/ppermute | solution.py:381
  97.9 10.4 %collective-permute-start.2 = (bf16[224,512]{1,0:T(8,128)(2,1)S(1)}, bf16[224,512]{1,0:T(8,128)(2,1)S(1)}, u32[]{:S(2)}, u32[]{:S(2)}) collective-permute-start(bf16[224,512]{1,0:T(8,128)(2,1)S(1)} %get-tuple-element.34), channel_id=1, source_target_pairs={{0,2},{1,3},{2,4},{3,5},{4,6},{5,7},{6,0},{7,1},{8,10},{9,11},{10,... | collective-permute-start | bytes 688136 | tf_op jit(solution)/shard_map/ppermute | solution.py:381
  101.9 10.2 %collective-permute-start.3 = (bf16[224,512]{1,0:T(8,128)(2,1)S(1)}, bf16[224,512]{1,0:T(8,128)(2,1)S(1)}, u32[]{:S(2)}, u32[]{:S(2)}) collective-permute-start(bf16[224,512]{1,0:T(8,128)(2,1)S(1)} %get-tuple-element.35), channel_id=1, source_target_pairs={{0,6},{1,7},{2,0},{3,1},{4,2},{5,3},{6,4},{7,5},{8,14},{9,15},{10,... | collective-permute-start | bytes 688136 | tf_op jit(solution)/shard_map/ppermute | solution.py:381
  104.0 1.4 copy-start.1
  118.9 29.5 %all-to-all-start.3 = ((bf16[64,8,256]{2,1,0:T(8,128)(2,1)}), bf16[64,8,256]{2,1,0:T(8,128)(2,1)S(1)}, u32[]{:S(2)}, u32[]{:S(2)}) async-start(bf16[64,8,256]{2,1,0:T(8,128)(2,1)} %bitcast.13), calls=%async_computation.3 | async-start | bytes 524288 | tf_op jit(solution)/shard_map/all_to_all | solution.py:410
  128.6 3.2 %collective-permute-start.4 = (bf16[4,32,512]{2,1,0:T(8,128)(2,1)S(1)}, bf16[4,32,512]{2,1,0:T(8,128)(2,1)S(1)}, u32[]{:S(2)}, u32[]{:S(2)}) collective-permute-start(bf16[4,32,512]{2,1,0:T(8,128)(2,1)S(1)} %get-tuple-element.42), channel_id=1, source_target_pairs={{0,1},{1,0},{2,3},{3,2},{4,5},{5,4},{6,7},{7,6},{8,9},{9,8},{10,11... | collective-permute-start | bytes 393224 | tf_op jit(solution)/shard_map/ppermute | solution.py:430
  131.9 6.2 %collective-permute-start.5 = (bf16[2,32,512]{2,1,0:T(8,128)(2,1)S(1)}, bf16[2,32,512]{2,1,0:T(8,128)(2,1)S(1)}, u32[]{:S(2)}, u32[]{:S(2)}) collective-permute-start(bf16[2,32,512]{2,1,0:T(8,128)(2,1)S(1)} %get-tuple-element.44), channel_id=1, source_target_pairs={{0,2},{1,3},{2,0},{3,1},{4,6},{5,7},{6,4},{7,5},{8,10},{9,11},{10,... | collective-permute-start | bytes 196616 | tf_op jit(solution)/shard_map/ppermute | solution.py:430
  138.0 7.0 %collective-permute-start.6 = (bf16[1,32,512]{2,1,0:T(8,128)(2,1)S(1)}, bf16[1,32,512]{2,1,0:T(8,128)(2,1)S(1)}, u32[]{:S(2)}, u32[]{:S(2)}) collective-permute-start(bf16[1,32,512]{2,1,0:T(8,128)(2,1)S(1)} %get-tuple-element.46), channel_id=1, source_target_pairs={{0,6},{1,7},{2,4},{3,5},{4,2},{5,3},{6,0},{7,1},{8,14},{9,15},{10,... | collective-permute-start | bytes 98312 | tf_op jit(solution)/shard_map/ppermute | solution.py:430

commit v10 on v8

--- a/solution.py
+++ b/solution.py
@@ -12,7 +12,7 @@
 F32 = jnp.float32
 I32 = jnp.int32
 MIB = 1 << 20
-TILE = 1024
+TILE = 512
 LAST = 0
 WHOLE = pl.BlockSpec(memory_space=pltpu.VMEM)
 FREE = pl.CostEstimate(flops=0, bytes_accessed=0, transcendentals=0)

time: 150 us -> 150 us (level)
  no operation moved by 1% of the time
where the time goes in v10:
time: 150 us; the launch traced here: 149 us
  waiting for transfers between devices  54.7 us (36%)
  starting transfers between devices  38.3 us (26%)
  blocking collectives  32.9 us (22%)
  Pallas kernels  17.2 us (11%)
  local copies, waits for them, and re-layouts  3.96 us (3%)
  between operations  1.52 us (1%)
    all_to_all x1, blocking collectives, body(): lax.all_to_all(requests, 'dom', split_axis=0, concat_axis=0, tiled=True)  32.9 us
    all_to_all x1, waiting for transfers between devices, body(): lax.all_to_all(answer.reshape(parts, cap, width), 'dom', split_axis=0, co...  29 us
    ppermute x3, waiting for transfers between devices, body(): got = lax.ppermute(sent, 'edge', partner)  10.8 us
    pallas_call x1, Pallas kernels, body(): pl.pallas_call(functools.partial(pair_kernel, scale, n_edge), out_shape=t...  9.74 us
    all_to_all x1, starting transfers between devices, body(): lax.all_to_all(packed.reshape(parts, share, lanes), 'dom', split_axis=0,...  9.64 us
    ppermute x3, starting transfers between devices, body(): lax.ppermute(packs[step - 1], 'edge', ahead(step))  9.41 us
    all_to_all x1, starting transfers between devices, body(): lax.all_to_all(slot_grad.reshape(parts, cap, width), 'dom', split_axis=0,...  6.9 us
    ppermute x3, starting transfers between devices, body(): got = lax.ppermute(sent, 'edge', partner)  5.76 us
  transfers between devices with their start and end apart: 10, of which 9 were waited for; matrix products, arithmetic and copies ran while one was open for 1% of the time, Pallas kernels for 3%

profile of v10, /device:TPU:6, one launch (start us, length us, event | category | flops | bytes accessed | tf_op | source)
XLA Modules:
  0.0 149.4 jit_solution(9651067710970707836)
XLA Ops:
  0.7 0.8 copy.20
  1.5 32.9 %all_to_all.26 = s32[64,1,8]{2,1,0:T(1,128)S(1)} all-to-all(s32[64,1,8]{2,1,0:T(1,128)S(1)} %bitcast.24), channel_id=1, replica_groups=mesh['dom'=64,'edge'=8] {'dom'}, dimensions={0} | all-to-all | bytes 4096 | tf_op jit(solution)/shard_map/all_to_all | solution.py:311
  34.5 2.0 %answer.1 = (bf16[512,512]{1,0:T(8,128)(2,1)}, s32[1,512]{1,0:T(1,128)S(1)}) custom-call(s32[64,8]{1,0:T(8,128)S(1)} %bitcast.20, bf16[256,512]{1,0:T(8,128)(2,1)} %node_ref.1), custom_call_target="tpu_custom_call" | custom-call | tf_op jit(solution)/shard_map/answer/pallas_call | solution.py:312
  36.5 4.6 %all-to-all-start.1 = ((bf16[64,8,512]{2,1,0:T(8,128)(2,1)}), bf16[64,8,512]{2,1,0:T(8,128)(2,1)S(1)}, u32[]{:S(2)}, u32[]{:S(2)}) async-start(bf16[64,8,512]{2,1,0:T(8,128)(2,1)} %bitcast.23), calls=%async_computation.1 | async-start | bytes 1048576 | tf_op jit(solution)/shard_map/all_to_all | solution.py:328
  41.8 0.7 pad_add_fusion
  42.6 0.2 copy.22.cols_ref
  42.8 29.0 %all-to-all-done.1 = bf16[64,8,512]{2,1,0:T(8,128)(2,1)S(1)} async-done(((bf16[64,8,512]{2,1,0:T(8,128)(2,1)}), bf16[64,8,512]{2,1,0:T(8,128)(2,1)S(1)}, u32[]{:S(2)}, u32[]{:S(2)}) %all-to-all-start.1) | async-done | bytes 524320 | tf_op jit(solution)/shard_map/all_to_all | solution.py:328
  71.8 9.7 %pair.1 = (bf16[512,512]{1,0:T(8,128)(2,1)}, bf16[1024,512]{1,0:T(8,128)(2,1)}, f32[4,216,512]{2,1,0:T(8,128)}, bf16[4,224,512]{2,1,0:T(8,128)(2,1)}) custom-call(s32[1]{0:T(128)S(6)} %copy.24.live_ref, s32[1]{0:T(128)} %bitcast.edge_ref, s32[1024,3]{1,0:T(8,128)S(1)} %copy.22.cols_ref, s32[2,1024]{1,0:T(2,128)S(1)} %pad_add_fusion.1.lines_ref, ...), custom_call_target="tpu_custom_call" | custom-call | flops 6000000000 | bytes 8388608 | tf_op jit(solution)/shard_map/pair/pallas_call | solution.py:333
  81.6 6.9 %all-to-all-start.2 = ((bf16[64,8,512]{2,1,0:T(8,128)(2,1)}), bf16[64,8,512]{2,1,0:T(8,128)(2,1)S(1)}, u32[]{:S(2)}, u32[]{:S(2)}) async-start(bf16[64,8,512]{2,1,0:T(8,128)(2,1)} %bitcast.22), calls=%async_computation.2 | async-start | bytes 1048576 | tf_op jit(solution)/shard_map/all_to_all | solution.py:357
  88.5 1.9 %collective-permute-start = (bf16[4,224,512]{2,1,0:T(8,128)(2,1)}, bf16[4,224,512]{2,1,0:T(8,128)(2,1)S(1)}, u32[]{:S(2)}, u32[]{:S(2)}) collective-permute-start(bf16[4,224,512]{2,1,0:T(8,128)(2,1)} %get-tuple-element.31), channel_id=1, source_target_pairs={{0,1},{1,0},{2,3},{3,2},{4,5},{5,4},{6,7},{7,6},{8,9},{9,8},{10,11... | collective-permute-start | bytes 2752520 | tf_op jit(solution)/shard_map/ppermute | solution.py:380
  90.4 2.6 %collective-permute-done.got_ref = bf16[4,224,512]{2,1,0:T(8,128)(2,1)S(1)} collective-permute-done((bf16[4,224,512]{2,1,0:T(8,128)(2,1)}, bf16[4,224,512]{2,1,0:T(8,128)(2,1)S(1)}, u32[]{:S(2)}, u32[]{:S(2)}) %collective-permute-start) | collective-permute-done | bytes 917536 | tf_op jit(solution)/shard_map/ppermute | solution.py:380
  93.1 1.5 copy-done
  94.7 3.3 %collective-permute-start.1 = (bf16[224,512]{1,0:T(8,128)(2,1)S(1)}, bf16[224,512]{1,0:T(8,128)(2,1)S(1)}, u32[]{:S(2)}, u32[]{:S(2)}) collective-permute-start(bf16[224,512]{1,0:T(8,128)(2,1)S(1)} %get-tuple-element.33), channel_id=1, source_target_pairs={{0,4},{1,5},{2,6},{3,7},{4,0},{5,1},{6,2},{7,3},{8,12},{9,13},{10,... | collective-permute-start | bytes 688136 | tf_op jit(solution)/shard_map/ppermute | solution.py:381
  98.0 4.0 %collective-permute-start.2 = (bf16[224,512]{1,0:T(8,128)(2,1)S(1)}, bf16[224,512]{1,0:T(8,128)(2,1)S(1)}, u32[]{:S(2)}, u32[]{:S(2)}) collective-permute-start(bf16[224,512]{1,0:T(8,128)(2,1)S(1)} %get-tuple-element.34), channel_id=1, source_target_pairs={{0,2},{1,3},{2,4},{3,5},{4,6},{5,7},{6,0},{7,1},{8,10},{9,11},{10,... | collective-permute-start | bytes 688136 | tf_op jit(solution)/shard_map/ppermute | solution.py:381
  102.0 2.1 %collective-permute-start.3 = (bf16[224,512]{1,0:T(8,128)(2,1)S(1)}, bf16[224,512]{1,0:T(8,128)(2,1)S(1)}, u32[]{:S(2)}, u32[]{:S(2)}) collective-permute-start(bf16[224,512]{1,0:T(8,128)(2,1)S(1)} %get-tuple-element.35), channel_id=1, source_target_pairs={{0,6},{1,7},{2,0},{3,1},{4,2},{5,3},{6,4},{7,5},{8,14},{9,15},{10,... | collective-permute-start | bytes 688136 | tf_op jit(solution)/shard_map/ppermute | solution.py:381
  104.2 1.4 copy-done.1
  105.6 2.5 %near.1.refs_4_.near_ref = f32[256,512]{1,0:T(8,128)S(1)} custom-call(s32[2,1024]{1,0:T(2,128)S(1)} %pad_add_fusion.1.lines_ref, s32[1024,3]{1,0:T(8,128)S(1)} %copy.22.cols_ref, bf16[512,512]{1,0:T(8,128)(2,1)S(1)} %bitcast.19, bf16[1024,512]{1,0:T(8,128)(2,1)S(1)} %copy-done.2, bf16[1536,512]{1,0:T(8,128)(2,1)S(1)} %copy-done.1), custom_call_target="tpu_custom_call" | custom-call | tf_op jit(solution)/shard_map/near/pallas_call | solution.py:361
  108.1 0.4 collective-permute-done.2.refs_2_
  108.4 3.8 %collective-permute-done.3.refs_3_ = bf16[224,512]{1,0:T(8,128)(2,1)S(1)} collective-permute-done((bf16[224,512]{1,0:T(8,128)(2,1)S(1)}, bf16[224,512]{1,0:T(8,128)(2,1)S(1)}, u32[]{:S(2)}, u32[]{:S(2)}) %collective-permute-start.3) | collective-permute-done | bytes 229408 | tf_op jit(solution)/shard_map/ppermute | solution.py:381
  112.2 1.0 total.1.packed_ref
  113.2 5.5 %all-to-all-done.2 = bf16[64,8,512]{2,1,0:T(8,128)(2,1)S(1)} async-done(((bf16[64,8,512]{2,1,0:T(8,128)(2,1)}), bf16[64,8,512]{2,1,0:T(8,128)(2,1)S(1)}, u32[]{:S(2)}, u32[]{:S(2)}) %all-to-all-start.2) | async-done | bytes 524320 | tf_op jit(solution)/shard_map/all_to_all | solution.py:357
  118.7 0.3 owned.1
  119.1 9.6 %all-to-all-start.3 = ((bf16[64,8,256]{2,1,0:T(8,128)(2,1)}), bf16[64,8,256]{2,1,0:T(8,128)(2,1)S(1)}, u32[]{:S(2)}, u32[]{:S(2)}) async-start(bf16[64,8,256]{2,1,0:T(8,128)(2,1)} %bitcast.13), calls=%async_computation.3 | async-start | bytes 524288 | tf_op jit(solution)/shard_map/all_to_all | solution.py:406
  128.7 1.9 %collective-permute-start.4 = (f32[4,32,512]{2,1,0:T(8,128)S(1)}, f32[4,32,512]{2,1,0:T(8,128)S(1)}, u32[]{:S(2)}, u32[]{:S(2)}) collective-permute-start(f32[4,32,512]{2,1,0:T(8,128)S(1)} %get-tuple-element.42), channel_id=1, source_target_pairs={{0,1},{1,0},{2,3},{3,2},{4,5},{5,4},{6,7},{7,6},{8,9},{9,8},{10,11... | collective-permute-start | bytes 786440 | tf_op jit(solution)/shard_map/ppermute | solution.py:426
  130.7 1.5 %collective-permute-done.4.got_ref = f32[4,32,512]{2,1,0:T(8,128)S(1)} collective-permute-done((f32[4,32,512]{2,1,0:T(8,128)S(1)}, f32[4,32,512]{2,1,0:T(8,128)S(1)}, u32[]{:S(2)}, u32[]{:S(2)}) %collective-permute-start.4) | collective-permute-done | bytes 262176 | tf_op jit(solution)/shard_map/ppermute | solution.py:426
  132.2 1.9 %collective-permute-start.5 = (bf16[2,32,512]{2,1,0:T(8,128)(2,1)S(1)}, bf16[2,32,512]{2,1,0:T(8,128)(2,1)S(1)}, u32[]{:S(2)}, u32[]{:S(2)}) collective-permute-start(bf16[2,32,512]{2,1,0:T(8,128)(2,1)S(1)} %get-tuple-element.44), channel_id=1, source_target_pairs={{0,2},{1,3},{2,0},{3,1},{4,6},{5,7},{6,4},{7,5},{8,10},{9,11},{10,... | collective-permute-start | bytes 196616 | tf_op jit(solution)/shard_map/ppermute | solution.py:426
  134.1 4.2 %collective-permute-done.5.got_ref = bf16[2,32,512]{2,1,0:T(8,128)(2,1)S(1)} collective-permute-done((bf16[2,32,512]{2,1,0:T(8,128)(2,1)S(1)}, bf16[2,32,512]{2,1,0:T(8,128)(2,1)S(1)}, u32[]{:S(2)}, u32[]{:S(2)}) %collective-permute-start.5) | collective-permute-done | bytes 65568 | tf_op jit(solution)/shard_map/ppermute | solution.py:426
  138.4 1.9 %collective-permute-start.6 = (bf16[1,32,512]{2,1,0:T(8,128)(2,1)S(1)}, bf16[1,32,512]{2,1,0:T(8,128)(2,1)S(1)}, u32[]{:S(2)}, u32[]{:S(2)}) collective-permute-start(bf16[1,32,512]{2,1,0:T(8,128)(2,1)S(1)} %get-tuple-element.46), channel_id=1, source_target_pairs={{0,6},{1,7},{2,4},{3,5},{4,2},{5,3},{6,0},{7,1},{8,14},{9,15},{10,... | collective-permute-start | bytes 98312 | tf_op jit(solution)/shard_map/ppermute | solution.py:426
  140.3 5.1 %collective-permute-done.6.got_ref = bf16[1,32,512]{2,1,0:T(8,128)(2,1)S(1)} collective-permute-done((bf16[1,32,512]{2,1,0:T(8,128)(2,1)S(1)}, bf16[1,32,512]{2,1,0:T(8,128)(2,1)S(1)}, u32[]{:S(2)}, u32[]{:S(2)}) %collective-permute-start.6) | collective-permute-done | bytes 32800 | tf_op jit(solution)/shard_map/ppermute | solution.py:426
  145.4 0.6 last.1
  146.0 2.5 %all-to-all-done.3.got_ref = bf16[64,8,256]{2,1,0:T(8,128)(2,1)S(1)} async-done(((bf16[64,8,256]{2,1,0:T(8,128)(2,1)}), bf16[64,8,256]{2,1,0:T(8,128)(2,1)S(1)}, u32[]{:S(2)}, u32[]{:S(2)}) %all-to-all-start.3) | async-done | bytes 262176 | tf_op jit(solution)/shard_map/all_to_all | solution.py:406
  148.6 0.8 final.1
  (19 shorter events, 0.3 us)
Async XLA Ops:
  0.6 71.2 %copy-start.3 = (bf16[256,512]{1,0:T(8,128)(2,1)S(1)}, bf16[256,512]{1,0:T(8,128)(2,1)}, u32[]{:S(2)}) copy-start(bf16[256,512]{1,0:T(8,128)(2,1)} %node_ref.1) | copy-start | bytes 786436
  0.6 42.1 %copy-start.7 = (s32[1024]{0:T(1024)S(1)}, s32[1024]{0:T(1024)}, u32[]{:S(2)}) copy-start(s32[1024]{0:T(1024)} %param.13) | copy-start | bytes 12292
  0.7 42.1 %copy-start.6 = (s32[1024]{0:T(1024)S(1)}, s32[1024]{0:T(1024)}, u32[]{:S(2)}) copy-start(s32[1024]{0:T(1024)} %param.15) | copy-start | bytes 12292
  0.7 71.1 %copy-start.5 = (bf16[128]{0:T(256)(128)(2,1)S(1)}, bf16[128]{0:T(256)(128)(2,1)}, u32[]{:S(2)}) copy-start(bf16[128]{0:T(256)(128)(2,1)} %param.12) | copy-start | bytes 772
  0.7 71.1 %copy-start.4 = (bf16[512,128]{1,0:T(8,128)(2,1)S(1)}, bf16[512,128]{1,0:T(8,128)(2,1)}, u32[]{:S(2)}) copy-start(bf16[512,128]{1,0:T(8,128)(2,1)} %ws_ref.1) | copy-start | bytes 393220
  36.5 35.3 %all-to-all-start.1 = ((bf16[64,8,512]{2,1,0:T(8,128)(2,1)}), bf16[64,8,512]{2,1,0:T(8,128)(2,1)S(1)}, u32[]{:S(2)}, u32[]{:S(2)}) async-start(bf16[64,8,512]{2,1,0:T(8,128)(2,1)} %bitcast.23), calls=%async_computation.1 | async-start | bytes 1048576 | tf_op jit(solution)/shard_map/all_to_all | solution.py:328
  81.6 22.6 %copy-start.2 = (bf16[1024,512]{1,0:T(8,128)(2,1)S(1)}, bf16[1024,512]{1,0:T(8,128)(2,1)}, u32[]{:S(2)}) copy-start(bf16[1024,512]{1,0:T(8,128)(2,1)} %get-tuple-element.28.bfirst_ref) | copy-start | bytes 3145732
  81.6 37.2 %all-to-all-start.2 = ((bf16[64,8,512]{2,1,0:T(8,128)(2,1)}), bf16[64,8,512]{2,1,0:T(8,128)(2,1)S(1)}, u32[]{:S(2)}, u32[]{:S(2)}) async-start(bf16[64,8,512]{2,1,0:T(8,128)(2,1)} %bitcast.22), calls=%async_computation.2 | async-start | bytes 1048576 | tf_op jit(solution)/shard_map/all_to_all | solution.py:357
  88.5 4.6 %collective-permute-start = (bf16[4,224,512]{2,1,0:T(8,128)(2,1)}, bf16[4,224,512]{2,1,0:T(8,128)(2,1)S(1)}, u32[]{:S(2)}, u32[]{:S(2)}) collective-permute-start(bf16[4,224,512]{2,1,0:T(8,128)(2,1)} %get-tuple-element.31), channel_id=1, source_target_pairs={{0,1},{1,0},{2,3},{3,2},{4,5},{5,4},{6,7},{7,6},{8,9},{9,8},{10,11... | collective-permute-start | bytes 2752520 | tf_op jit(solution)/shard_map/ppermute | solution.py:380
  93.1 1.5 copy-start
  94.7 13.3 %collective-permute-start.1 = (bf16[224,512]{1,0:T(8,128)(2,1)S(1)}, bf16[224,512]{1,0:T(8,128)(2,1)S(1)}, u32[]{:S(2)}, u32[]{:S(2)}) collective-permute-start(bf16[224,512]{1,0:T(8,128)(2,1)S(1)} %get-tuple-element.33), channel_id=1, source_target_pairs={{0,4},{1,5},{2,6},{3,7},{4,0},{5,1},{6,2},{7,3},{8,12},{9,13},{10,... | collective-permute-start | bytes 688136 | tf_op jit(solution)/shard_map/ppermute | solution.py:381
  98.0 10.4 %collective-permute-start.2 = (bf16[224,512]{1,0:T(8,128)(2,1)S(1)}, bf16[224,512]{1,0:T(8,128)(2,1)S(1)}, u32[]{:S(2)}, u32[]{:S(2)}) collective-permute-start(bf16[224,512]{1,0:T(8,128)(2,1)S(1)} %get-tuple-element.34), channel_id=1, source_target_pairs={{0,2},{1,3},{2,4},{3,5},{4,6},{5,7},{6,0},{7,1},{8,10},{9,11},{10,... | collective-permute-start | bytes 688136 | tf_op jit(solution)/shard_map/ppermute | solution.py:381
  102.0 10.2 %collective-permute-start.3 = (bf16[224,512]{1,0:T(8,128)(2,1)S(1)}, bf16[224,512]{1,0:T(8,128)(2,1)S(1)}, u32[]{:S(2)}, u32[]{:S(2)}) collective-permute-start(bf16[224,512]{1,0:T(8,128)(2,1)S(1)} %get-tuple-element.35), channel_id=1, source_target_pairs={{0,6},{1,7},{2,0},{3,1},{4,2},{5,3},{6,4},{7,5},{8,14},{9,15},{10,... | collective-permute-start | bytes 688136 | tf_op jit(solution)/shard_map/ppermute | solution.py:381
  104.1 1.4 copy-start.1
  119.1 29.5 %all-to-all-start.3 = ((bf16[64,8,256]{2,1,0:T(8,128)(2,1)}), bf16[64,8,256]{2,1,0:T(8,128)(2,1)S(1)}, u32[]{:S(2)}, u32[]{:S(2)}) async-start(bf16[64,8,256]{2,1,0:T(8,128)(2,1)} %bitcast.13), calls=%async_computation.3 | async-start | bytes 524288 | tf_op jit(solution)/shard_map/all_to_all | solution.py:406
  128.7 3.4 %collective-permute-start.4 = (f32[4,32,512]{2,1,0:T(8,128)S(1)}, f32[4,32,512]{2,1,0:T(8,128)S(1)}, u32[]{:S(2)}, u32[]{:S(2)}) collective-permute-start(f32[4,32,512]{2,1,0:T(8,128)S(1)} %get-tuple-element.42), channel_id=1, source_target_pairs={{0,1},{1,0},{2,3},{3,2},{4,5},{5,4},{6,7},{7,6},{8,9},{9,8},{10,11... | collective-permute-start | bytes 786440 | tf_op jit(solution)/shard_map/ppermute | solution.py:426
  132.2 6.2 %collective-permute-start.5 = (bf16[2,32,512]{2,1,0:T(8,128)(2,1)S(1)}, bf16[2,32,512]{2,1,0:T(8,128)(2,1)S(1)}, u32[]{:S(2)}, u32[]{:S(2)}) collective-permute-start(bf16[2,32,512]{2,1,0:T(8,128)(2,1)S(1)} %get-tuple-element.44), channel_id=1, source_target_pairs={{0,2},{1,3},{2,0},{3,1},{4,6},{5,7},{6,4},{7,5},{8,10},{9,11},{10,... | collective-permute-start | bytes 196616 | tf_op jit(solution)/shard_map/ppermute | solution.py:426
  138.4 7.0 %collective-permute-start.6 = (bf16[1,32,512]{2,1,0:T(8,128)(2,1)S(1)}, bf16[1,32,512]{2,1,0:T(8,128)(2,1)S(1)}, u32[]{:S(2)}, u32[]{:S(2)}) collective-permute-start(bf16[1,32,512]{2,1,0:T(8,128)(2,1)S(1)} %get-tuple-element.46), channel_id=1, source_target_pairs={{0,6},{1,7},{2,4},{3,5},{4,2},{5,3},{6,0},{7,1},{8,14},{9,15},{10,... | collective-permute-start | bytes 98312 | tf_op jit(solution)/shard_map/ppermute | solution.py:426
